TPU v7x, 128 devices: a whole 4x4x4 slice. The times are simulated.
128 devices in a mesh: prow: 8 (over z, core), pcol: 16 (over x, y).
Axes of the slice: x: 4, y: 4, z: 4, core: 2. Of those that a mesh axis runs over, the one named last changes fastest.
Arguments:
- matrix: float32 [6, 8, 256, 3, 16, 256], P(None, 'prow', None, None, 'pcol'), may hold values from -6 to 6
- row_order: int32 [12288], replicated, may hold values from 0 to 12287, as said below
- inverses: float32 [4, 256, 256], replicated, may hold values from -0.0234375 to 0.0234375
- lower_fill: int32 [4, 48], replicated, may hold values 0 or 1
- upper_fill: int32 [4, 48], replicated, may hold values 0 or 1
Outputs:
- factored: float32 [6, 8, 256, 3, 16, 256], P(None, 'prow', None, None, 'pcol')
Inputs may be any that keep to these rules, and one draw needn't show every extreme that they name: row_order is a permutation of the rows; of the rows whose block row index is congruent to p modulo the number of indices of prow, exactly 6 * 256 divided by that number go to rows whose block row index is congruent to s, for every p and s.
All inputs are finite; a program needn't handle non-finite values.
Results may differ from a plain program's by a relative error of at most 0.0002.
Values sent between devices are 32-bit elements; how exact they have to be, the bound alone decides.
No kernel may reach another device: no remote copies, remote signals or barrier semaphores. Data moves between devices by JAX's collectives and lax.ppermute only.
A program may use at most 128 MiB of HBM per device.

v0:
```python
import jax
import jax.numpy as jnp
from jax import lax
from jax.sharding import PartitionSpec as P


def spread(value, axis, source):
    kept = jnp.where(lax.axis_index(axis) == source, value, 0).astype(value.dtype)
    return lax.psum(kept, axis)


def permute_rows(work, row_order, width, prows, here_row):
    total = row_order.shape[0]
    local_rows = work.shape[0]
    share = local_rows // prows
    local = jnp.arange(local_rows, dtype=jnp.int32)
    mine = (local // width * prows + here_row) * width + local % width
    targets = row_order[mine]
    target_prow = targets // width % prows
    sending = jnp.argsort(target_prow, stable=True)
    outgoing = work[sending].reshape(prows, share, work.shape[1])
    incoming = lax.all_to_all(outgoing, "prow", split_axis=0, concat_axis=0, tiled=True)
    everyone = jnp.arange(total, dtype=jnp.int32)
    source_prow = everyone // width % prows
    source_local = everyone // width // prows * width + everyone % width
    dest_prow = row_order // width % prows
    dest_local = row_order // width // prows * width + row_order % width
    sort_key = jnp.where(
        dest_prow == here_row, source_prow * local_rows + source_local, prows * local_rows
    )
    chosen = jnp.argsort(sort_key, stable=True)[:local_rows]
    places = dest_local[chosen]
    return jnp.zeros_like(work).at[places].set(incoming.reshape(local_rows, work.shape[1]))


def block_keep(fill_row, block_ids, width):
    total_blocks = fill_row.shape[0]
    match = block_ids[:, None] == jnp.arange(total_blocks, dtype=jnp.int32)[None, :]
    picked = jnp.sum(jnp.where(match, fill_row[None, :], 0), axis=1)
    return jnp.repeat(picked, width)


def factors(column, row, inverse, panel, lower_fill, upper_fill, row_blocks, col_blocks, width):
    row_ids = jnp.repeat(row_blocks, width)
    col_ids = jnp.repeat(col_blocks, width)
    keep_rows = (
        (row_ids > panel) & (block_keep(lower_fill[panel], row_blocks, width) == 1)
    ).astype(jnp.float32)
    keep_cols = (
        (col_ids > panel) & (block_keep(upper_fill[panel], col_blocks, width) == 1)
    ).astype(jnp.float32)
    lower = (
        jnp.dot(
            column, inverse, precision=lax.Precision.HIGHEST, preferred_element_type=jnp.float32
        )
        * keep_rows[:, None]
    )
    upper = row * keep_cols[None, :]
    return (lower, upper)


def place_lower(work, lower, panel, row_blocks, here_col, pcols, width):
    local_col = panel // pcols
    row_ids = jnp.repeat(row_blocks, width)
    old = work[:, local_col * width : (local_col + 1) * width]
    placed = jnp.where(((row_ids > panel) & (here_col == panel % pcols))[:, None], lower, old)
    return work.at[:, local_col * width : (local_col + 1) * width].set(placed)


def trailing(work, lower, upper, panel, row_blocks, here_col, pcols, width):
    work = work - jnp.dot(
        lower, upper, precision=lax.Precision.HIGHEST, preferred_element_type=jnp.float32
    )
    return place_lower(work, lower, panel, row_blocks, here_col, pcols, width)


def body(matrix, row_order, inverses, lower_fill, upper_fill):
    nrows = matrix.shape[0]
    width = matrix.shape[2]
    ncols = matrix.shape[3]
    prows = lax.axis_size("prow")
    pcols = lax.axis_size("pcol")
    here_row = lax.axis_index("prow")
    here_col = lax.axis_index("pcol")
    panels = inverses.shape[0]
    work = matrix.reshape(nrows * width, ncols * width)
    work = permute_rows(work, row_order, width, prows, here_row)
    row_blocks = jnp.arange(nrows, dtype=jnp.int32) * prows + here_row
    col_blocks = jnp.arange(ncols, dtype=jnp.int32) * pcols + here_col
    for panel in range(panels):
        local_col = panel // pcols
        local_row = panel // prows
        column = spread(work[:, local_col * width : (local_col + 1) * width], "pcol", panel % pcols)
        row = spread(work[local_row * width : (local_row + 1) * width, :], "prow", panel % prows)
        lower, upper = factors(
            column,
            row,
            inverses[panel],
            panel,
            lower_fill,
            upper_fill,
            row_blocks,
            col_blocks,
            width,
        )
        work = trailing(work, lower, upper, panel, row_blocks, here_col, pcols, width)
    return work.reshape(nrows, 1, width, ncols, 1, width)


def solution(mesh):
    in_specs = (P(None, "prow", None, None, "pcol", None), P(), P(), P(), P())
    out_specs = P(None, "prow", None, None, "pcol", None)
    return jax.shard_map(body, mesh=mesh, in_specs=in_specs, out_specs=out_specs, check_vma=False)
```

profile of v0, /device:TPU:1, one launch (start us, length us, event | category | flops | bytes accessed | tf_op | source)
XLA Modules:
  0.0 790.2 jit_solution(12800814390088315431)
XLA Ops:
  6.6 7.8 gather_fusion.1
  14.4 5.0 sort.35
  19.4 17.2 %reduce.14 = f32[6,256,3,256]{3,2,1,0:T(4,128)} reduce(f32[6,1,256,3,1,256]{5,4,3,2,1,0:T(1,128)} %param.13, f32[]{:T(128)} %constant.238), dimensions={1,4}, to_apply=%param.13.reduce_sub_computation | reduce | bytes 9437188 | tf_op args[0]
  36.7 6.1 copy.13
  42.8 9.2 %gather_fusion.2 = f32[1536,768]{1,0:T(8,128)} fusion(f32[1536,768]{1,0:T(8,128)} %bitcast.41, s32[2048]{0:T(1024)S(1)} %pad_clamp_fusion), kind=kCustom, calls=%fused_computation.2 | custom fusion | bytes 9443328 | tf_op jit(solution)/shard_map/gather | solution.py:21
  52.0 6.9 all-to-all-start
  58.9 0.1 fusion.33
  59.1 8.2 %sort.34 = (s32[12288]{0:T(1024)}, s32[12288]{0:T(1024)S(1)}) sort(s32[12288]{0:T(1024)S(1)} %get-tuple-element.71, s32[12288]{0:T(1024)S(1)} %iota.43), dimensions={0}, to_apply=%region_0.1 | sort | flops 172032 | bytes 196608 | tf_op jit(solution)/shard_map/jit(argsort)/sort | solution.py:31
  67.3 8.4 %gather_fusion = s32[1536]{0:T(1024)S(1)} fusion(s32[12288]{0:T(1024)S(1)} %get-tuple-element.72, s32[2048]{0:T(1024)S(1)} %pad_clamp_fusion.2), kind=kCustom, calls=%fused_computation | custom fusion | bytes 18432 | tf_op jit(solution)/shard_map/gather | solution.py:32
  75.7 37.7 %all-to-all-done = f32[8,192,768]{2,1,0:T(8,128)} async-done(((f32[8,192,768]{2,1,0:T(8,128)}), f32[8,192,768]{2,1,0:T(8,128)}, u32[]{:S(2)}, u32[]{:S(2)}) %all-to-all-start) | async-done | bytes 4718624 | tf_op jit(solution)/shard_map/all_to_all | solution.py:22
  113.5 10.2 %scatter_custom_fusion = f32[1536,768]{1,0:T(8,128)} fusion(s32[1536]{0:T(1024)S(1)} %fusion.52, f32[1536,768]{1,0:T(8,128)} %bitcast.1, f32[]{:T(128)} %constant.218.clone.1), kind=kCustom, calls=%fused_computation.16 | custom fusion | bytes 4719104 | tf_op jit(solution)/shard_map/scatter | solution.py:33
  123.6 2.7 slice_select_fusion
  126.4 0.6 copy-done.2
  127.0 0.2 select_reduce_fusion
  127.3 0.2 select_reduce_fusion.4
  127.6 2.1 slice_select_fusion.4
  129.7 0.3 all-reduce.13.cloned.1.call-start
  130.0 0.1 broadcast_in_dim.214
  130.1 0.6 compare_reduce_fusion
  130.7 82.5 %all-reduce.9.cloned.1.call-done = f32[1536,256]{1,0:T(8,128)} async-done(((f32[1536,256]{1,0:T(8,128)}), f32[1536,256]{1,0:T(8,128)}) %all-reduce.9.cloned.1.call-update) | async-done | bytes 1572880 | tf_op jit(solution)/shard_map/psum | solution.py:9
  213.2 2.8 convolution_multiply_fusion.3
  216.0 60.3 %all-reduce.11.cloned.1.call-done = f32[256,768]{1,0:T(8,128)} async-done(((f32[256,768]{1,0:T(8,128)}), f32[256,768]{1,0:T(8,128)}) %all-reduce.11.cloned.1.call-update) | async-done | bytes 786448 | tf_op jit(solution)/shard_map/psum | solution.py:9
  276.3 7.5 convolution_subtract_fusion.3
  283.8 3.9 broadcast_select_fusion.2
  287.9 2.1 slice_select_fusion.3
  290.1 0.1 broadcast_in_dim.222
  290.2 85.9 %all-reduce.13.cloned.1.call-done = f32[1536,256]{1,0:T(8,128)} async-done(((f32[1536,256]{1,0:T(8,128)}), f32[1536,256]{1,0:T(8,128)}) %all-reduce.13.cloned.1.call-update) | async-done | bytes 1572880 | tf_op jit(solution)/shard_map/psum | solution.py:9
  376.0 2.8 convolution_multiply_fusion.2
  378.8 60.3 %all-reduce.15.cloned.1.call-done = f32[256,768]{1,0:T(8,128)} async-done(((f32[256,768]{1,0:T(8,128)}), f32[256,768]{1,0:T(8,128)}) %all-reduce.15.cloned.1.call-update) | async-done | bytes 786448 | tf_op jit(solution)/shard_map/psum | solution.py:9
  439.1 7.5 convolution_subtract_fusion.2
  446.6 3.9 broadcast_select_fusion.1
  450.7 0.1 broadcast_in_dim.229
  450.8 2.1 slice_select_fusion.2
  452.9 0.3 all-reduce.21.cloned.1.call-start
  453.2 0.1 broadcast_in_dim.230
  453.3 85.6 %all-reduce.17.cloned.1.call-done = f32[1536,256]{1,0:T(8,128)} async-done(((f32[1536,256]{1,0:T(8,128)}), f32[1536,256]{1,0:T(8,128)}) %all-reduce.17.cloned.1.call-update) | async-done | bytes 1572880 | tf_op jit(solution)/shard_map/psum | solution.py:9
  538.9 2.8 convolution_multiply_fusion.1
  541.7 60.2 %all-reduce.19.cloned.1.call-done = f32[256,768]{1,0:T(8,128)} async-done(((f32[256,768]{1,0:T(8,128)}), f32[256,768]{1,0:T(8,128)}) %all-reduce.19.cloned.1.call-update) | async-done | bytes 786448 | tf_op jit(solution)/shard_map/psum | solution.py:9
  601.9 7.5 convolution_subtract_fusion.1
  609.3 3.9 broadcast_select_fusion
  613.5 2.1 slice_select_fusion.1
  615.6 0.1 broadcast_in_dim.238
  615.7 85.9 %all-reduce.21.cloned.1.call-done = f32[1536,256]{1,0:T(8,128)} async-done(((f32[1536,256]{1,0:T(8,128)}), f32[1536,256]{1,0:T(8,128)}) %all-reduce.21.cloned.1.call-update) | async-done | bytes 1572880 | tf_op jit(solution)/shard_map/psum | solution.py:9
  701.5 2.8 convolution_multiply_fusion
  704.3 60.4 %all-reduce.23.cloned.1.call-done = f32[256,768]{1,0:T(8,128)} async-done(((f32[256,768]{1,0:T(8,128)}), f32[256,768]{1,0:T(8,128)}) %all-reduce.23.cloned.1.call-update) | async-done | bytes 786448 | tf_op jit(solution)/shard_map/psum | solution.py:9
  764.8 7.5 convolution_subtract_fusion
  772.2 3.4 fusion.2
  775.7 7.7 reshape.427
  (64 shorter events, 1.2 us)
Async XLA Ops:
  52.0 7.0 copy-start
  52.0 61.5 %all-to-all-start = ((f32[8,192,768]{2,1,0:T(8,128)}), f32[8,192,768]{2,1,0:T(8,128)}, u32[]{:S(2)}, u32[]{:S(2)}) async-start(f32[8,192,768]{2,1,0:T(8,128)} %bitcast.43), calls=%async_computation | async-start | bytes 9437184 | tf_op jit(solution)/shard_map/all_to_all | solution.py:22
  58.9 154.3 %all-reduce.9.cloned.1.call-start = ((), (), s32[]{:S(2)}) async-start(), calls=%async_computation.1 | async-start | bytes 3145728 | tf_op jit(solution)/shard_map/psum | solution.py:9
  126.3 0.7 copy-start.2
  126.3 1.0 copy-start.3
  126.3 86.9 %copy-start.1 = (f32[4,256,256]{2,1,0:T(8,128)S(1)}, f32[4,256,256]{2,1,0:T(8,128)}, u32[]{:S(2)}) copy-start(f32[4,256,256]{2,1,0:T(8,128)} %param.15) | copy-start | bytes 3145732
  126.3 150.0 %all-reduce.11.cloned.1.call-start = ((), (), s32[]{:S(2)}) async-start(), calls=%async_computation.2 | async-start | bytes 1572864 | tf_op jit(solution)/shard_map/psum | solution.py:9
  129.7 246.3 %all-reduce.13.cloned.1.call-start = ((), (), s32[]{:S(2)}) async-start(), calls=%async_computation.3 | async-start | bytes 3145728 | tf_op jit(solution)/shard_map/psum | solution.py:9
  287.7 151.4 %all-reduce.15.cloned.1.call-start = ((), (), s32[]{:S(2)}) async-start(), calls=%async_computation.4 | async-start | bytes 1572864 | tf_op jit(solution)/shard_map/psum | solution.py:9
  290.0 248.9 %all-reduce.17.cloned.1.call-start = ((), (), s32[]{:S(2)}) async-start(), calls=%async_computation.5 | async-start | bytes 3145728 | tf_op jit(solution)/shard_map/psum | solution.py:9
  450.5 151.3 %all-reduce.19.cloned.1.call-start = ((), (), s32[]{:S(2)}) async-start(), calls=%async_computation.6 | async-start | bytes 1572864 | tf_op jit(solution)/shard_map/psum | solution.py:9
  452.9 248.7 %all-reduce.21.cloned.1.call-start = ((), (), s32[]{:S(2)}) async-start(), calls=%async_computation.7 | async-start | bytes 3145728 | tf_op jit(solution)/shard_map/psum | solution.py:9
  613.3 151.5 %all-reduce.23.cloned.1.call-start = ((), (), s32[]{:S(2)}) async-start(), calls=%async_computation.8 | async-start | bytes 1572864 | tf_op jit(solution)/shard_map/psum | solution.py:9
Sparse Core Ops, SparseCore 0:
  126.5 86.6 all-reduce.8
  215.5 60.7 all-reduce.10
  287.8 88.1 all-reduce.12
  378.4 60.7 all-reduce.14
  450.7 88.1 all-reduce.16
  541.1 60.7 all-reduce.18
  613.4 88.1 all-reduce.20
  704.0 60.7 all-reduce.22
where the time goes:
time: 793 us; the launch traced here: 790 us
  waiting for transfers between devices  619 us (78%)
  other arithmetic  57.8 us (7%)
  local copies, waits for them, and re-layouts  51 us (6%)
  matrix products  41.1 us (5%)
  between operations  13.7 us (2%)
    psum x8, waiting for transfers between devices, spread(): return lax.psum(kept, axis)  581 us
    all_to_all x1, waiting for transfers between devices, permute_rows(): lax.all_to_all(outgoing, 'prow', split_axis=0, concat_axis=0, tiled=True)  37.7 us
    dot_general x4, matrix products, trailing(): jnp.dot(lower, upper, precision=lax.Precision.HIGHEST, preferred_element_...  29.9 us
    select_n x8, other arithmetic, spread(): jnp.where(lax.axis_index(axis) == source, value, 0).astype(value.dtype)  22.6 us
    unnamed x1, other arithmetic  17.2 us
  transfers between devices with their start and end apart: 9, of which 9 were waited for; matrix products, arithmetic and copies ran while one was open for 5% of the time, Pallas kernels for 0%

commit v1 on v0

v1 whole, which is shorter than its diff:
```python
import jax
import jax.numpy as jnp
from jax import lax
from jax.experimental import pallas as pl
from jax.experimental.pallas import tpu as pltpu
from jax.sharding import PartitionSpec as P

HIGH = lax.Precision.HIGH
VMEM = pl.BlockSpec(memory_space=pltpu.VMEM)
SMEM = pl.BlockSpec(memory_space=pltpu.SMEM)
PARAMS = pltpu.CompilerParams(vmem_limit_bytes=48 * 1024 * 1024)


def dot(a, b):
    return jnp.dot(a, b, precision=HIGH, preferred_element_type=jnp.float32)


def send_kernel(order, x, first, rest):
    def step(j, carry):
        r = order[j] * 3
        first[j] = x[r]
        rest[2 * j] = x[r + 1]
        rest[2 * j + 1] = x[r + 2]
        return carry

    lax.fori_loop(0, first.shape[0], step, 0, unroll=8)


def rows_kernel(order, first, rest, out):
    def step(d, carry):
        m = order[d]
        out[3 * d] = first[m]
        out[3 * d + 1] = rest[2 * m]
        out[3 * d + 2] = rest[2 * m + 1]
        return carry

    lax.fori_loop(0, out.shape[0] // 3, step, 0, unroll=8)


def f32(*shape):
    return jax.ShapeDtypeStruct(shape, jnp.float32)


def scatter_x(blocks, here_x):
    got = [
        lax.ppermute(blocks[s], "pcol", [(k, k + 4 * s) for k in range(4)]) for s in range(1, 4)
    ]
    return jnp.where(here_x == 0, blocks[0], got[0] + got[1] + got[2])


def body(matrix, row_order, inverses, lower_fill, upper_fill):
    here_row = lax.axis_index("prow")
    here_col = lax.axis_index("pcol")
    here_x = here_col // 4
    core = here_row % 2
    x = matrix.reshape(4608, 2, 128)
    targets = row_order.reshape(6, 8, 256).transpose(1, 0, 2).reshape(8, 1536)
    local = jnp.arange(1536, dtype=jnp.int32)

    def keys(t):
        owner, row = t // 256 % 8, t // 2048 * 256 + t % 256
        return (owner * 2048 + local) * 2048 + row

    mine = lax.dynamic_slice(targets, (here_row, 0), (1, 1536))[0]
    order = lax.sort(keys(mine)) // 2048 % 2048
    first, rest = pl.pallas_call(
        send_kernel,
        out_shape=(f32(1536, 2, 128), f32(3072, 2, 128)),
        in_specs=[SMEM, VMEM],
        out_specs=(VMEM, VMEM),
        compiler_params=PARAMS,
        name="send_rows",
    )(order, x)
    quarters = first.reshape(8, 4, 96, 128).transpose(1, 0, 2, 3)
    mine_q = scatter_x(quarters, here_x)
    mine_q = lax.all_to_all(mine_q, "prow", 0, 0, tiled=True).reshape(384, 256)
    got_first = lax.all_to_all(first.reshape(8, 384, 128), "prow", 0, 0, tiled=True)
    got_rest = lax.all_to_all(rest.reshape(8, 768, 128), "prow", 0, 0, tiled=True)
    all_keys = lax.sort(keys(targets), dimension=1)
    places = lax.dynamic_slice(all_keys, (0, here_row * 192), (8, 192)).reshape(1536) % 2048
    backward = lax.sort(places * 2048 + local) % 2048
    got_first = got_first.reshape(1536, 2, 128)
    got_rest = got_rest.reshape(3072, 2, 128)
    top = pl.pallas_call(
        rows_kernel,
        out_shape=f32(768, 2, 128),
        in_specs=[SMEM, VMEM, VMEM],
        out_specs=VMEM,
        compiler_params=PARAMS,
        name="top_rows",
    )(backward[:256], got_first, got_rest).reshape(256, 768)
    half = lax.ppermute(top[128:], "prow", [(p, p + 4) for p in range(4)])
    piece = jnp.where(here_row < 4, top[:128], half)
    rows = lax.all_gather(piece, "prow", axis=0, tiled=True).reshape(2, 4, 128, 768)
    rows = rows.transpose(1, 0, 2, 3).reshape(1024, 768)
    columns = lax.all_gather(mine_q, "pcol", axis=0, tiled=True)
    columns = columns.reshape(4, 4, 8, 48, 256).transpose(1, 2, 0, 3, 4).reshape(4, 1536, 256)
    corner = lax.dynamic_slice(rows, (core * 512, 0), (512, 256)).reshape(4, 128, 256)
    corner = lax.all_gather(scatter_x(corner, here_x), "pcol", axis=0, tiled=True)
    corner = corner.reshape(4, 4, 128, 256).transpose(1, 0, 2, 3).reshape(4, 512, 256)
    other = lax.ppermute(corner, "prow", [(p, p ^ 1) for p in range(8)])
    corner = jnp.where(core == 0, jnp.stack([corner, other]), jnp.stack([other, corner]))
    corner = corner.reshape(2, 4, 2, 256, 256)
    tl = [[corner[i // 2, j, i % 2] for j in range(4)] for i in range(4)]
    lf = (lower_fill == 1).astype(jnp.float32)
    uf = (upper_fill == 1).astype(jnp.float32)
    low, upp = {}, {}
    for k in range(4):
        for m in range(k):
            t = tl[k][m]
            for n in range(m):
                t = t - dot(low[k, n], upp[n, m])
            low[k, m] = dot(t, inverses[m]) * lf[m, k]
        for j in range(k + 1, 4):
            t = tl[k][j]
            for m in range(k):
                t = t - dot(low[k, m], upp[m, j])
            upp[k, j] = t * uf[k, j]
    blocks = jnp.arange(3, dtype=jnp.int32) * 16 + here_col
    upper = []
    for k in range(4):
        keep = jnp.where(blocks > k, uf[k][blocks], 0.0)
        t = rows[256 * k : 256 * k + 256]
        for m in range(k):
            t = t - dot(low[k, m], upper[m])
        upper.append(t * jnp.repeat(keep, 256)[None, :])
    row_block = places // 256 * 8 + here_row
    lower = []
    for k in range(4):
        keep6 = jnp.arange(6, dtype=jnp.int32) * 8 + here_row
        keep6 = jnp.where(keep6 > k, lf[k][keep6], 0.0)
        keep = jnp.zeros((1536,), jnp.float32)
        for r in range(6):
            keep = jnp.where(places // 256 == r, keep6[r], keep)
        t = columns[k]
        for m in range(k):
            t = t - dot(lower[m], upp[m, k])
        lower.append(dot(t, inverses[k]) * keep[:, None])
    lower = jnp.concatenate(lower, axis=1)
    upper = jnp.concatenate(upper, axis=0)
    done = dot(lower, upper)
    new_first = got_first.reshape(1536, 256) - done[:, :256]
    own = lax.dynamic_slice(lower, (0, jnp.minimum(here_col, 3) * 256), (1536, 256))
    new_first = jnp.where(((here_col < 4) & (row_block > here_col))[:, None], own, new_first)
    new_rest = got_rest.reshape(1536, 512) - done[:, 256:]
    out = pl.pallas_call(
        rows_kernel,
        out_shape=f32(4608, 2, 128),
        in_specs=[SMEM, VMEM, VMEM],
        out_specs=VMEM,
        compiler_params=PARAMS,
        name="place_rows",
    )(backward, new_first.reshape(1536, 2, 128), new_rest.reshape(3072, 2, 128))
    return out.reshape(6, 1, 256, 3, 1, 256)


def solution(mesh):
    in_specs = (P(None, "prow", None, None, "pcol", None), P(), P(), P(), P())
    out_specs = P(None, "prow", None, None, "pcol", None)
    return jax.shard_map(body, mesh=mesh, in_specs=in_specs, out_specs=out_specs, check_vma=False)
```

time: 793 us -> 360 us (0.45)
  waiting for transfers between devices: 619 us -> 105 us
  blocking collectives: 0 us -> 41.4 us
  local copies, waits for them, and re-layouts: 51 us -> 68.5 us
  starting transfers between devices: 7.72 us -> 22.1 us
  other arithmetic: 57.8 us -> 43.5 us
  Pallas kernels: 0 us -> 12.8 us
  matrix products: 41.1 us -> 51.6 us
    psum x8 -> x0, waiting for transfers between devices: 581 us -> none  [spread(): return lax.psum(kept, axis)]
    all_gather x0 -> x3, waiting for transfers between devices: none -> 60 us  [the longest x1 32.2 us: body(): lax.all_gather(piece, 'prow', axis=0, tiled=True).reshape(2, 4, 128, 768)]
    all_to_all x0 -> x2, blocking collectives: none -> 41.4 us  [the longest x1 27.5 us: body(): lax.all_to_all(first.reshape(8, 384, 128), 'prow', 0, 0, tiled=True)]
    ppermute x0 -> x8, waiting for transfers between devices: none -> 22.6 us  [the longest x6 16.3 us: scatter_x(): lax.ppermute(blocks[s], 'pcol', [(k, k + 4 * s) for k in range(4)])]
    gather x3 -> x8, local copies, waits for them, and re-layouts: 25.4 us -> 5.14 us  [the longest x4 2.59 us: body(): keep6 = jnp.where(keep6 > k, lf[k][keep6], 0.0)]
    ppermute x0 -> x8, starting transfers between devices: none -> 17.4 us  [the longest x6 13.6 us: scatter_x(): lax.ppermute(blocks[s], 'pcol', [(k, k + 4 * s) for k in range(4)])]
    unnamed x1 -> x0, other arithmetic: 17.2 us -> none
    all_to_all x1, waiting for transfers between devices: 37.7 us -> 22.9 us  [body(): lax.all_to_all(rest.reshape(8, 768, 128), 'prow', 0, 0, tiled=True)]
  transfers between devices with their start and end apart: 9 -> 12, of which waited for: 9 -> 8; matrix products, arithmetic and copies ran while one was open for 5% -> 16% of each run, Pallas kernels for 0% -> 0%
where the time goes in v1:
time: 360 us; the launch traced here: 359 us
  waiting for transfers between devices  105 us (29%)
  local copies, waits for them, and re-layouts  68.5 us (19%)
  matrix products  51.6 us (14%)
  other arithmetic  43.5 us (12%)
  blocking collectives  41.4 us (12%)
  starting transfers between devices  22.1 us (6%)
  between operations  14 us (4%)
  Pallas kernels  12.8 us (4%)
    dot_general x31, matrix products, dot(): return jnp.dot(a, b, precision=HIGH, preferred_element_type=jnp.float32)  51.6 us
    all_gather x1, waiting for transfers between devices, body(): lax.all_gather(piece, 'prow', axis=0, tiled=True).reshape(2, 4, 128, 768)  32.2 us
    all_gather x1, waiting for transfers between devices, body(): columns = lax.all_gather(mine_q, 'pcol', axis=0, tiled=True)  27.8 us
    all_to_all x1, blocking collectives, body(): lax.all_to_all(first.reshape(8, 384, 128), 'prow', 0, 0, tiled=True)  27.5 us
    all_to_all x1, waiting for transfers between devices, body(): lax.all_to_all(rest.reshape(8, 768, 128), 'prow', 0, 0, tiled=True)  22.9 us
    ppermute x6, waiting for transfers between devices, scatter_x(): lax.ppermute(blocks[s], 'pcol', [(k, k + 4 * s) for k in range(4)])  16.3 us
    select_n x3, other arithmetic, body(): keep = jnp.where(places // 256 == r, keep6[r], keep)  14.9 us
    all_to_all x1, blocking collectives, body(): mine_q = lax.all_to_all(mine_q, 'prow', 0, 0, tiled=True).reshape(384, 256)  13.9 us
  transfers between devices with their start and end apart: 12, of which 8 were waited for; matrix products, arithmetic and copies ran while one was open for 16% of the time, Pallas kernels for 0%

profile of v1, /device:TPU:1, one launch (start us, length us, event | category | flops | bytes accessed | tf_op | source)
XLA Modules:
  0.0 359.3 jit_solution(13792532095440488266)
XLA Ops:
  7.4 5.0 %sort.37 = (s32[1536]{0:T(1024)S(1)}, s32[1536]{0:T(1024)}) sort(s32[1536]{0:T(1024)S(1)} %fusion.99, s32[1536]{0:T(1024)S(1)} %iota.32), dimensions={0}, to_apply=%region_2.3 | sort | flops 16896 | bytes 24576 | tf_op jit(solution)/shard_map/sort | solution.py:65
  12.5 5.3 %send_rows.1 = (f32[1536,2,128]{2,1,0:T(2,128)S(1)}, f32[3072,2,128]{2,1,0:T(2,128)S(1)}) custom-call(s32[1536]{0:T(1024)S(1)} %add_select_fusion.4.order, f32[4608,2,128]{2,1,0:T(2,128)} %bitcast.247), custom_call_target="tpu_custom_call" | custom-call | tf_op jit(solution)/shard_map/send_rows/pallas_call | solution.py:66
  17.8 1.7 copy-done.3
  19.4 27.5 %all_to_all.15 = f32[8,384,128]{2,1,0:T(8,128)} all-to-all(f32[8,384,128]{2,1,0:T(8,128)S(1)} %bitcast.234), channel_id=1, replica_groups=mesh['prow'=8,'pcol'=16] {'prow'}, dimensions={0} | all-to-all | bytes 3145728 | tf_op jit(solution)/shard_map/all_to_all | solution.py:77
  46.9 4.6 %all-to-all-start.2 = ((f32[8,768,128]{2,1,0:T(8,128)}), f32[8,768,128]{2,1,0:T(8,128)S(1)}, u32[]{:S(2)}, u32[]{:S(2)}) async-start(f32[8,768,128]{2,1,0:T(8,128)} %bitcast.237), calls=%async_computation.2 | async-start | bytes 6291456 | tf_op jit(solution)/shard_map/all_to_all | solution.py:78
  52.3 8.0 %sort.39.cloned.1.call-done = s32[8,1536]{1,0:T(8,128)} async-done(((s32[8,1536]{1,0:T(8,128)}), s32[8,1536]{1,0:T(8,128)}) %sort.39.cloned.1.call-update) | async-done | bytes 49168 | tf_op jit(solution)/shard_map/sort | solution.py:79
  61.2 5.0 %sort.36 = (s32[1536]{0:T(1024)S(1)}, s32[1536]{0:T(1024)}) sort(s32[1536]{0:T(1024)S(1)} %iota_add_fusion, s32[1536]{0:T(1024)S(1)} %iota.30), dimensions={0}, to_apply=%region_1.2 | sort | flops 16896 | bytes 24576 | tf_op jit(solution)/shard_map/sort | solution.py:81
  66.2 22.9 %all-to-all-done.2 = f32[8,768,128]{2,1,0:T(8,128)S(1)} async-done(((f32[8,768,128]{2,1,0:T(8,128)}), f32[8,768,128]{2,1,0:T(8,128)S(1)}, u32[]{:S(2)}, u32[]{:S(2)}) %all-to-all-start.2) | async-done | bytes 3145760 | tf_op jit(solution)/shard_map/all_to_all | solution.py:78
  92.4 2.1 slice.293
  94.5 2.9 collective-permute-start.3
  98.5 6.3 %collective-permute-done.3 = f32[128,768]{1,0:T(8,128)} collective-permute-done((f32[128,768]{1,0:T(8,128)}, f32[128,768]{1,0:T(8,128)}, u32[]{:S(2)}, u32[]{:S(2)}) %collective-permute-start.3) | collective-permute-done | bytes 393248 | tf_op jit(solution)/shard_map/ppermute | solution.py:92
  104.8 1.8 broadcast_select_fusion
  106.7 32.2 %all-gather.6.cloned.1.call-done = f32[1024,768]{1,0:T(8,128)} async-done(((f32[128,768]{1,0:T(8,128)}), f32[1024,768]{1,0:T(8,128)}) %all-gather.6.cloned.1.call-update) | async-done | bytes 3145744 | tf_op jit(solution)/shard_map/all_gather | solution.py:94
  138.9 2.2 copy.44
  141.2 1.7 copy-done.4
  143.6 4.6 %collective-permute-start.5 = (f32[128,256]{1,0:T(8,128)}, f32[128,256]{1,0:T(8,128)S(1)}, u32[]{:S(2)}, u32[]{:S(2)}) collective-permute-start(f32[128,256]{1,0:T(8,128)} %get-tuple-element.32), channel_id=1, source_target_pairs={{0,8},{1,9},{2,10},{3,11},{16,24},{17,25},{18,26},{19,27},{32,40},... | collective-permute-start | bytes 393224 | tf_op jit(solution)/shard_map/ppermute | solution.py:46
  151.1 2.8 collective-permute-done.4
  153.9 1.6 dynamic-slice_select_fusion
  156.9 2.7 collective-permute-start.1
  159.6 2.0 collective-permute-start
  161.6 1.7 collective-permute-start.2
  163.3 2.9 collective-permute-done.1
  166.3 10.3 %collective-permute-done = f32[8,96,128]{2,1,0:T(8,128)S(1)} collective-permute-done((f32[8,96,128]{2,1,0:T(8,128)S(1)}, f32[8,96,128]{2,1,0:T(8,128)S(1)}, u32[]{:S(2)}, u32[]{:S(2)}) %collective-permute-start) | collective-permute-done | bytes 393248 | tf_op jit(solution)/shard_map/ppermute | solution.py:46
  177.7 13.9 %all_to_all.16 = f32[8,96,128]{2,1,0:T(8,128)S(1)} all-to-all(f32[8,96,128]{2,1,0:T(8,128)S(1)} %fusion.12), channel_id=1, replica_groups=mesh['prow'=8,'pcol'=16] {'prow'}, dimensions={0} | all-to-all | bytes 786432 | tf_op jit(solution)/shard_map/all_to_all | solution.py:76
  202.7 3.1 copy.29
  206.6 3.7 %select_select_fusion = (f32[1536]{0:T(1024)S(1)}, pred[1536]{0:T(1024)(128)(4,1)S(1)}, pred[1536]{0:T(1024)(128)(4,1)S(1)}, pred[1536]{0:T(1024)(128)(4,1)S(1)}...) fusion(f32[]{:T(128)} %bitcast.81, f32[]{:T(128)} %bitcast.80, ...), kind=kLoop, calls=%fused_computation.181 | loop fusion | flops 18432 | bytes 21528 | tf_op jit(solution)/shard_map/jit(_where)/select_n | solution.py:134
  210.4 3.9 %select_select_fusion.3 = f32[1536]{0:T(1024)S(1)} fusion(pred[1536]{0:T(1024)(128)(4,1)S(1)} %get-tuple-element.23, pred[1536]{0:T(1024)(128)(4,1)S(1)} %get-tuple-element.22, pred[1536]{0:T(1024)(128)(4,1)S(1)} %get-tuple-element.21, pred[1536]{0:T(1024)(128)(4,1)S(1)} %get-tuple-element.20, pred[1536]{0:T(1024)(128)(4,1)S(1)} %get-tuple-element.19, ...), kind=kLoop, calls=%fused_computation.184 | loop fusion | flops 9216 | bytes 15384 | tf_op jit(solution)/shard_map/jit(_where)/select_n | solution.py:134
  214.2 7.4 %select_select_fusion.1 = (f32[1536]{0:T(1024)S(1)}, f32[1536]{0:T(1024)S(1)}) fusion(pred[1536]{0:T(1024)(128)(4,1)S(1)} %get-tuple-element.23, pred[1536]{0:T(1024)(128)(4,1)S(1)} %get-tuple-element.22, pred[1536]{0:T(1024)(128)(4,1)S(1)} %get-tuple-element.21, pred[1536]{0:T(1024)(128)(4,1)S(1)} %get-tuple-element.20, ...), kind=kLoop, calls=%fused_computation.182 | loop fusion | flops 18432 | bytes 21552 | tf_op jit(solution)/shard_map/jit(_where)/select_n | solution.py:134
  221.6 2.7 reshape_reshape.6
  224.4 3.1 copy.33
  227.4 2.3 reshape_reshape.7
  229.7 4.0 %copy.35 = f32[1536,512]{0,1:T(8,128)} copy(f32[1536,512]{1,0:T(8,128)} %reshape_reshape.7) | data formatting | bytes 6291456 | tf_op jit(solution)/shard_map/reshape;reshape | solution.py:145
  236.1 27.8 %all-gather.4.cloned.1.call-done = f32[6144,256]{1,0:T(8,128)} async-done(((f32[384,256]{1,0:T(8,128)}), f32[6144,256]{1,0:T(8,128)}) %all-gather.4.cloned.1.call-update) | async-done | bytes 6291472 | tf_op jit(solution)/shard_map/all_gather | solution.py:96
  263.9 3.5 fusion.115
  269.9 4.0 %maximum_select_fusion = f32[2,4,2,256,256]{4,3,2,1,0:T(8,128)S(1)} fusion(f32[1,4,2,256,256]{4,3,2,1,0:T(8,128)} %bitcast.37, f32[1,4,2,256,256]{4,3,2,1,0:T(8,128)} %bitcast.34, pred[]{:T(512)S(6)} %eq.146), kind=kLoop, calls=%fused_computation.9 | loop fusion | flops 3145728 | bytes 8388609 | tf_op jit(solution)/shard_map/jit(_where)/select_n | solution.py:102
  279.5 2.0 convolution_subtract_fusion.2
  281.5 2.1 convolution_subtract_fusion.4
  283.5 2.1 convolution_subtract_fusion.5
  293.1 13.9 %convolution_subtract_fusion.3 = f32[1536,256]{1,0:T(8,128)S(1)} fusion(f32[1536,256]{1,0:T(8,128)S(1)} %convolution_subtract_fusion.4, f32[1536,256]{0,1:T(8,128)S(1)} %convolution_multiply_fusion.2, f32[256,256]{1,0:T(8,128)S(1)} %fusion.28), kind=kOutput, calls=%fused_computation.24 | convolution fusion | flops 604372992 | bytes 4980736 | tf_op jit(solution)/shard_map/dot_general | solution.py:15
  310.8 2.1 convolution_subtract_fusion
  313.8 2.9 pad_maximum_fusion
  319.9 8.3 %fusion = f32[1536,768]{0,1:T(8,128)S(1)} fusion(f32[256,768]{1,0:T(8,128)S(1)} %fusion.9, f32[256,768]{1,0:T(8,128)S(1)} %fusion.10, f32[256,768]{1,0:T(8,128)S(1)} %fusion.11, f32[256,768]{1,0:T(8,128)S(1)} %copy-done.7, f32[1536,256]{0,1:T(8,128)S(1)} %convolution_multiply_fusion, f32[1536,256]{0,1:T(8,128)S(1)} %convolution_multiply_fusion.1, ...), kind=kOutput, calls=%fused_computation.11 | convolution fusion | flops 7254835200 | bytes 14155776 | tf_op jit(solution)/shard_map/dot_general | solution.py:15
  328.2 2.2 copy-done.9
  331.0 2.4 copy.36
  333.4 3.8 %reshape.250.rest = f32[3072,2,128]{2,1,0:T(2,128)S(1)} reshape(f32[1536,512]{1,0:T(8,128)} %copy.36) | data formatting | bytes 6291456 | tf_op jit(solution)/shard_map/reshape | solution.py:153
  337.2 4.0 %fusion.8 = f32[1536,256]{0,1:T(8,128)} fusion(f32[1536,256]{0,1:T(8,128)} %copy.33, f32[1536,768]{0,1:T(8,128)} %copy-done.9, f32[1536,1024]{0,1:T(8,128)} %pad_maximum_fusion, s32[]{:T(128)S(6)} %select_n.446, pred[1536]{0:T(1024)(128)(4,1)S(1)} %get-tuple-element.15), kind=kLoop, calls=%fused_computation.30 | loop fusion | flops 786432 | bytes 6292996 | tf_op jit(solution)/shard_map/jit(_where)/select_n | solution.py:144
  341.1 3.6 %copy.38.first = f32[1536,2,128]{2,1,0:T(2,128)} copy(f32[1536,2,128]{0,2,1:T(8,128)} %bitcast.245) | data formatting | bytes 3145728 | tf_op jit(solution)/shard_map/reshape | solution.py:153
  346.2 6.4 %place_rows.1 = f32[4608,2,128]{2,1,0:T(2,128)} custom-call(s32[1536]{0:T(1024)S(1)} %add_select_fusion.11.order, f32[1536,2,128]{2,1,0:T(2,128)S(1)} %copy-done.2, f32[3072,2,128]{2,1,0:T(2,128)S(1)} %reshape.250.rest), custom_call_target="tpu_custom_call" | custom-call | tf_op jit(solution)/shard_map/place_rows/pallas_call | solution.py:146
  (127 shorter events, 52.5 us)
Async XLA Ops:
  17.8 1.7 copy-start.3
  19.4 27.5 %copy-start.1 = (f32[1536,2,128]{2,1,0:T(2,128)}, f32[1536,2,128]{2,1,0:T(2,128)S(1)}, u32[]{:S(2)}) copy-start(f32[1536,2,128]{2,1,0:T(2,128)S(1)} %get-tuple-element.13) | copy-start | bytes 4718596
  46.9 42.2 %all-to-all-start.2 = ((f32[8,768,128]{2,1,0:T(8,128)}), f32[8,768,128]{2,1,0:T(8,128)S(1)}, u32[]{:S(2)}, u32[]{:S(2)}) async-start(f32[8,768,128]{2,1,0:T(8,128)} %bitcast.237), calls=%async_computation.2 | async-start | bytes 6291456 | tf_op jit(solution)/shard_map/all_to_all | solution.py:78
  51.5 8.8 %sort.39.cloned.1.call-start = ((), (), s32[]{:S(2)}) async-start(), calls=%async_computation.6 | async-start | bytes 147488 | tf_op jit(solution)/shard_map/sort | solution.py:79
  52.2 86.7 %all-gather.6.cloned.1.call-start = ((), (), s32[]{:S(2)}) async-start(), calls=%async_computation.4 | async-start | bytes 3538944 | tf_op jit(solution)/shard_map/all_gather | solution.py:94
  89.1 1.4 copy-start
  94.5 10.3 %collective-permute-start.3 = (f32[128,768]{1,0:T(8,128)}, f32[128,768]{1,0:T(8,128)}, u32[]{:S(2)}, u32[]{:S(2)}) collective-permute-start(f32[128,768]{1,0:T(8,128)} %slice.293), channel_id=1, source_target_pairs={{0,64},{16,80},{32,96},{48,112},{1,65},{17,81},{33,97},{49,113},{2... | collective-permute-start | bytes 1179656 | tf_op jit(solution)/shard_map/ppermute | solution.py:92
  106.6 96.1 %all-gather.8.cloned.1.call-start = ((), (), s32[]{:S(2)}) async-start(), calls=%async_computation.5 | async-start | bytes 2228224 | tf_op jit(solution)/shard_map/all_gather | solution.py:99
  141.2 1.7 copy-start.4
  143.6 7.5 %collective-permute-start.5 = (f32[128,256]{1,0:T(8,128)}, f32[128,256]{1,0:T(8,128)S(1)}, u32[]{:S(2)}, u32[]{:S(2)}) collective-permute-start(f32[128,256]{1,0:T(8,128)} %get-tuple-element.32), channel_id=1, source_target_pairs={{0,8},{1,9},{2,10},{3,11},{16,24},{17,25},{18,26},{19,27},{32,40},... | collective-permute-start | bytes 393224 | tf_op jit(solution)/shard_map/ppermute | solution.py:46
  148.2 5.7 %collective-permute-start.4 = (f32[128,256]{1,0:T(8,128)}, f32[128,256]{1,0:T(8,128)S(1)}, u32[]{:S(2)}, u32[]{:S(2)}) collective-permute-start(f32[128,256]{1,0:T(8,128)} %get-tuple-element.33), channel_id=1, source_target_pairs={{0,4},{1,5},{2,6},{3,7},{16,20},{17,21},{18,22},{19,23},{32,36},{3... | collective-permute-start | bytes 393224 | tf_op jit(solution)/shard_map/ppermute | solution.py:46
  149.5 4.4 %collective-permute-start.6 = (f32[128,256]{1,0:T(8,128)}, f32[128,256]{1,0:T(8,128)S(1)}, u32[]{:S(2)}, u32[]{:S(2)}) collective-permute-start(f32[128,256]{1,0:T(8,128)} %get-tuple-element.34), channel_id=1, source_target_pairs={{0,12},{1,13},{2,14},{3,15},{16,28},{17,29},{18,30},{19,31},{32,44... | collective-permute-start | bytes 393224 | tf_op jit(solution)/shard_map/ppermute | solution.py:46
  155.5 108.3 %all-gather.4.cloned.1.call-start = ((), (), s32[]{:S(2)}) async-start(), calls=%async_computation.3 | async-start | bytes 6684672 | tf_op jit(solution)/shard_map/all_gather | solution.py:96
  156.9 9.3 %collective-permute-start.1 = (f32[8,96,128]{2,1,0:T(8,128)S(1)}, f32[8,96,128]{2,1,0:T(8,128)S(1)}, u32[]{:S(2)}, u32[]{:S(2)}) collective-permute-start(f32[8,96,128]{2,1,0:T(8,128)S(1)} %get-tuple-element.37), channel_id=1, source_target_pairs={{0,8},{1,9},{2,10},{3,11},{16,24},{17,25},{18,26},{19,27},{32,40},... | collective-permute-start | bytes 1179656 | tf_op jit(solution)/shard_map/ppermute | solution.py:46
  159.6 16.9 %collective-permute-start = (f32[8,96,128]{2,1,0:T(8,128)S(1)}, f32[8,96,128]{2,1,0:T(8,128)S(1)}, u32[]{:S(2)}, u32[]{:S(2)}) collective-permute-start(f32[8,96,128]{2,1,0:T(8,128)S(1)} %get-tuple-element.38), channel_id=1, source_target_pairs={{0,4},{1,5},{2,6},{3,7},{16,20},{17,21},{18,22},{19,23},{32,36},{3... | collective-permute-start | bytes 1179656 | tf_op jit(solution)/shard_map/ppermute | solution.py:46
  161.6 14.9 %collective-permute-start.2 = (f32[8,96,128]{2,1,0:T(8,128)S(1)}, f32[8,96,128]{2,1,0:T(8,128)S(1)}, u32[]{:S(2)}, u32[]{:S(2)}) collective-permute-start(f32[8,96,128]{2,1,0:T(8,128)S(1)} %get-tuple-element.39), channel_id=1, source_target_pairs={{0,12},{1,13},{2,14},{3,15},{16,28},{17,29},{18,30},{19,31},{32,44... | collective-permute-start | bytes 1179656 | tf_op jit(solution)/shard_map/ppermute | solution.py:46
  192.4 3.3 copy-start.13
  205.8 64.1 %collective-permute-start.7 = (f32[4,512,256]{2,1,0:T(8,128)}, f32[4,512,256]{2,1,0:T(8,128)}, u32[]{:S(2)}, u32[]{:S(2)}) collective-permute-start(f32[4,512,256]{2,1,0:T(8,128)} %bitcast.36), channel_id=1, source_target_pairs={{0,16},{16,0},{32,48},{48,32},{64,80},{80,64},{96,112},{112,96},{1... | collective-permute-start | bytes 6291464 | tf_op jit(solution)/shard_map/ppermute | solution.py:101
  229.7 4.0 %copy-start.5 = (f32[2,4,128,768]{3,2,0,1:T(8,128)S(1)}, f32[2,4,128,768]{3,2,0,1:T(8,128)}, u32[]{:S(2)}) copy-start(f32[2,4,128,768]{3,2,0,1:T(8,128)} %copy-done.4) | copy-start | bytes 9437188
  267.8 1.2 copy-start.8
  307.1 1.4 copy-start.7
  307.1 1.4 copy-start.12
  308.2 1.2 copy-start.11
  313.8 2.9 copy-start.10
  319.9 10.5 %copy-start.6 = (f32[1536,512]{0,1:T(8,128)S(1)}, f32[1536,512]{0,1:T(8,128)}, u32[]{:S(2)}) copy-start(f32[1536,512]{0,1:T(8,128)} %copy.35) | copy-start | bytes 9437188
  328.2 2.2 copy-start.9
  344.8 1.4 copy-start.2
Sparse Core Ops, SparseCore 0:
  54.8 5.2 sort.41.cloned.1.call-done
  106.7 32.1 all-gather.5
  155.7 44.7 all-gather.7
  202.5 61.3 all-gather.3
  (1 shorter events, 0.0 us)

commit v2 on v1

v2 whole, which is shorter than its diff:
```python
import jax
import jax.numpy as jnp
from jax import lax
from jax.experimental import pallas as pl
from jax.experimental.pallas import tpu as pltpu
from jax.sharding import PartitionSpec as P

VMEM = pl.BlockSpec(memory_space=pltpu.VMEM)
SMEM = pl.BlockSpec(memory_space=pltpu.SMEM)
PARAMS = pltpu.CompilerParams(vmem_limit_bytes=50 * 1024 * 1024)
BF = jnp.bfloat16


def f32(*shape):
    return jax.ShapeDtypeStruct(shape, jnp.float32)


def b16(*shape):
    return jax.ShapeDtypeStruct(shape, BF)


def split(t):
    high = t.astype(BF)
    return high, (t - high.astype(jnp.float32)).astype(BF)


def dot3(a, b):
    dot = lambda u, v: jnp.dot(u, v, preferred_element_type=jnp.float32)
    return dot(a[0], b[0]) + (dot(a[0], b[1]) + dot(a[1], b[0]))


def permute_kernel(order, *refs):
    half = len(refs) // 2

    def step(j, carry):
        m = order[j]
        for src, dst in zip(refs[:half], refs[half:]):
            dst[j] = src[m]
        return carry

    lax.fori_loop(0, refs[half].shape[0], step, 0, unroll=8)


def send_rows(order, x, columns):
    specs = [pl.BlockSpec((1536, None, 2, 128), lambda i, c=c: (0, c, 0, 0)) for c in columns]
    return pl.pallas_call(
        permute_kernel,
        out_shape=[f32(1536, 2, 128)] * len(columns),
        grid=(1,),
        in_specs=[SMEM] + specs,
        out_specs=[pl.BlockSpec((1536, 2, 128), lambda i: (0, 0, 0))] * len(columns),
        compiler_params=PARAMS,
        name="send_rows",
    )(order, *[x] * len(columns))


def place_rows(order, arrived):
    return pl.pallas_call(
        permute_kernel,
        out_shape=f32(1536, 2, 128),
        in_specs=[SMEM, VMEM],
        out_specs=VMEM,
        compiler_params=PARAMS,
        name="place_rows",
    )(order, arrived)


def pair(ref, index, start, rows):
    left = ref[index + (pl.ds(2 * start, rows, stride=2),)]
    right = ref[index + (pl.ds(2 * start + 1, rows, stride=2),)]
    return jnp.concatenate([left, right], axis=1)


NUMBER = {(0, 1): 0, (0, 2): 1, (0, 3): 2, (1, 2): 3, (1, 3): 4, (2, 3): 5}


def upper_kernel(
    place, lower_fill, upper_fill, own, other, r0, r1, r2, inv, uh, ul, vh, vl, ih, il, corner
):
    here_x, here_y, core, here_col = place[0], place[1], place[2], place[3]
    for half in range(2):
        for i in range(4):
            for k in range(4):
                b = 2 * half + i // 2
                if b == k:
                    continue
                at = (lax.rem(here_x - i + 4, 4), lax.rem(here_y - k + 4, 4))
                rows = slice(128 * (i % 2), 128 * (i % 2) + 128)

                @pl.when(core == half)
                def _():
                    corner[b, k, rows, :] = pair(own, at, 0, 128)

                @pl.when(core != half)
                def _():
                    corner[b, k, rows, :] = pair(other, at, 0, 128)

    for k in range(4):
        ih[k], il[k] = split(inv[k])
    low = {}
    for k in range(4):
        for m in range(k):
            t = corner[k, m]
            for n in range(m):
                e = NUMBER[n, m]
                t = t - dot3(low[k, n], (vh[e], vl[e]))
            keep = (lower_fill[m, k] == 1).astype(jnp.float32)
            low[k, m] = split(dot3(split(t), (ih[m], il[m])) * keep)
        for j in range(k + 1, 4):
            t = corner[k, j]
            for m in range(k):
                e = NUMBER[m, j]
                t = t - dot3(low[k, m], (vh[e], vl[e]))
            keep = (upper_fill[k, j] == 1).astype(jnp.float32)
            vh[NUMBER[k, j]], vl[NUMBER[k, j]] = split(t * keep)
        for c, ref in enumerate((r0, r1, r2)):
            cols = slice(256 * c, 256 * c + 256)
            t = pair(ref, (k,), 0, 256)
            for m in range(k):
                before = slice(256 * m, 256 * m + 256)
                t = t - dot3(low[k, m], (uh[before, cols], ul[before, cols]))
            block = c * 16 + here_col
            keep = ((block > k) & (upper_fill[k, block] == 1)).astype(jnp.float32)
            mine = slice(256 * k, 256 * k + 256)
            uh[mine, cols], ul[mine, cols] = split(t * keep)


def update_kernel(
    place, lower_fill, panels, p0, p1, p2, uh, ul, vh, vl, ih, il, out, lh, ll, kept
):
    here_col, here_row = place[3], place[4]
    i = pl.program_id(0)
    row = lax.broadcasted_iota(jnp.int32, (384, 1), 0)
    blocks = [(3 * i + g) // 2 * 8 + here_row for g in range(3)]
    rowblock = jnp.where(row < 128, blocks[0], jnp.where(row < 256, blocks[1], blocks[2]))
    for k in range(4):
        cols = slice(256 * k, 256 * k + 256)
        t = pair(panels, (0, k), 0, 384)
        for m in range(k):
            e, before = NUMBER[m, k], slice(256 * m, 256 * m + 256)
            t = t - dot3((lh[:, before], ll[:, before]), (vh[e], vl[e]))
        keep = [((b > k) & (lower_fill[k, b] == 1)).astype(jnp.float32) for b in blocks]
        keep = jnp.where(row < 128, keep[0], jnp.where(row < 256, keep[1], keep[2]))
        t = dot3(split(t), (ih[k], il[k])) * keep
        lh[:, cols], ll[:, cols] = split(t)

        @pl.when(here_col == k)
        def _():
            kept[...] = t

    for c, ref in enumerate((p0, p1, p2)):
        cols = slice(256 * c, 256 * c + 256)
        t = dot3((lh[...], ll[...]), (uh[:, cols], ul[:, cols]))
        t = pair(ref, (), 0, 384) - t
        if c == 0:
            t = jnp.where((here_col < 4) & (rowblock > here_col), kept[...], t)
        out[pl.ds(2 * c, 384, stride=6), :] = t[:, :128]
        out[pl.ds(2 * c + 1, 384, stride=6), :] = t[:, 128:]


def whole(*shape):
    return pl.BlockSpec(shape, lambda i: (0,) * len(shape))


def scatter_x(blocks, here_x):
    got = [
        lax.ppermute(blocks[s], "pcol", [(k, k + 4 * s) for k in range(4)]) for s in range(1, 4)
    ]
    return jnp.where(here_x == 0, blocks[0], got[0] + got[1] + got[2])


def spread_z(top, here_z, core):
    def go(value, pairs):
        return lax.ppermute(value, "prow", [(2 * a + c, 2 * b + c) for a, b in pairs for c in (0, 1)])

    away = go(top, [(0, 3), (1, 2)])
    near = go(top, [(0, 1), (1, 0)])
    on = go(away, [(3, 2), (2, 3)])
    d0 = jnp.where(here_z == 0, top, jnp.where(here_z == 1, near, jnp.where(here_z == 2, on, away)))
    d1 = jnp.where(here_z == 1, top, jnp.where(here_z == 0, near, jnp.where(here_z == 3, on, away)))
    mine = jnp.stack([d0, d1])
    other = lax.ppermute(mine, "prow", [(p, p ^ 1) for p in range(8)])
    even, odd = jnp.where(core == 0, mine, other), jnp.where(core == 0, other, mine)
    return jnp.stack([even, odd], axis=1).reshape(4, 512, 128)


def body(matrix, row_order, inverses, lower_fill, upper_fill):
    here_row = lax.axis_index("prow")
    here_col = lax.axis_index("pcol")
    here_x, here_y = here_col // 4, here_col % 4
    here_z, core = here_row // 2, here_row % 2
    x = matrix.reshape(1536, 3, 2, 128)
    targets = row_order.reshape(6, 8, 256)
    local = jnp.arange(1536, dtype=jnp.int32)

    def keys(t):
        owner, row = t // 256 % 8, t // 2048 * 256 + t % 256
        return (owner * 2048 + local) * 2048 + row

    mine = lax.dynamic_slice(targets, (0, here_row, 0), (6, 1, 256)).reshape(1536)
    order = lax.sort(keys(mine)) // 2048 % 2048
    (s0,) = send_rows(order, x, (0,))
    s1, s2 = send_rows(order, x, (1, 2))
    a2a = lambda s: lax.all_to_all(s.reshape(8, 384, 128), "prow", 0, 0, tiled=True)
    g0, g1, g2 = [a2a(s).reshape(1536, 2, 128) for s in (s0, s1, s2)]
    all_keys = lax.sort(keys(targets.transpose(1, 0, 2).reshape(8, 1536)), dimension=1)
    places = lax.dynamic_slice(all_keys, (0, here_row * 192), (8, 192)).reshape(1536) % 2048
    backward = lax.sort(places * 2048 + local) % 2048
    p0, p1, p2 = [place_rows(backward, g).reshape(3072, 128) for g in (g0, g1, g2)]
    quarter = scatter_x(p0.reshape(4, 768, 128), here_x)
    panels = lax.all_gather(quarter, "pcol", axis=0, tiled=True).reshape(4, 4, 768, 128)
    r0, r1, r2 = [spread_z(p[:512], here_z, core) for p in (p0, p1, p2)]
    corner = lax.dynamic_slice(r0, (core * 2, 0, 0), (2, 512, 128)).reshape(4, 256, 128)
    corner = scatter_x(corner, here_x)
    along_y = lambda s: [(q, q // 4 * 4 + (q + s) % 4) for q in range(16)]
    along_x = lambda s: [(q, (q + 4 * s) % 16) for q in range(16)]
    corner = jnp.stack([corner] + [lax.ppermute(corner, "pcol", along_y(s)) for s in (1, 2, 3)])
    corner = jnp.stack([corner] + [lax.ppermute(corner, "pcol", along_x(s)) for s in (1, 2, 3)])
    other = lax.ppermute(corner, "prow", [(p, p ^ 1) for p in range(8)])
    place = jnp.stack([here_x, here_y, core, here_col, here_row]).astype(jnp.int32)
    parts = pl.pallas_call(
        upper_kernel,
        out_shape=[b16(1024, 768)] * 2 + [b16(6, 256, 256)] * 2 + [b16(4, 256, 256)] * 2,
        in_specs=[SMEM] * 3 + [VMEM] * 6,
        out_specs=[VMEM] * 6,
        scratch_shapes=[pltpu.VMEM((4, 4, 256, 256), jnp.float32)],
        compiler_params=PARAMS,
        name="upper",
    )(place, lower_fill, upper_fill, corner, other, r0, r1, r2, inverses)
    rows = pl.BlockSpec((768, 128), lambda i: (i, 0))
    out = pl.pallas_call(
        update_kernel,
        out_shape=f32(9216, 128),
        grid=(4,),
        in_specs=[SMEM, SMEM, pl.BlockSpec((1, 4, 768, 128), lambda i: (i, 0, 0, 0))]
        + [rows] * 3
        + [whole(1024, 768)] * 2
        + [whole(6, 256, 256)] * 2
        + [whole(4, 256, 256)] * 2,
        out_specs=pl.BlockSpec((2304, 128), lambda i: (i, 0)),
        scratch_shapes=[
            pltpu.VMEM((384, 1024), BF),
            pltpu.VMEM((384, 1024), BF),
            pltpu.VMEM((384, 256), jnp.float32),
        ],
        compiler_params=PARAMS,
        name="update",
    )(place, lower_fill, panels, p0, p1, p2, *parts)
    return out.reshape(6, 1, 256, 3, 1, 256)


def solution(mesh):
    in_specs = (P(None, "prow", None, None, "pcol", None), P(), P(), P(), P())
    out_specs = P(None, "prow", None, None, "pcol", None)
    return jax.shard_map(body, mesh=mesh, in_specs=in_specs, out_specs=out_specs, check_vma=False)
```

time: 360 us -> 244 us (0.68)
  local copies, waits for them, and re-layouts: 68.5 us -> 12.4 us
  matrix products: 51.6 us -> 0 us
  starting transfers between devices: 22.1 us -> 69.9 us
  Pallas kernels: 12.8 us -> 58.7 us
  blocking collectives: 41.4 us -> 0 us
  waiting for transfers between devices: 105 us -> 65.8 us
  other arithmetic: 43.5 us -> 22 us
    all_gather x3 -> x1, waiting for transfers between devices: 60 us -> 0.01 us  [body(): lax.all_gather(quarter, 'pcol', axis=0, tiled=True).reshape(4, 4, 768, 128)]
    dot_general x31 -> x0, matrix products: 51.6 us -> none  [dot(): return jnp.dot(a, b, precision=HIGH, preferred_element_type=jnp.float32)]
    pallas_call x3 -> x7, Pallas kernels: 12.8 us -> 58.7 us  [the longest x1 27.2 us: body(): pl.pallas_call(update_kernel, out_shape=f32(9216, 128), grid=(4,), in_spe...]
    all_to_all x2 -> x0, blocking collectives: 41.4 us -> none  [the longest x1 27.5 us: body(): lax.all_to_all(first.reshape(8, 384, 128), 'prow', 0, 0, tiled=True)]
    ppermute x1 -> x18, starting transfers between devices: 2.95 us -> 29.9 us  [the longest x9 18 us: go(): lax.ppermute(value, 'prow', [(2 * a + c, 2 * b + c) for a, b in pairs for...]
    select_n x12 -> x0, other arithmetic: 24.8 us -> none  [the longest x3 14.9 us: body(): keep = jnp.where(places // 256 == r, keep6[r], keep)]
    ppermute x1 -> x18, waiting for transfers between devices: 6.3 us -> 25.3 us  [the longest x9 10.6 us: go(): lax.ppermute(value, 'prow', [(2 * a + c, 2 * b + c) for a, b in pairs for...]
    all_to_all x1 -> x3, starting transfers between devices: 4.59 us -> 22.2 us  [body(): lax.all_to_all(s.reshape(8, 384, 128), 'prow', 0, 0, tiled=True)]
  transfers between devices with their start and end apart: 12 -> 29, of which waited for: 8 -> 14; matrix products, arithmetic and copies ran while one was open for 16% -> 7% of each run, Pallas kernels for 0% -> 10%
where the time goes in v2:
time: 244 us; the launch traced here: 243 us
  starting transfers between devices  69.9 us (29%)
  waiting for transfers between devices  65.8 us (27%)
  Pallas kernels  58.7 us (24%)
  other arithmetic  22 us (9%)
  between operations  13.8 us (6%)
  local copies, waits for them, and re-layouts  12.4 us (5%)
    pallas_call x1, Pallas kernels, body(): pl.pallas_call(update_kernel, out_shape=f32(9216, 128), grid=(4,), in_spe...  27.2 us
    all_to_all x3, waiting for transfers between devices, body(): lax.all_to_all(s.reshape(8, 384, 128), 'prow', 0, 0, tiled=True)  24.3 us
    all_to_all x3, starting transfers between devices, body(): lax.all_to_all(s.reshape(8, 384, 128), 'prow', 0, 0, tiled=True)  22.2 us
    ppermute x9, starting transfers between devices, go(): lax.ppermute(value, 'prow', [(2 * a + c, 2 * b + c) for a, b in pairs for...  18 us
    ppermute x6, waiting for transfers between devices, scatter_x(): lax.ppermute(blocks[s], 'pcol', [(k, k + 4 * s) for k in range(4)])  16.1 us
    ppermute x6, starting transfers between devices, scatter_x(): lax.ppermute(blocks[s], 'pcol', [(k, k + 4 * s) for k in range(4)])  15.8 us
    pallas_call x2, Pallas kernels, send_rows(): pl.pallas_call(permute_kernel, out_shape=[f32(1536, 2, 128)] * len(column...  11.4 us
    ppermute x9, waiting for transfers between devices, go(): lax.ppermute(value, 'prow', [(2 * a + c, 2 * b + c) for a, b in pairs for...  10.6 us
  transfers between devices with their start and end apart: 29, of which 14 were waited for; matrix products, arithmetic and copies ran while one was open for 7% of the time, Pallas kernels for 10%

profile of v2, /device:TPU:1, one launch (start us, length us, event | category | flops | bytes accessed | tf_op | source)
XLA Modules:
  0.0 242.7 jit_solution(8063984187862897973)
XLA Ops:
  7.4 5.0 %sort.37 = (s32[1536]{0:T(1024)S(1)}, s32[1536]{0:T(1024)}) sort(s32[1536]{0:T(1024)S(1)} %fusion.21, s32[1536]{0:T(1024)S(1)} %iota.17), dimensions={0}, to_apply=%region_2.3 | sort | flops 16896 | bytes 24576 | tf_op jit(solution)/shard_map/sort | solution.py:201
  12.5 5.2 %send_rows.2 = f32[1536,2,128]{2,1,0:T(2,128)} custom-call(s32[1536]{0:T(1024)S(1)} %add_select_fusion.5.order, f32[1536,3,2,128]{3,2,1,0:T(2,128)} %bitcast.84), custom_call_target="tpu_custom_call" | custom-call | tf_op jit(solution)/shard_map/send_rows/pallas_call | solution.py:46
  17.7 6.8 %all-to-all-start = ((f32[8,384,128]{2,1,0:T(8,128)}), f32[8,384,128]{2,1,0:T(8,128)S(1)}, u32[]{:S(2)}, u32[]{:S(2)}) async-start(f32[8,384,128]{2,1,0:T(8,128)} %bitcast.9), calls=%async_computation | async-start | bytes 3145728 | tf_op jit(solution)/shard_map/all_to_all | solution.py:204
  25.3 8.0 %sort.39.cloned.1.call-done = s32[8,1536]{1,0:T(8,128)} async-done(((s32[8,1536]{1,0:T(8,128)}), s32[8,1536]{1,0:T(8,128)}) %sort.39.cloned.1.call-update) | async-done | bytes 49168 | tf_op jit(solution)/shard_map/sort | solution.py:206
  34.2 5.0 %sort.36 = (s32[1536]{0:T(1024)S(1)}, s32[1536]{0:T(1024)}) sort(s32[1536]{0:T(1024)S(1)} %fusion.15, s32[1536]{0:T(1024)S(1)} %iota.15), dimensions={0}, to_apply=%region_1.2 | sort | flops 16896 | bytes 24576 | tf_op jit(solution)/shard_map/sort | solution.py:208
  39.2 6.0 %all-to-all-done = f32[8,384,128]{2,1,0:T(8,128)S(1)} async-done(((f32[8,384,128]{2,1,0:T(8,128)}), f32[8,384,128]{2,1,0:T(8,128)S(1)}, u32[]{:S(2)}, u32[]{:S(2)}) %all-to-all-start) | async-done | bytes 1572896 | tf_op jit(solution)/shard_map/all_to_all | solution.py:204
  45.2 3.2 %place_rows.3 = f32[1536,2,128]{2,1,0:T(2,128)S(1)} custom-call(s32[1536]{0:T(1024)S(1)} %add_select_fusion.11.order, f32[1536,2,128]{2,1,0:T(2,128)S(1)} %bitcast.82), custom_call_target="tpu_custom_call" | custom-call | tf_op jit(solution)/shard_map/place_rows/pallas_call | solution.py:58
  48.5 3.1 %collective-permute-start = (f32[768,128]{1,0:T(8,128)S(1)}, f32[768,128]{1,0:T(8,128)S(1)}, u32[]{:S(2)}, u32[]{:S(2)}) collective-permute-start(f32[768,128]{1,0:T(8,128)S(1)} %bitcast.105), channel_id=1, source_target_pairs={{0,4},{1,5},{2,6},{3,7},{16,20},{17,21},{18,22},{19,23},{32,36},{3... | collective-permute-start | bytes 1179656 | tf_op jit(solution)/shard_map/ppermute | solution.py:167
  51.6 3.0 %collective-permute-start.1 = (f32[768,128]{1,0:T(8,128)S(1)}, f32[768,128]{1,0:T(8,128)}, u32[]{:S(2)}, u32[]{:S(2)}) collective-permute-start(f32[768,128]{1,0:T(8,128)S(1)} %bitcast.104), channel_id=1, source_target_pairs={{0,8},{1,9},{2,10},{3,11},{16,24},{17,25},{18,26},{19,27},{32,40},... | collective-permute-start | bytes 1179656 | tf_op jit(solution)/shard_map/ppermute | solution.py:167
  54.6 2.0 collective-permute-start.2
  56.6 2.5 %collective-permute-done = f32[768,128]{1,0:T(8,128)S(1)} collective-permute-done((f32[768,128]{1,0:T(8,128)S(1)}, f32[768,128]{1,0:T(8,128)S(1)}, u32[]{:S(2)}, u32[]{:S(2)}) %collective-permute-start) | collective-permute-done | bytes 393248 | tf_op jit(solution)/shard_map/ppermute | solution.py:167
  59.2 8.4 %collective-permute-done.1 = f32[768,128]{1,0:T(8,128)} collective-permute-done((f32[768,128]{1,0:T(8,128)S(1)}, f32[768,128]{1,0:T(8,128)}, u32[]{:S(2)}, u32[]{:S(2)}) %collective-permute-start.1) | collective-permute-done | bytes 393248 | tf_op jit(solution)/shard_map/ppermute | solution.py:167
  67.6 1.9 add_select_fusion
  69.6 2.8 %collective-permute-start.4 = (f32[512,128]{1,0:T(8,128)S(1)}, f32[512,128]{1,0:T(8,128)S(1)}, u32[]{:S(2)}, u32[]{:S(2)}) collective-permute-start(f32[512,128]{1,0:T(8,128)S(1)} %bitcast.93), channel_id=1, source_target_pairs={{0,96},{16,112},{32,64},{48,80},{1,97},{17,113},{33,65},{49,81},{2... | collective-permute-start | bytes 786440 | tf_op jit(solution)/shard_map/ppermute | solution.py:174
  72.4 1.9 collective-permute-start.3
  74.3 1.8 collective-permute-done.4
  76.9 6.2 %send_rows.3 = (f32[1536,2,128]{2,1,0:T(2,128)}, f32[1536,2,128]{2,1,0:T(2,128)S(1)}) custom-call(s32[1536]{0:T(1024)S(1)} %add_select_fusion.5.order, f32[1536,3,2,128]{3,2,1,0:T(2,128)} %bitcast.85, f32[1536,3,2,128]{3,2,1,0:T(2,128)} %bitcast.86), custom_call_target="tpu_custom_call" | custom-call | tf_op jit(solution)/shard_map/send_rows/pallas_call | solution.py:46
  83.0 1.1 copy-done.5
  84.2 10.4 %all-to-all-start.1 = ((f32[8,384,128]{2,1,0:T(8,128)}), f32[8,384,128]{2,1,0:T(8,128)S(1)}, u32[]{:S(2)}, u32[]{:S(2)}) async-start(f32[8,384,128]{2,1,0:T(8,128)} %bitcast.17), calls=%async_computation.1 | async-start | bytes 3145728 | tf_op jit(solution)/shard_map/all_to_all | solution.py:204
  94.8 1.9 collective-permute-done.6
  96.9 18.4 %all-to-all-done.1 = f32[8,384,128]{2,1,0:T(8,128)S(1)} async-done(((f32[8,384,128]{2,1,0:T(8,128)}), f32[8,384,128]{2,1,0:T(8,128)S(1)}, u32[]{:S(2)}, u32[]{:S(2)}) %all-to-all-start.1) | async-done | bytes 1572896 | tf_op jit(solution)/shard_map/all_to_all | solution.py:204
  115.3 5.0 %all-to-all-start.2 = ((f32[8,384,128]{2,1,0:T(8,128)}), f32[8,384,128]{2,1,0:T(8,128)}, u32[]{:S(2)}, u32[]{:S(2)}) async-start(f32[8,384,128]{2,1,0:T(8,128)} %bitcast.83), calls=%async_computation.2 | async-start | bytes 3145728 | tf_op jit(solution)/shard_map/all_to_all | solution.py:204
  120.4 1.3 collective-permute-start.7
  121.7 5.1 %collective-permute-start.8 = (f32[256,128]{1,0:T(8,128)S(1)}, f32[256,128]{1,0:T(8,128)S(1)}, u32[]{:S(2)}, u32[]{:S(2)}) collective-permute-start(f32[256,128]{1,0:T(8,128)S(1)} %get-tuple-element.45), channel_id=1, source_target_pairs={{0,8},{1,9},{2,10},{3,11},{16,24},{17,25},{18,26},{19,27},{32,40},... | collective-permute-start | bytes 393224 | tf_op jit(solution)/shard_map/ppermute | solution.py:167
  126.8 1.3 collective-permute-start.9
  128.1 5.2 %collective-permute-done.8 = f32[256,128]{1,0:T(8,128)S(1)} collective-permute-done((f32[256,128]{1,0:T(8,128)S(1)}, f32[256,128]{1,0:T(8,128)S(1)}, u32[]{:S(2)}, u32[]{:S(2)}) %collective-permute-start.8) | collective-permute-done | bytes 131104 | tf_op jit(solution)/shard_map/ppermute | solution.py:167
  133.3 1.3 collective-permute-start.10
  134.7 2.6 %collective-permute-start.11 = (f32[256,128]{1,0:T(8,128)S(1)}, f32[256,128]{1,0:T(8,128)S(1)}, u32[]{:S(2)}, u32[]{:S(2)}) collective-permute-start(f32[256,128]{1,0:T(8,128)S(1)} %fusion), channel_id=1, source_target_pairs={{0,2},{1,3},{2,0},{3,1},{4,6},{5,7},{6,4},{7,5},{8,10},{9,11},{10,... | collective-permute-start | bytes 393224 | tf_op jit(solution)/shard_map/ppermute | solution.py:217
  139.1 3.8 %collective-permute-done.11 = f32[256,128]{1,0:T(8,128)S(1)} collective-permute-done((f32[256,128]{1,0:T(8,128)S(1)}, f32[256,128]{1,0:T(8,128)S(1)}, u32[]{:S(2)}, u32[]{:S(2)}) %collective-permute-start.11) | collective-permute-done | bytes 131104 | tf_op jit(solution)/shard_map/ppermute | solution.py:217
  144.0 3.9 %collective-permute-start.14 = (f32[4,256,128]{2,1,0:T(8,128)}, f32[4,256,128]{2,1,0:T(8,128)}, u32[]{:S(2)}, u32[]{:S(2)}) collective-permute-start(f32[4,256,128]{2,1,0:T(8,128)} %get-tuple-element.44), channel_id=1, source_target_pairs={{0,8},{1,9},{2,10},{3,11},{4,12},{5,13},{6,14},{7,15},{8,0},{9,1},... | collective-permute-start | bytes 1572872 | tf_op jit(solution)/shard_map/ppermute | solution.py:218
  147.9 2.1 collective-permute-start.15
  150.0 3.2 %place_rows.4 = f32[1536,2,128]{2,1,0:T(2,128)S(1)} custom-call(s32[1536]{0:T(1024)S(1)} %add_select_fusion.11.order, f32[1536,2,128]{2,1,0:T(2,128)S(1)} %bitcast.81), custom_call_target="tpu_custom_call" | custom-call | tf_op jit(solution)/shard_map/place_rows/pallas_call | solution.py:58
  153.2 4.7 %collective-permute-start.18 = (f32[512,128]{1,0:T(8,128)S(1)}, f32[512,128]{1,0:T(8,128)}, u32[]{:S(2)}, u32[]{:S(2)}) collective-permute-start(f32[512,128]{1,0:T(8,128)S(1)} %bitcast.96), channel_id=1, source_target_pairs={{0,96},{16,112},{32,64},{48,80},{1,97},{17,113},{33,65},{49,81},{2... | collective-permute-start | bytes 786440 | tf_op jit(solution)/shard_map/ppermute | solution.py:174
  157.9 3.9 %place_rows.5 = f32[1536,2,128]{2,1,0:T(2,128)S(1)} custom-call(s32[1536]{0:T(1024)S(1)} %add_select_fusion.11.order, f32[1536,2,128]{2,1,0:T(2,128)} %bitcast.21.refs_0_), custom_call_target="tpu_custom_call" | custom-call | tf_op jit(solution)/shard_map/place_rows/pallas_call | solution.py:58
  161.9 1.3 collective-permute-start.22
  163.2 7.0 %collective-permute-done.14 = f32[4,256,128]{2,1,0:T(8,128)} collective-permute-done((f32[4,256,128]{2,1,0:T(8,128)}, f32[4,256,128]{2,1,0:T(8,128)}, u32[]{:S(2)}, u32[]{:S(2)}) %collective-permute-start.14) | collective-permute-done | bytes 524320 | tf_op jit(solution)/shard_map/ppermute | solution.py:218
  170.5 1.7 pad_maximum_fusion.own
  172.2 1.9 collective-permute-start.16
  174.1 2.8 %collective-permute-start.17 = (f32[512,128]{1,0:T(8,128)S(1)}, f32[512,128]{1,0:T(8,128)S(1)}, u32[]{:S(2)}, u32[]{:S(2)}) collective-permute-start(f32[512,128]{1,0:T(8,128)S(1)} %bitcast.97), channel_id=1, source_target_pairs={{0,32},{16,48},{32,0},{48,16},{1,33},{17,49},{33,1},{49,17},{2,34}... | collective-permute-start | bytes 786440 | tf_op jit(solution)/shard_map/ppermute | solution.py:174
  176.9 2.5 %collective-permute-start.21 = (f32[512,128]{1,0:T(8,128)S(1)}, f32[512,128]{1,0:T(8,128)S(1)}, u32[]{:S(2)}, u32[]{:S(2)}) collective-permute-start(f32[512,128]{1,0:T(8,128)S(1)} %bitcast.100), channel_id=1, source_target_pairs={{0,32},{16,48},{32,0},{48,16},{1,33},{17,49},{33,1},{49,17},{2,34}... | collective-permute-start | bytes 786440 | tf_op jit(solution)/shard_map/ppermute | solution.py:174
  180.8 3.1 %collective-permute-done.17 = f32[512,128]{1,0:T(8,128)S(1)} collective-permute-done((f32[512,128]{1,0:T(8,128)S(1)}, f32[512,128]{1,0:T(8,128)S(1)}, u32[]{:S(2)}, u32[]{:S(2)}) %collective-permute-start.17) | collective-permute-done | bytes 262176 | tf_op jit(solution)/shard_map/ppermute | solution.py:174
  183.9 5.6 %collective-permute-done.21 = f32[512,128]{1,0:T(8,128)S(1)} collective-permute-done((f32[512,128]{1,0:T(8,128)S(1)}, f32[512,128]{1,0:T(8,128)S(1)}, u32[]{:S(2)}, u32[]{:S(2)}) %collective-permute-start.21) | collective-permute-done | bytes 262176 | tf_op jit(solution)/shard_map/ppermute | solution.py:174
  189.5 1.1 select_bitcast_fusion.7
  194.1 1.1 select_bitcast_fusion.3
  196.4 1.2 select_bitcast_fusion.1
  197.7 1.1 pad_maximum_fusion.3
  198.8 9.8 %upper.1 = (bf16[1024,768]{1,0:T(8,128)(2,1)}, bf16[1024,768]{1,0:T(8,128)(2,1)}, bf16[6,256,256]{2,1,0:T(8,128)(2,1)S(1)}, bf16[6,256,256]{2,1,0:T(8,128)(2,1)S...) custom-call(s32[5]{0:T(128)S(1)} %stack.107.place, s32[4,48]{1,0:T(4,128)S(1)} %copy-done.6, ...), custom_call_target="tpu_custom_call" | custom-call | tf_op jit(solution)/shard_map/upper/pallas_call | solution.py:221
  208.6 27.2 %update.1 = f32[9216,128]{1,0:T(8,128)} custom-call(s32[5]{0:T(128)S(1)} %stack.107.place, s32[4,48]{1,0:T(4,128)S(1)} %copy-done.6, f32[4,4,768,128]{3,2,1,0:T(8,128)} %bitcast.87, f32[3072,128]{1,0:T(8,128)} %bitcast.76, f32[3072,128]{1,0:T(8,128)} %bitcast.77, f32[3072,128]{1,0:T(8,128)} %bitcast.78, bf16[1024,768]{1,0:T(8,128)(2,1)} %get-tuple-element.21.uh, ...), custom_call_target="tpu_custom_call" | custom-call | tf_op jit(solution)/shard_map/update/pallas_call | solution.py:231
  (77 shorter events, 13.1 us)
Async XLA Ops:
  17.7 27.5 %all-to-all-start = ((f32[8,384,128]{2,1,0:T(8,128)}), f32[8,384,128]{2,1,0:T(8,128)S(1)}, u32[]{:S(2)}, u32[]{:S(2)}) async-start(f32[8,384,128]{2,1,0:T(8,128)} %bitcast.9), calls=%async_computation | async-start | bytes 3145728 | tf_op jit(solution)/shard_map/all_to_all | solution.py:204
  24.5 8.8 %sort.39.cloned.1.call-start = ((), (), s32[]{:S(2)}) async-start(), calls=%async_computation.4 | async-start | bytes 147488 | tf_op jit(solution)/shard_map/sort | solution.py:206
  25.2 183.4 %all-gather.2.cloned.1.call-start = ((), (), s32[]{:S(2)}) async-start(), calls=%async_computation.3 | async-start | bytes 6684672 | tf_op jit(solution)/shard_map/all_gather | solution.py:211
  48.4 21.2 %copy-start = (f32[1536,2,128]{2,1,0:T(2,128)}, f32[1536,2,128]{2,1,0:T(2,128)S(1)}, u32[]{:S(2)}) copy-start(f32[1536,2,128]{2,1,0:T(2,128)S(1)} %place_rows.3) | copy-start | bytes 4718596
  48.5 10.7 %collective-permute-start = (f32[768,128]{1,0:T(8,128)S(1)}, f32[768,128]{1,0:T(8,128)S(1)}, u32[]{:S(2)}, u32[]{:S(2)}) collective-permute-start(f32[768,128]{1,0:T(8,128)S(1)} %bitcast.105), channel_id=1, source_target_pairs={{0,4},{1,5},{2,6},{3,7},{16,20},{17,21},{18,22},{19,23},{32,36},{3... | collective-permute-start | bytes 1179656 | tf_op jit(solution)/shard_map/ppermute | solution.py:167
  51.6 15.9 %collective-permute-start.1 = (f32[768,128]{1,0:T(8,128)S(1)}, f32[768,128]{1,0:T(8,128)}, u32[]{:S(2)}, u32[]{:S(2)}) collective-permute-start(f32[768,128]{1,0:T(8,128)S(1)} %bitcast.104), channel_id=1, source_target_pairs={{0,8},{1,9},{2,10},{3,11},{16,24},{17,25},{18,26},{19,27},{32,40},... | collective-permute-start | bytes 1179656 | tf_op jit(solution)/shard_map/ppermute | solution.py:167
  54.6 13.0 %collective-permute-start.2 = (f32[768,128]{1,0:T(8,128)S(1)}, f32[768,128]{1,0:T(8,128)}, u32[]{:S(2)}, u32[]{:S(2)}) collective-permute-start(f32[768,128]{1,0:T(8,128)S(1)} %bitcast.103), channel_id=1, source_target_pairs={{0,12},{1,13},{2,14},{3,15},{16,28},{17,29},{18,30},{19,31},{32,44... | collective-permute-start | bytes 1179656 | tf_op jit(solution)/shard_map/ppermute | solution.py:167
  69.6 6.6 %collective-permute-start.4 = (f32[512,128]{1,0:T(8,128)S(1)}, f32[512,128]{1,0:T(8,128)S(1)}, u32[]{:S(2)}, u32[]{:S(2)}) collective-permute-start(f32[512,128]{1,0:T(8,128)S(1)} %bitcast.93), channel_id=1, source_target_pairs={{0,96},{16,112},{32,64},{48,80},{1,97},{17,113},{33,65},{49,81},{2... | collective-permute-start | bytes 786440 | tf_op jit(solution)/shard_map/ppermute | solution.py:174
  72.4 22.2 %collective-permute-start.3 = (f32[512,128]{1,0:T(8,128)S(1)}, f32[512,128]{1,0:T(8,128)S(1)}, u32[]{:S(2)}, u32[]{:S(2)}) collective-permute-start(f32[512,128]{1,0:T(8,128)S(1)} %bitcast.94), channel_id=1, source_target_pairs={{0,32},{16,48},{32,0},{48,16},{1,33},{17,49},{33,1},{49,17},{2,34}... | collective-permute-start | bytes 786440 | tf_op jit(solution)/shard_map/ppermute | solution.py:174
  76.2 18.4 %collective-permute-start.5 = (f32[512,128]{1,0:T(8,128)S(1)}, f32[512,128]{1,0:T(8,128)S(1)}, u32[]{:S(2)}, u32[]{:S(2)}) collective-permute-start(f32[512,128]{1,0:T(8,128)S(1)} %collective-permute-done.4), channel_id=1, source_target_pairs={{96,64},{112,80},{64,96},{80,112},{97,65},{113,81},{65,97},{81,113... | collective-permute-start | bytes 786440 | tf_op jit(solution)/shard_map/ppermute | solution.py:174
  83.0 1.1 copy-start.5
  84.2 31.1 %all-to-all-start.1 = ((f32[8,384,128]{2,1,0:T(8,128)}), f32[8,384,128]{2,1,0:T(8,128)S(1)}, u32[]{:S(2)}, u32[]{:S(2)}) async-start(f32[8,384,128]{2,1,0:T(8,128)} %bitcast.17), calls=%async_computation.1 | async-start | bytes 3145728 | tf_op jit(solution)/shard_map/all_to_all | solution.py:204
  94.7 2.0 collective-permute-start.6
  96.9 23.4 %copy-start.3 = (f32[2,2,512,128]{3,2,1,0:T(8,128)}, f32[2,2,512,128]{3,2,1,0:T(8,128)S(1)}, u32[]{:S(2)}) copy-start(f32[2,2,512,128]{3,2,1,0:T(8,128)S(1)} %copy.10) | copy-start | bytes 3145732
  115.3 42.6 %all-to-all-start.2 = ((f32[8,384,128]{2,1,0:T(8,128)}), f32[8,384,128]{2,1,0:T(8,128)}, u32[]{:S(2)}, u32[]{:S(2)}) async-start(f32[8,384,128]{2,1,0:T(8,128)} %bitcast.83), calls=%async_computation.2 | async-start | bytes 3145728 | tf_op jit(solution)/shard_map/all_to_all | solution.py:204
  120.4 7.7 %collective-permute-start.7 = (f32[256,128]{1,0:T(8,128)S(1)}, f32[256,128]{1,0:T(8,128)S(1)}, u32[]{:S(2)}, u32[]{:S(2)}) collective-permute-start(f32[256,128]{1,0:T(8,128)S(1)} %get-tuple-element.47), channel_id=1, source_target_pairs={{0,4},{1,5},{2,6},{3,7},{16,20},{17,21},{18,22},{19,23},{32,36},{3... | collective-permute-start | bytes 393224 | tf_op jit(solution)/shard_map/ppermute | solution.py:167
  121.7 11.6 %collective-permute-start.8 = (f32[256,128]{1,0:T(8,128)S(1)}, f32[256,128]{1,0:T(8,128)S(1)}, u32[]{:S(2)}, u32[]{:S(2)}) collective-permute-start(f32[256,128]{1,0:T(8,128)S(1)} %get-tuple-element.45), channel_id=1, source_target_pairs={{0,8},{1,9},{2,10},{3,11},{16,24},{17,25},{18,26},{19,27},{32,40},... | collective-permute-start | bytes 393224 | tf_op jit(solution)/shard_map/ppermute | solution.py:167
  126.8 6.5 %collective-permute-start.9 = (f32[256,128]{1,0:T(8,128)S(1)}, f32[256,128]{1,0:T(8,128)S(1)}, u32[]{:S(2)}, u32[]{:S(2)}) collective-permute-start(f32[256,128]{1,0:T(8,128)S(1)} %get-tuple-element.46), channel_id=1, source_target_pairs={{0,12},{1,13},{2,14},{3,15},{16,28},{17,29},{18,30},{19,31},{32,44... | collective-permute-start | bytes 393224 | tf_op jit(solution)/shard_map/ppermute | solution.py:167
  133.3 5.8 %collective-permute-start.10 = (f32[256,128]{1,0:T(8,128)S(1)}, f32[256,128]{1,0:T(8,128)S(1)}, u32[]{:S(2)}, u32[]{:S(2)}) collective-permute-start(f32[256,128]{1,0:T(8,128)S(1)} %fusion), channel_id=1, source_target_pairs={{0,1},{1,2},{2,3},{3,0},{4,5},{5,6},{6,7},{7,4},{8,9},{9,10},{10,1... | collective-permute-start | bytes 393224 | tf_op jit(solution)/shard_map/ppermute | solution.py:217
  134.7 8.3 %collective-permute-start.11 = (f32[256,128]{1,0:T(8,128)S(1)}, f32[256,128]{1,0:T(8,128)S(1)}, u32[]{:S(2)}, u32[]{:S(2)}) collective-permute-start(f32[256,128]{1,0:T(8,128)S(1)} %fusion), channel_id=1, source_target_pairs={{0,2},{1,3},{2,0},{3,1},{4,6},{5,7},{6,4},{7,5},{8,10},{9,11},{10,... | collective-permute-start | bytes 393224 | tf_op jit(solution)/shard_map/ppermute | solution.py:217
  137.3 5.7 %collective-permute-start.12 = (f32[256,128]{1,0:T(8,128)S(1)}, f32[256,128]{1,0:T(8,128)S(1)}, u32[]{:S(2)}, u32[]{:S(2)}) collective-permute-start(f32[256,128]{1,0:T(8,128)S(1)} %fusion), channel_id=1, source_target_pairs={{0,3},{1,0},{2,1},{3,2},{4,7},{5,4},{6,5},{7,6},{8,11},{9,8},{10,9... | collective-permute-start | bytes 393224 | tf_op jit(solution)/shard_map/ppermute | solution.py:217
  144.0 19.2 %collective-permute-start.13 = (f32[4,256,128]{2,1,0:T(8,128)}, f32[4,256,128]{2,1,0:T(8,128)}, u32[]{:S(2)}, u32[]{:S(2)}) collective-permute-start(f32[4,256,128]{2,1,0:T(8,128)} %get-tuple-element.44), channel_id=1, source_target_pairs={{0,4},{1,5},{2,6},{3,7},{4,8},{5,9},{6,10},{7,11},{8,12},{9,13},{1... | collective-permute-start | bytes 1572872 | tf_op jit(solution)/shard_map/ppermute | solution.py:218
  144.0 26.2 %collective-permute-start.14 = (f32[4,256,128]{2,1,0:T(8,128)}, f32[4,256,128]{2,1,0:T(8,128)}, u32[]{:S(2)}, u32[]{:S(2)}) collective-permute-start(f32[4,256,128]{2,1,0:T(8,128)} %get-tuple-element.44), channel_id=1, source_target_pairs={{0,8},{1,9},{2,10},{3,11},{4,12},{5,13},{6,14},{7,15},{8,0},{9,1},... | collective-permute-start | bytes 1572872 | tf_op jit(solution)/shard_map/ppermute | solution.py:218
  147.9 22.6 %collective-permute-start.15 = (f32[4,256,128]{2,1,0:T(8,128)}, f32[4,256,128]{2,1,0:T(8,128)}, u32[]{:S(2)}, u32[]{:S(2)}) collective-permute-start(f32[4,256,128]{2,1,0:T(8,128)} %get-tuple-element.44), channel_id=1, source_target_pairs={{0,12},{1,13},{2,14},{3,15},{4,0},{5,1},{6,2},{7,3},{8,4},{9,5},{1... | collective-permute-start | bytes 1572872 | tf_op jit(solution)/shard_map/ppermute | solution.py:218
  153.1 8.7 %copy-start.1 = (f32[1536,2,128]{2,1,0:T(2,128)}, f32[1536,2,128]{2,1,0:T(2,128)S(1)}, u32[]{:S(2)}) copy-start(f32[1536,2,128]{2,1,0:T(2,128)S(1)} %place_rows.4) | copy-start | bytes 4718596
  153.2 26.2 %collective-permute-start.18 = (f32[512,128]{1,0:T(8,128)S(1)}, f32[512,128]{1,0:T(8,128)}, u32[]{:S(2)}, u32[]{:S(2)}) collective-permute-start(f32[512,128]{1,0:T(8,128)S(1)} %bitcast.96), channel_id=1, source_target_pairs={{0,96},{16,112},{32,64},{48,80},{1,97},{17,113},{33,65},{49,81},{2... | collective-permute-start | bytes 786440 | tf_op jit(solution)/shard_map/ppermute | solution.py:174
  161.9 10.4 %copy-start.2 = (f32[1536,2,128]{2,1,0:T(2,128)}, f32[1536,2,128]{2,1,0:T(2,128)S(1)}, u32[]{:S(2)}) copy-start(f32[1536,2,128]{2,1,0:T(2,128)S(1)} %place_rows.5) | copy-start | bytes 4718596
  161.9 18.2 %collective-permute-start.22 = (f32[512,128]{1,0:T(8,128)S(1)}, f32[512,128]{1,0:T(8,128)S(1)}, u32[]{:S(2)}, u32[]{:S(2)}) collective-permute-start(f32[512,128]{1,0:T(8,128)S(1)} %bitcast.99), channel_id=1, source_target_pairs={{0,96},{16,112},{32,64},{48,80},{1,97},{17,113},{33,65},{49,81},{2... | collective-permute-start | bytes 786440 | tf_op jit(solution)/shard_map/ppermute | solution.py:174
  172.2 19.2 %copy-start.8 = (f32[4,4,256,128]{3,2,1,0:T(8,128)}, f32[4,4,256,128]{3,2,1,0:T(8,128)S(1)}, u32[]{:S(2)}) copy-start(f32[4,4,256,128]{3,2,1,0:T(8,128)S(1)} %pad_maximum_fusion.own) | copy-start | bytes 6291460
  172.2 26.5 %collective-permute-start.16 = (f32[4,4,256,128]{3,2,1,0:T(8,128)S(1)}, f32[4,4,256,128]{3,2,1,0:T(8,128)}, u32[]{:S(2)}, u32[]{:S(2)}) collective-permute-start(f32[4,4,256,128]{3,2,1,0:T(8,128)S(1)} %pad_maximum_fusion.own), channel_id=1, source_target_pairs={{0,16},{16,0},{32,48},{48,32},{64,80},{80,64},{96,112},{112,96},{1... | collective-permute-start | bytes 6291464 | tf_op jit(solution)/shard_map/ppermute | solution.py:219
  174.1 9.8 %collective-permute-start.17 = (f32[512,128]{1,0:T(8,128)S(1)}, f32[512,128]{1,0:T(8,128)S(1)}, u32[]{:S(2)}, u32[]{:S(2)}) collective-permute-start(f32[512,128]{1,0:T(8,128)S(1)} %bitcast.97), channel_id=1, source_target_pairs={{0,32},{16,48},{32,0},{48,16},{1,33},{17,49},{33,1},{49,17},{2,34}... | collective-permute-start | bytes 786440 | tf_op jit(solution)/shard_map/ppermute | solution.py:174
  176.9 12.7 %collective-permute-start.21 = (f32[512,128]{1,0:T(8,128)S(1)}, f32[512,128]{1,0:T(8,128)S(1)}, u32[]{:S(2)}, u32[]{:S(2)}) collective-permute-start(f32[512,128]{1,0:T(8,128)S(1)} %bitcast.100), channel_id=1, source_target_pairs={{0,32},{16,48},{32,0},{48,16},{1,33},{17,49},{33,1},{49,17},{2,34}... | collective-permute-start | bytes 786440 | tf_op jit(solution)/shard_map/ppermute | solution.py:174
  179.4 10.1 %collective-permute-start.19 = (f32[512,128]{1,0:T(8,128)}, f32[512,128]{1,0:T(8,128)S(1)}, u32[]{:S(2)}, u32[]{:S(2)}) collective-permute-start(f32[512,128]{1,0:T(8,128)} %collective-permute-done.18), channel_id=1, source_target_pairs={{96,64},{112,80},{64,96},{80,112},{97,65},{113,81},{65,97},{81,113... | collective-permute-start | bytes 786440 | tf_op jit(solution)/shard_map/ppermute | solution.py:174
  180.1 9.4 %collective-permute-start.23 = (f32[512,128]{1,0:T(8,128)S(1)}, f32[512,128]{1,0:T(8,128)S(1)}, u32[]{:S(2)}, u32[]{:S(2)}) collective-permute-start(f32[512,128]{1,0:T(8,128)S(1)} %collective-permute-done.22), channel_id=1, source_target_pairs={{96,64},{112,80},{64,96},{80,112},{97,65},{113,81},{65,97},{81,113... | collective-permute-start | bytes 786440 | tf_op jit(solution)/shard_map/ppermute | solution.py:174
  191.5 2.7 %collective-permute-start.20 = (f32[2,512,128]{2,1,0:T(8,128)}, f32[2,512,128]{2,1,0:T(8,128)}, u32[]{:S(2)}, u32[]{:S(2)}) collective-permute-start(f32[2,512,128]{2,1,0:T(8,128)} %pad_maximum_fusion.6), channel_id=1, source_target_pairs={{0,16},{16,0},{32,48},{48,32},{64,80},{80,64},{96,112},{112,96},{1... | collective-permute-start | bytes 1572872 | tf_op jit(solution)/shard_map/ppermute | solution.py:182
  193.1 3.3 %collective-permute-start.24 = (f32[2,512,128]{2,1,0:T(8,128)}, f32[2,512,128]{2,1,0:T(8,128)}, u32[]{:S(2)}, u32[]{:S(2)}) collective-permute-start(f32[2,512,128]{2,1,0:T(8,128)} %pad_maximum_fusion.7), channel_id=1, source_target_pairs={{0,16},{16,0},{32,48},{48,32},{64,80},{80,64},{96,112},{112,96},{1... | collective-permute-start | bytes 1572872 | tf_op jit(solution)/shard_map/ppermute | solution.py:182
  196.4 2.3 copy-start.4
  196.4 2.3 copy-start.6
  196.4 2.3 copy-start.7
Sparse Core Ops, SparseCore 0:
  27.8 5.2 sort.41.cloned.1.call-done
  69.7 64.5 all-gather.1
  (1 shorter events, 0.0 us)

commit v3 on v2

v3 whole, which is shorter than its diff:
```python
import jax
import jax.numpy as jnp
from jax import lax
from jax.experimental import pallas as pl
from jax.experimental.pallas import tpu as pltpu
from jax.sharding import PartitionSpec as P

VMEM = pl.BlockSpec(memory_space=pltpu.VMEM)
SMEM = pl.BlockSpec(memory_space=pltpu.SMEM)
PARAMS = pltpu.CompilerParams(vmem_limit_bytes=50 * 1024 * 1024)
BF = jnp.bfloat16


def f32(*shape):
    return jax.ShapeDtypeStruct(shape, jnp.float32)


def b16(*shape):
    return jax.ShapeDtypeStruct(shape, BF)


def split(t):
    high = t.astype(BF)
    return high, (t - high.astype(jnp.float32)).astype(BF)


def dot3(a, b):
    dot = lambda u, v: jnp.dot(u, v, preferred_element_type=jnp.float32)
    return dot(a[0], b[0]) + (dot(a[0], b[1]) + dot(a[1], b[0]))


def first_kernel(targets, x, out, slots, spots, sem):
    @pl.when(pl.program_id(0) == 0)
    def _():
        owner = lax.rem(lax.div(targets[...], 256), 8)
        hot = jnp.concatenate([(owner == d).astype(jnp.float32) for d in range(8)], axis=0)
        r = lax.broadcasted_iota(jnp.int32, (128, 128), 0)
        c = lax.broadcasted_iota(jnp.int32, (128, 128), 1)
        ahead = jnp.dot(hot, (r < c).astype(jnp.float32), preferred_element_type=jnp.float32)
        r = lax.broadcasted_iota(jnp.int32, (96, 96), 0)
        c = lax.broadcasted_iota(jnp.int32, (96, 96), 1)
        earlier = ((c < r) & (lax.div(r, 12) == lax.div(c, 12))).astype(jnp.float32)
        total = jnp.broadcast_to(jnp.sum(hot, axis=1, keepdims=True), (96, 128))
        ahead = ahead + jnp.dot(earlier, total, preferred_element_type=jnp.float32)
        slot = jnp.zeros((12, 128), jnp.float32)
        for d in range(8):
            part = slice(12 * d, 12 * d + 12)
            slot = slot + hot[part] * (ahead[part] + 192.0 * d)
        slots[...] = slot.astype(jnp.int32)
        copy = pltpu.make_async_copy(slots, spots, sem)
        copy.start()
        copy.wait()

    base = pl.program_id(0) * 3

    def step(j, carry):
        for q in range(3):
            out[spots[base + q, j]] = x[384 * q + 3 * j]
        return carry

    lax.fori_loop(0, 128, step, 0, unroll=4)


def send_first(targets, x):
    return pl.pallas_call(
        first_kernel,
        out_shape=(f32(1536, 2, 128), jax.ShapeDtypeStruct((12, 128), jnp.int32)),
        grid=(4,),
        in_specs=[
            pl.BlockSpec((12, 128), lambda i: (0, 0)),
            pl.BlockSpec((1152, 2, 128), lambda i: (i, 0, 0)),
        ],
        out_specs=(
            pl.BlockSpec((1536, 2, 128), lambda i: (0, 0, 0)),
            pl.BlockSpec((12, 128), lambda i: (0, 0)),
        ),
        scratch_shapes=[pltpu.SMEM((12, 128), jnp.int32), pltpu.SemaphoreType.DMA],
        compiler_params=PARAMS,
        name="send_first",
    )(targets, x)


def rest_kernel(slots, x, second, third):
    base = pl.program_id(0) * 3

    def step(j, carry):
        for q in range(3):
            d, r = slots[base + q, j], 384 * q + 3 * j
            second[d] = x[r + 1]
            third[d] = x[r + 2]
        return carry

    lax.fori_loop(0, 128, step, 0, unroll=4)


def send_rest(slots, x):
    return pl.pallas_call(
        rest_kernel,
        out_shape=[f32(1536, 2, 128)] * 2,
        grid=(4,),
        in_specs=[SMEM, pl.BlockSpec((1152, 2, 128), lambda i: (i, 0, 0))],
        out_specs=[pl.BlockSpec((1536, 2, 128), lambda i: (0, 0, 0))] * 2,
        compiler_params=PARAMS,
        name="send_rest",
    )(slots, x)


def top_kernel(order, p0, p1, arrived, out):
    out[:256] = p0[...]
    out[256:512] = p1[...]

    def step(d, carry):
        out[512 + d] = arrived[order[d]]
        return carry

    lax.fori_loop(0, 256, step, 0, unroll=8)


def top_rows(order, p0, p1, arrived):
    own = pl.BlockSpec((256, 2, 128), lambda i: (0, 0, 0))
    return pl.pallas_call(
        top_kernel,
        out_shape=f32(768, 2, 128),
        grid=(1,),
        in_specs=[SMEM, own, own, pl.BlockSpec((1536, 2, 128), lambda i: (0, 0, 0))],
        out_specs=pl.BlockSpec((768, 2, 128), lambda i: (0, 0, 0)),
        compiler_params=PARAMS,
        name="top_rows",
    )(order, p0, p1, arrived)


def place_kernel(order, arrived, out):
    def step(d, carry):
        out[d] = arrived[order[d]]
        return carry

    lax.fori_loop(0, 1536, step, 0, unroll=8)


def place_rows(order, arrived):
    return pl.pallas_call(
        place_kernel,
        out_shape=f32(*arrived.shape),
        in_specs=[SMEM, VMEM],
        out_specs=VMEM,
        compiler_params=PARAMS,
        name="place_rows",
    )(order, arrived)


def corner_rows_kernel(place, pieces, out):
    here_y, here_row = place[1], place[4]
    for j in range(3):
        k = j + (here_row <= j).astype(jnp.int32)
        out[j] = pieces[lax.rem(here_y - k + 4, 4)]


def pair(ref, index, rows, first=0):
    left = ref[index + (pl.ds(first, rows, stride=2),)]
    right = ref[index + (pl.ds(first + 1, rows, stride=2),)]
    return jnp.concatenate([left, right], axis=1)


def block(k):
    return slice(256 * k, 256 * k + 256)


RIGHT = (0, 768, 1280, 1536)
LEFT = (0, 0, 256, 768)


def right(k, j):
    return block(RIGHT[k] // 256 + j - k - 1)


def left(k, m):
    return block(LEFT[k] // 256 + m)


def corner_kernel(place, lower_fill, upper_fill, mine, other, inv, vh, vl, ih, il, wh, wl):
    here_x, core = place[0], place[2]

    def corner(b, k):
        parts = []
        for i in range(4):
            at = (lax.rem(here_x - i + 4, 4), b // 2, k - (k > b))
            parts.append(jnp.where(core == b % 2, pair(mine, at, 64), pair(other, at, 64)))
        return jnp.concatenate(parts, axis=0)

    for k in range(4):
        ih[k], il[k] = split(inv[k])
    low, high = {}, {}
    for k in range(4):
        for m in range(k):
            t = dot3(split(corner(k, m)), (ih[m], il[m]))
            for n in range(m):
                t = t - dot3(low[k, n], (vh[:, right(n, m)], vl[:, right(n, m)]))
            keep = (lower_fill[m, k] == 1).astype(jnp.float32)
            low[k, m] = split(t * keep)
            wh[:, left(k, m)], wl[:, left(k, m)] = low[k, m]
        for j in range(k + 1, 4):
            t = corner(k, j)
            for m in range(k):
                t = t - dot3(low[k, m], high[m, j])
            keep = (upper_fill[k, j] == 1).astype(jnp.float32)
            high[k, j] = split(t * keep)
            t = dot3(high[k, j], (ih[j], il[j]))
            vh[:, right(k, j)], vl[:, right(k, j)] = split(t)


def update_kernel(
    place, lower_fill, upper_fill, panels, p0, p1, p2, mine, other, vh, vl, ih, il, wh, wl,
    out, acc, lh, ll, uh, ul
):
    core, here_col, here_row = place[2], place[3], place[4]

    @pl.when(pl.program_id(0) == 0)
    def _():
        for k in range(4):
            before = slice(0, 256 * k)
            lefts = slice(LEFT[k], LEFT[k] + 256 * k)
            for c in range(3):
                at, first = (k // 2,), 512 * c
                t = jnp.where(
                    core == k % 2, pair(mine, at, 256, first), pair(other, at, 256, first)
                )
                if k:
                    t = t - dot3(
                        (wh[:, lefts], wl[:, lefts]), (uh[before, block(c)], ul[before, block(c)])
                    )
                j = c * 16 + here_col
                keep = ((j > k) & (upper_fill[k, j] == 1)).astype(jnp.float32)
                uh[block(k), block(c)], ul[block(k), block(c)] = split(t * keep)

    group = lax.broadcasted_iota(jnp.int32, (384, 1), 0) // 64

    def per_row(values):
        t = values[5]
        for g in range(5):
            t = jnp.where(group == g, values[g], t)
        return t

    blocks = [g * 8 + here_row for g in range(6)]
    for k in range(4):
        acc[:, block(k)] = dot3(split(pair(panels, (0, k), 384)), (ih[k], il[k]))
    for k in range(4):
        keep = [((b > k) & (lower_fill[k, b] == 1)).astype(jnp.float32) for b in blocks]
        t = acc[:, block(k)] * per_row(keep)
        acc[:, block(k)] = t
        high, low = split(t)
        lh[:, block(k)], ll[:, block(k)] = high, low
        if k < 3:
            after = slice(256 * k + 256, 1024)
            rights = slice(RIGHT[k], RIGHT[k + 1])
            acc[:, after] -= dot3((high, low), (vh[:, rights], vl[:, rights]))
    done = (here_col < 4) & (per_row(blocks) > here_col)
    own = pl.ds(pl.multiple_of(jnp.minimum(here_col, 3) * 256, 256), 256)
    for c in range(3):
        t = dot3((lh[...], ll[...]), (uh[:, block(c)], ul[:, block(c)]))
        for g in range(6):
            here = slice(64 * g, 64 * g + 64)
            new = pair((p0, p1, p2)[c], (g, 0), 64) - t[here]
            if c == 0:
                new = jnp.where(done[here], acc[here, own], new)
            out[g, 0, pl.ds(2 * c, 64, stride=6), :] = new[:, :128]
            out[g, 0, pl.ds(2 * c + 1, 64, stride=6), :] = new[:, 128:]


def whole(*shape):
    return pl.BlockSpec(shape, lambda i: (0,) * len(shape))


def scatter_x(blocks):
    return [
        lax.ppermute(blocks[s], "pcol", [(k, k + 4 * s) for k in range(4)]) for s in range(1, 4)
    ]


def scattered(block, got, here_x):
    return jnp.where(here_x == 0, block, got[0] + got[1] + got[2])


def hop_z(value, pairs):
    return lax.ppermute(value, "prow", [(2 * a + c, 2 * b + c) for a, b in pairs for c in (0, 1)])


def spread_z(top, hops, here_z):
    away, near = hops
    on = hop_z(away, [(3, 2), (2, 3)])
    d0 = jnp.where(here_z == 0, top, jnp.where(here_z == 1, near, jnp.where(here_z == 2, on, away)))
    d1 = jnp.where(here_z == 1, top, jnp.where(here_z == 0, near, jnp.where(here_z == 3, on, away)))
    return jnp.stack([d0, d1])


def with_other(mine):
    return mine, lax.ppermute(mine, "prow", [(p, p ^ 1) for p in range(8)])


def first_hops(top):
    return hop_z(top, [(0, 3), (1, 2)]), hop_z(top, [(0, 1), (1, 0)])


def body(matrix, row_order, inverses, lower_fill, upper_fill):
    here_row = lax.axis_index("prow")
    here_col = lax.axis_index("pcol")
    here_x, here_y = here_col // 4, here_col % 4
    here_z, core = here_row // 2, here_row % 2
    x = matrix.reshape(4608, 2, 128)
    targets = row_order.reshape(6, 8, 256)
    local = jnp.arange(1536, dtype=jnp.int32)

    def keys(t):
        owner, row = t // 256 % 8, t // 2048 * 256 + t % 256
        return (owner * 2048 + local) * 2048 + row

    mine = lax.dynamic_slice(targets, (0, here_row, 0), (6, 1, 256)).reshape(12, 128)
    s0, slots = send_first(mine, x)
    s1, s2 = send_rest(slots, x)
    a2a = lambda s: lax.all_to_all(s.reshape(8, -1, 128), "prow", 0, 0, tiled=True)
    g0 = a2a(s0).reshape(1536, 2, 128)
    all_keys = lax.sort(keys(targets.transpose(1, 0, 2).reshape(8, 1536)), dimension=1)
    places = lax.dynamic_slice(all_keys, (0, here_row * 192), (8, 192)).reshape(1536) % 2048
    backward = lax.sort(places * 2048 + local) % 2048
    backward, s1 = lax.optimization_barrier((backward, s1))
    g1, g2 = [a2a(s).reshape(1536, 2, 128) for s in (s1, s2)]
    p0 = place_rows(backward, g0)
    parts0 = p0.reshape(6, 4, 128, 128)
    got, g1 = lax.optimization_barrier((scatter_x([parts0[:, i] for i in range(4)]), g1))
    quarter = scattered(parts0[:, 0], got, here_x)
    panels = lax.all_gather(quarter.reshape(768, 128), "pcol", axis=0, tiled=True)
    panels = panels.reshape(4, 4, 768, 128)
    p1 = place_rows(backward, g1)
    along_y = lambda s: [(q, q // 4 * 4 + (q + s) % 4) for q in range(16)]
    along_x = lambda s: [(q, (q + 4 * s) % 16) for q in range(16)]
    shifts = lambda v, along: [lax.ppermute(v, "pcol", along(s)) for s in (1, 2, 3)]
    corner, p1 = lax.optimization_barrier((jnp.stack([quarter[0]] + shifts(quarter[0], along_y)), p1))
    place = jnp.stack([here_x, here_y, core, here_col, here_row]).astype(jnp.int32)
    corner = pl.pallas_call(
        corner_rows_kernel,
        out_shape=f32(3, 128, 128),
        in_specs=[SMEM, VMEM],
        out_specs=VMEM,
        compiler_params=PARAMS,
        name="corner_rows",
    )(place, corner)
    hops, g2 = lax.optimization_barrier((first_hops(corner), g2))
    corner = spread_z(corner, hops, here_z)
    top = top_rows(backward[:256], p0, p1, g2).reshape(1536, 128)
    far, hops = lax.optimization_barrier((shifts(corner, along_x), first_hops(top)))
    corner = with_other(jnp.stack([corner] + far))
    p2 = place_rows(backward, g2)
    rows = with_other(spread_z(top, hops, here_z))
    parts = pl.pallas_call(
        corner_kernel,
        out_shape=[b16(256, 1536)] * 2 + [b16(4, 256, 256)] * 2 + [b16(256, 1536)] * 2,
        in_specs=[SMEM] * 3 + [VMEM] * 3,
        out_specs=[VMEM] * 6,
        compiler_params=PARAMS,
        name="corner",
    )(place, lower_fill, upper_fill, *corner, inverses)
    part = lambda n: pl.BlockSpec((6, 1, n, 128), lambda i: (0, i, 0, 0))
    out = pl.pallas_call(
        update_kernel,
        out_shape=f32(6, 4, 384, 128),
        grid=(4,),
        in_specs=[SMEM] * 3
        + [pl.BlockSpec((1, 4, 768, 128), lambda i: (i, 0, 0, 0))]
        + [part(128)] * 3
        + [whole(2, 1536, 128)] * 2
        + [whole(256, 1536)] * 2
        + [whole(4, 256, 256)] * 2
        + [whole(256, 1536)] * 2,
        out_specs=part(384),
        scratch_shapes=[
            pltpu.VMEM((384, 1024), jnp.float32),
            pltpu.VMEM((384, 1024), BF),
            pltpu.VMEM((384, 1024), BF),
            pltpu.VMEM((1024, 768), BF),
            pltpu.VMEM((1024, 768), BF),
        ],
        compiler_params=PARAMS,
        name="update",
    )(
        place, lower_fill, upper_fill, panels,
        *[p.reshape(6, 4, 128, 128) for p in (p0, p1, p2)], *rows, *parts
    )
    return out.reshape(6, 1, 256, 3, 1, 256)


def solution(mesh):
    in_specs = (P(None, "prow", None, None, "pcol", None), P(), P(), P(), P())
    out_specs = P(None, "prow", None, None, "pcol", None)
    return jax.shard_map(body, mesh=mesh, in_specs=in_specs, out_specs=out_specs, check_vma=False)
```

time: 244 us -> 225 us (0.922)
  the two profiles are of different devices: /device:TPU:1 before, /device:TPU:90 now
where the time goes in v3:
time: 225 us; the launch traced here: 224 us
  waiting for transfers between devices  78 us (35%)
  Pallas kernels  58.6 us (26%)
  starting transfers between devices  46.9 us (21%)
  local copies, waits for them, and re-layouts  16.6 us (7%)
  between operations  13.8 us (6%)
  other arithmetic  10.6 us (5%)
    ppermute x6, waiting for transfers between devices, body(): lax.ppermute(v, 'pcol', along(s))  34.7 us
    pallas_call x1, Pallas kernels, body(): pl.pallas_call(update_kernel, out_shape=f32(6, 4, 384, 128), grid=(4,), i...  26.3 us
    ppermute x6, waiting for transfers between devices, hop_z(): lax.ppermute(value, 'prow', [(2 * a + c, 2 * b + c) for a, b in pairs for...  21.6 us
    all_to_all x3, waiting for transfers between devices, body(): lax.all_to_all(s.reshape(8, -1, 128), 'prow', 0, 0, tiled=True)  16.8 us
    all_to_all x3, starting transfers between devices, body(): lax.all_to_all(s.reshape(8, -1, 128), 'prow', 0, 0, tiled=True)  16.5 us
    ppermute x6, starting transfers between devices, body(): lax.ppermute(v, 'pcol', along(s))  15 us
    unnamed x35, local copies, waits for them, and re-layouts  12.8 us
    ppermute x6, starting transfers between devices, hop_z(): lax.ppermute(value, 'prow', [(2 * a + c, 2 * b + c) for a, b in pairs for...  10.9 us
  transfers between devices with their start and end apart: 21, of which 8 were waited for; matrix products, arithmetic and copies ran while one was open for 5% of the time, Pallas kernels for 11%

profile of v3, /device:TPU:90, one launch (start us, length us, event | category | flops | bytes accessed | tf_op | source)
XLA Modules:
  0.0 224.4 jit_solution(3837220076190142008)
XLA Ops:
  6.5 0.8 reshape.55
  7.4 7.6 %send_first.1 = (f32[1536,2,128]{2,1,0:T(2,128)}, s32[12,128]{1,0:T(8,128)S(1)}) custom-call(s32[12,128]{1,0:T(8,128)S(1)} %reshape.58.targets, f32[4608,2,128]{2,1,0:T(2,128)} %bitcast.67), custom_call_target="tpu_custom_call" | custom-call | tf_op jit(solution)/shard_map/send_first/pallas_call | solution.py:65
  15.0 5.0 %all-to-all-start = ((f32[8,384,128]{2,1,0:T(8,128)}), f32[8,384,128]{2,1,0:T(8,128)S(1)}, u32[]{:S(2)}, u32[]{:S(2)}) async-start(f32[8,384,128]{2,1,0:T(8,128)} %bitcast.9), calls=%async_computation | async-start | bytes 3145728 | tf_op jit(solution)/shard_map/all_to_all | solution.py:319
  20.8 5.9 %send_rest.1 = (f32[1536,2,128]{2,1,0:T(2,128)S(1)}, f32[1536,2,128]{2,1,0:T(2,128)S(1)}) custom-call(s32[12,128]{1,0:T(8,128)S(1)} %get-tuple-element.34.slots, f32[4608,2,128]{2,1,0:T(2,128)} %bitcast.68), custom_call_target="tpu_custom_call" | custom-call | tf_op jit(solution)/shard_map/send_rest/pallas_call | solution.py:97
  26.7 1.2 copy-done.10
  27.9 1.2 copy-done.11
  29.9 5.0 %sort.22 = (s32[1536]{0:T(1024)S(1)}, s32[1536]{0:T(1024)}) sort(s32[1536]{0:T(1024)S(1)} %fusion.15, s32[1536]{0:T(1024)S(1)} %iota.10), dimensions={0}, to_apply=%region_1.2 | sort | flops 16896 | bytes 24576 | tf_op jit(solution)/shard_map/sort | solution.py:323
  35.0 3.5 %all-to-all-done = f32[8,384,128]{2,1,0:T(8,128)S(1)} async-done(((f32[8,384,128]{2,1,0:T(8,128)}), f32[8,384,128]{2,1,0:T(8,128)S(1)}, u32[]{:S(2)}, u32[]{:S(2)}) %all-to-all-start) | async-done | bytes 1572896 | tf_op jit(solution)/shard_map/all_to_all | solution.py:319
  38.4 1.1 copy-done.7
  39.6 6.7 %all-to-all-start.1 = ((f32[8,384,128]{2,1,0:T(8,128)}), f32[8,384,128]{2,1,0:T(8,128)S(1)}, u32[]{:S(2)}, u32[]{:S(2)}) async-start(f32[8,384,128]{2,1,0:T(8,128)} %bitcast.66), calls=%async_computation.1 | async-start | bytes 3145728 | tf_op jit(solution)/shard_map/all_to_all | solution.py:319
  46.2 1.4 copy-done.8
  47.7 3.2 %place_rows.3.p0 = f32[1536,2,128]{2,1,0:T(2,128)S(1)} custom-call(s32[1536]{0:T(1024)S(1)} %add_select_fusion.4.order, f32[1536,2,128]{2,1,0:T(2,128)S(1)} %bitcast.63), custom_call_target="tpu_custom_call" | custom-call | tf_op jit(solution)/shard_map/place_rows/pallas_call | solution.py:141
  50.8 1.1 slice_bitcast_fusion
  52.0 1.4 collective-permute-start.2
  53.4 1.3 collective-permute-start
  54.7 1.4 collective-permute-start.1
  56.1 8.5 %all-to-all-done.1 = f32[8,384,128]{2,1,0:T(8,128)S(1)} async-done(((f32[8,384,128]{2,1,0:T(8,128)}), f32[8,384,128]{2,1,0:T(8,128)S(1)}, u32[]{:S(2)}, u32[]{:S(2)}) %all-to-all-start.1) | async-done | bytes 1572896 | tf_op jit(solution)/shard_map/all_to_all | solution.py:319
  64.6 4.8 %collective-permute-done = f32[6,128,128]{2,1,0:T(8,128)} collective-permute-done((f32[6,128,128]{2,1,0:T(8,128)}, f32[6,128,128]{2,1,0:T(8,128)}, u32[]{:S(2)}, u32[]{:S(2)}) %collective-permute-start) | collective-permute-done | bytes 393248 | tf_op jit(solution)/shard_map/ppermute | solution.py:275
  69.4 2.1 fusion
  71.5 4.8 %all-to-all-start.2 = ((f32[8,384,128]{2,1,0:T(8,128)}), f32[8,384,128]{2,1,0:T(8,128)S(1)}, u32[]{:S(2)}, u32[]{:S(2)}) async-start(f32[8,384,128]{2,1,0:T(8,128)} %bitcast.65), calls=%async_computation.2 | async-start | bytes 3145728 | tf_op jit(solution)/shard_map/all_to_all | solution.py:319
  76.3 0.8 fusion.18
  78.0 0.9 collective-permute-start.4
  79.0 2.2 collective-permute-start.3
  81.2 1.4 copy-done.6
  82.6 3.2 %place_rows.4.p1 = f32[1536,2,128]{2,1,0:T(2,128)S(1)} custom-call(s32[1536]{0:T(1024)S(1)} %add_select_fusion.4.order, f32[1536,2,128]{2,1,0:T(2,128)S(1)} %bitcast.62), custom_call_target="tpu_custom_call" | custom-call | tf_op jit(solution)/shard_map/place_rows/pallas_call | solution.py:141
  85.8 1.1 copy-done.3
  87.6 1.3 collective-permute-start.7
  88.9 1.3 collective-permute-start.6
  90.2 4.8 %all-to-all-done.2 = f32[8,384,128]{2,1,0:T(8,128)S(1)} async-done(((f32[8,384,128]{2,1,0:T(8,128)}), f32[8,384,128]{2,1,0:T(8,128)S(1)}, u32[]{:S(2)}, u32[]{:S(2)}) %all-to-all-start.2) | async-done | bytes 1572896 | tf_op jit(solution)/shard_map/all_to_all | solution.py:319
  95.0 4.1 %collective-permute-done.6 = f32[3,128,128]{2,1,0:T(8,128)} collective-permute-done((f32[3,128,128]{2,1,0:T(8,128)S(1)}, f32[3,128,128]{2,1,0:T(8,128)}, u32[]{:S(2)}, u32[]{:S(2)}) %collective-permute-start.6) | collective-permute-done | bytes 196640 | tf_op jit(solution)/shard_map/ppermute | solution.py:284
  99.1 4.2 %collective-permute-start.8 = (f32[3,128,128]{2,1,0:T(8,128)}, f32[3,128,128]{2,1,0:T(8,128)}, u32[]{:S(2)}, u32[]{:S(2)}) collective-permute-start(f32[3,128,128]{2,1,0:T(8,128)} %collective-permute-done.6), channel_id=1, source_target_pairs={{96,64},{112,80},{64,96},{80,112},{97,65},{113,81},{65,97},{81,113... | collective-permute-start | bytes 589832 | tf_op jit(solution)/shard_map/ppermute | solution.py:284
  103.3 1.4 copy-done.4
  104.7 2.8 %top_rows.1 = f32[768,2,128]{2,1,0:T(2,128)} custom-call(s32[256]{0:T(256)S(1)} %slice.24.order, f32[1536,2,128]{2,1,0:T(2,128)S(1)} %place_rows.3.p0, f32[1536,2,128]{2,1,0:T(2,128)S(1)} %copy-done.4, f32[1536,2,128]{2,1,0:T(2,128)} %bitcast.59), custom_call_target="tpu_custom_call" | custom-call | tf_op jit(solution)/shard_map/top_rows/pallas_call | solution.py:121
  108.2 1.3 collective-permute-start.12
  109.6 1.2 select_bitcast_fusion.3
  110.8 7.2 %collective-permute-start.11 = (f32[2,3,128,128]{3,2,1,0:T(8,128)S(1)}, f32[2,3,128,128]{3,2,1,0:T(8,128)S(1)}, u32[]{:S(2)}, u32[]{:S(2)}) collective-permute-start(f32[2,3,128,128]{3,2,1,0:T(8,128)S(1)} %get-tuple-element.68), channel_id=1, source_target_pairs={{0,12},{1,13},{2,14},{3,15},{4,0},{5,1},{6,2},{7,3},{8,4},{9,5},{1... | collective-permute-start | bytes 1179656 | tf_op jit(solution)/shard_map/ppermute | solution.py:335
  118.1 3.9 %collective-permute-start.10 = (f32[2,3,128,128]{3,2,1,0:T(8,128)S(1)}, f32[2,3,128,128]{3,2,1,0:T(8,128)S(1)}, u32[]{:S(2)}, u32[]{:S(2)}) collective-permute-start(f32[2,3,128,128]{3,2,1,0:T(8,128)S(1)} %get-tuple-element.68), channel_id=1, source_target_pairs={{0,8},{1,9},{2,10},{3,11},{4,12},{5,13},{6,14},{7,15},{8,0},{9,1},... | collective-permute-start | bytes 1179656 | tf_op jit(solution)/shard_map/ppermute | solution.py:335
  121.9 16.5 %collective-permute-done.11 = f32[2,3,128,128]{3,2,1,0:T(8,128)S(1)} collective-permute-done((f32[2,3,128,128]{3,2,1,0:T(8,128)S(1)}, f32[2,3,128,128]{3,2,1,0:T(8,128)S(1)}, u32[]{:S(2)}, u32[]{:S(2)}) %collective-permute-start.11) | collective-permute-done | bytes 393248 | tf_op jit(solution)/shard_map/ppermute | solution.py:335
  138.4 18.2 %collective-permute-done.10 = f32[2,3,128,128]{3,2,1,0:T(8,128)S(1)} collective-permute-done((f32[2,3,128,128]{3,2,1,0:T(8,128)S(1)}, f32[2,3,128,128]{3,2,1,0:T(8,128)S(1)}, u32[]{:S(2)}, u32[]{:S(2)}) %collective-permute-start.10) | collective-permute-done | bytes 393248 | tf_op jit(solution)/shard_map/ppermute | solution.py:335
  156.6 2.2 collective-permute-start.14
  159.0 17.5 %collective-permute-done.14 = f32[1536,128]{1,0:T(8,128)S(1)} collective-permute-done((f32[1536,128]{1,0:T(8,128)S(1)}, f32[1536,128]{1,0:T(8,128)S(1)}, u32[]{:S(2)}, u32[]{:S(2)}) %collective-permute-start.14) | collective-permute-done | bytes 786464 | tf_op jit(solution)/shard_map/ppermute | solution.py:284
  176.5 1.3 select_bitcast_fusion.1
  178.3 1.5 copy-done.2
  179.8 3.2 %place_rows.5 = f32[1536,2,128]{2,1,0:T(2,128)S(1)} custom-call(s32[1536]{0:T(1024)S(1)} %add_select_fusion.4.order, f32[1536,2,128]{2,1,0:T(2,128)S(1)} %bitcast.60), custom_call_target="tpu_custom_call" | custom-call | tf_op jit(solution)/shard_map/place_rows/pallas_call | solution.py:141
  183.0 1.2 copy-done.9
  184.2 1.1 copy-done.16
  185.4 5.9 %corner.1 = (bf16[256,1536]{1,0:T(8,128)(2,1)S(1)}, bf16[256,1536]{1,0:T(8,128)(2,1)S(1)}, bf16[4,256,256]{2,1,0:T(8,128)(2,1)S(1)}, bf16[4,256,256]{2,1,0:T(8,1...) custom-call(s32[5]{0:T(128)S(1)} %stack.68.place, s32[4,48]{1,0:T(4,128)S(1)} %copy-done.12, ...), custom_call_target="tpu_custom_call" | custom-call | tf_op jit(solution)/shard_map/corner/pallas_call | solution.py:353
  191.2 26.3 %update.1 = f32[6,4,384,128]{3,2,1,0:T(8,128)} custom-call(s32[5]{0:T(128)S(1)} %stack.68.place, s32[4,48]{1,0:T(4,128)S(1)} %copy-done.12, s32[4,48]{1,0:T(4,128)S(1)} %copy-done.13, f32[4,4,768,128]{3,2,1,0:T(8,128)} %bitcast.69, f32[6,4,128,128]{3,2,1,0:T(8,128)} %bitcast.58, f32[6,4,128,128]{3,2,1,0:T(8,128)} %bitcast.61, f32[6,4,128,128]{3,2,1,0:T(8,128)} %bitcast.64, ...), custom_call_target="tpu_custom_call" | custom-call | tf_op jit(solution)/shard_map/update/pallas_call | solution.py:362
  (62 shorter events, 4.6 us)
Async XLA Ops:
  15.0 23.4 %all-to-all-start = ((f32[8,384,128]{2,1,0:T(8,128)}), f32[8,384,128]{2,1,0:T(8,128)S(1)}, u32[]{:S(2)}, u32[]{:S(2)}) async-start(f32[8,384,128]{2,1,0:T(8,128)} %bitcast.9), calls=%async_computation | async-start | bytes 3145728 | tf_op jit(solution)/shard_map/all_to_all | solution.py:319
  20.0 9.0 %sort.24.cloned.1.call-start = ((), (), s32[]{:S(2)}) async-start(), calls=%async_computation.4 | async-start | bytes 147488 | tf_op jit(solution)/shard_map/sort | solution.py:321
  26.6 1.2 copy-start.10
  27.8 1.2 copy-start.11
  38.4 1.1 copy-start.7
  39.6 25.1 %all-to-all-start.1 = ((f32[8,384,128]{2,1,0:T(8,128)}), f32[8,384,128]{2,1,0:T(8,128)S(1)}, u32[]{:S(2)}, u32[]{:S(2)}) async-start(f32[8,384,128]{2,1,0:T(8,128)} %bitcast.66), calls=%async_computation.1 | async-start | bytes 3145728 | tf_op jit(solution)/shard_map/all_to_all | solution.py:319
  46.2 145.0 %all-gather.2.cloned.1.call-start = ((), (), s32[]{:S(2)}) async-start(), calls=%async_computation.3 | async-start | bytes 6684672 | tf_op jit(solution)/shard_map/all_gather | solution.py:330
  46.2 1.4 copy-start.8
  50.8 52.4 %copy-start = (f32[1536,2,128]{2,1,0:T(2,128)}, f32[1536,2,128]{2,1,0:T(2,128)S(1)}, u32[]{:S(2)}) copy-start(f32[1536,2,128]{2,1,0:T(2,128)S(1)} %place_rows.3.p0) | copy-start | bytes 4718596
  52.0 12.7 %collective-permute-start.2 = (f32[6,128,128]{2,1,0:T(8,128)}, f32[6,128,128]{2,1,0:T(8,128)}, u32[]{:S(2)}, u32[]{:S(2)}) collective-permute-start(f32[6,128,128]{2,1,0:T(8,128)} %get-tuple-element.62), channel_id=1, source_target_pairs={{0,12},{1,13},{2,14},{3,15},{16,28},{17,29},{18,30},{19,31},{32,44... | collective-permute-start | bytes 1179656 | tf_op jit(solution)/shard_map/ppermute | solution.py:275
  53.4 16.1 %collective-permute-start = (f32[6,128,128]{2,1,0:T(8,128)}, f32[6,128,128]{2,1,0:T(8,128)}, u32[]{:S(2)}, u32[]{:S(2)}) collective-permute-start(f32[6,128,128]{2,1,0:T(8,128)} %get-tuple-element.63), channel_id=1, source_target_pairs={{0,4},{1,5},{2,6},{3,7},{16,20},{17,21},{18,22},{19,23},{32,36},{3... | collective-permute-start | bytes 1179656 | tf_op jit(solution)/shard_map/ppermute | solution.py:275
  54.7 14.8 %collective-permute-start.1 = (f32[6,128,128]{2,1,0:T(8,128)}, f32[6,128,128]{2,1,0:T(8,128)}, u32[]{:S(2)}, u32[]{:S(2)}) collective-permute-start(f32[6,128,128]{2,1,0:T(8,128)} %get-tuple-element.64), channel_id=1, source_target_pairs={{0,8},{1,9},{2,10},{3,11},{16,24},{17,25},{18,26},{19,27},{32,40},... | collective-permute-start | bytes 1179656 | tf_op jit(solution)/shard_map/ppermute | solution.py:275
  64.6 6.9 %copy-start.5 = (f32[8,384,128]{2,1,0:T(8,128)}, f32[8,384,128]{2,1,0:T(8,128)S(1)}, u32[]{:S(2)}) copy-start(f32[8,384,128]{2,1,0:T(8,128)S(1)} %all-to-all-done.1) | copy-start | bytes 4718596
  71.5 23.5 %all-to-all-start.2 = ((f32[8,384,128]{2,1,0:T(8,128)}), f32[8,384,128]{2,1,0:T(8,128)S(1)}, u32[]{:S(2)}, u32[]{:S(2)}) async-start(f32[8,384,128]{2,1,0:T(8,128)} %bitcast.65), calls=%async_computation.2 | async-start | bytes 3145728 | tf_op jit(solution)/shard_map/all_to_all | solution.py:319
  77.2 9.7 %collective-permute-start.5 = (f32[128,128]{1,0:T(8,128)S(1)}, f32[128,128]{1,0:T(8,128)S(1)}, u32[]{:S(2)}, u32[]{:S(2)}) collective-permute-start(f32[128,128]{1,0:T(8,128)S(1)} %get-tuple-element.70), channel_id=1, source_target_pairs={{0,3},{1,0},{2,1},{3,2},{4,7},{5,4},{6,5},{7,6},{8,11},{9,8},{10,9... | collective-permute-start | bytes 196616 | tf_op jit(solution)/shard_map/ppermute | solution.py:335
  78.0 8.9 %collective-permute-start.4 = (f32[128,128]{1,0:T(8,128)S(1)}, f32[128,128]{1,0:T(8,128)S(1)}, u32[]{:S(2)}, u32[]{:S(2)}) collective-permute-start(f32[128,128]{1,0:T(8,128)S(1)} %get-tuple-element.70), channel_id=1, source_target_pairs={{0,2},{1,3},{2,0},{3,1},{4,6},{5,7},{6,4},{7,5},{8,10},{9,11},{10,... | collective-permute-start | bytes 196616 | tf_op jit(solution)/shard_map/ppermute | solution.py:335
  79.0 8.0 %collective-permute-start.3 = (f32[128,128]{1,0:T(8,128)S(1)}, f32[128,128]{1,0:T(8,128)S(1)}, u32[]{:S(2)}, u32[]{:S(2)}) collective-permute-start(f32[128,128]{1,0:T(8,128)S(1)} %get-tuple-element.70), channel_id=1, source_target_pairs={{0,1},{1,2},{2,3},{3,0},{4,5},{5,6},{6,7},{7,4},{8,9},{9,10},{10,1... | collective-permute-start | bytes 196616 | tf_op jit(solution)/shard_map/ppermute | solution.py:335
  81.2 1.4 copy-start.6
  85.8 1.1 copy-start.3
  87.6 7.4 %collective-permute-start.7 = (f32[3,128,128]{2,1,0:T(8,128)S(1)}, f32[3,128,128]{2,1,0:T(8,128)}, u32[]{:S(2)}, u32[]{:S(2)}) collective-permute-start(f32[3,128,128]{2,1,0:T(8,128)S(1)} %corner_rows.1), channel_id=1, source_target_pairs={{0,32},{16,48},{32,0},{48,16},{1,33},{17,49},{33,1},{49,17},{2,34}... | collective-permute-start | bytes 589832 | tf_op jit(solution)/shard_map/ppermute | solution.py:284
  88.9 10.2 %collective-permute-start.6 = (f32[3,128,128]{2,1,0:T(8,128)S(1)}, f32[3,128,128]{2,1,0:T(8,128)}, u32[]{:S(2)}, u32[]{:S(2)}) collective-permute-start(f32[3,128,128]{2,1,0:T(8,128)S(1)} %corner_rows.1), channel_id=1, source_target_pairs={{0,96},{16,112},{32,64},{48,80},{1,97},{17,113},{33,65},{49,81},{2... | collective-permute-start | bytes 589832 | tf_op jit(solution)/shard_map/ppermute | solution.py:284
  95.0 8.3 %copy-start.1 = (f32[8,384,128]{2,1,0:T(8,128)}, f32[8,384,128]{2,1,0:T(8,128)S(1)}, u32[]{:S(2)}) copy-start(f32[8,384,128]{2,1,0:T(8,128)S(1)} %all-to-all-done.2) | copy-start | bytes 4718596
  99.1 10.5 %collective-permute-start.8 = (f32[3,128,128]{2,1,0:T(8,128)}, f32[3,128,128]{2,1,0:T(8,128)}, u32[]{:S(2)}, u32[]{:S(2)}) collective-permute-start(f32[3,128,128]{2,1,0:T(8,128)} %collective-permute-done.6), channel_id=1, source_target_pairs={{96,64},{112,80},{64,96},{80,112},{97,65},{113,81},{65,97},{81,113... | collective-permute-start | bytes 589832 | tf_op jit(solution)/shard_map/ppermute | solution.py:284
  103.3 1.4 copy-start.4
  107.5 49.1 %collective-permute-start.13 = (f32[1536,128]{1,0:T(8,128)}, f32[1536,128]{1,0:T(8,128)S(1)}, u32[]{:S(2)}, u32[]{:S(2)}) collective-permute-start(f32[1536,128]{1,0:T(8,128)} %bitcast.28), channel_id=1, source_target_pairs={{0,32},{16,48},{32,0},{48,16},{1,33},{17,49},{33,1},{49,17},{2,34}... | collective-permute-start | bytes 2359304 | tf_op jit(solution)/shard_map/ppermute | solution.py:284
  108.2 48.4 %collective-permute-start.12 = (f32[1536,128]{1,0:T(8,128)}, f32[1536,128]{1,0:T(8,128)S(1)}, u32[]{:S(2)}, u32[]{:S(2)}) collective-permute-start(f32[1536,128]{1,0:T(8,128)} %bitcast.28), channel_id=1, source_target_pairs={{0,96},{16,112},{32,64},{48,80},{1,97},{17,113},{33,65},{49,81},{2... | collective-permute-start | bytes 2359304 | tf_op jit(solution)/shard_map/ppermute | solution.py:284
  110.8 27.6 %collective-permute-start.11 = (f32[2,3,128,128]{3,2,1,0:T(8,128)S(1)}, f32[2,3,128,128]{3,2,1,0:T(8,128)S(1)}, u32[]{:S(2)}, u32[]{:S(2)}) collective-permute-start(f32[2,3,128,128]{3,2,1,0:T(8,128)S(1)} %get-tuple-element.68), channel_id=1, source_target_pairs={{0,12},{1,13},{2,14},{3,15},{4,0},{5,1},{6,2},{7,3},{8,4},{9,5},{1... | collective-permute-start | bytes 1179656 | tf_op jit(solution)/shard_map/ppermute | solution.py:335
  118.1 38.5 %collective-permute-start.10 = (f32[2,3,128,128]{3,2,1,0:T(8,128)S(1)}, f32[2,3,128,128]{3,2,1,0:T(8,128)S(1)}, u32[]{:S(2)}, u32[]{:S(2)}) collective-permute-start(f32[2,3,128,128]{3,2,1,0:T(8,128)S(1)} %get-tuple-element.68), channel_id=1, source_target_pairs={{0,8},{1,9},{2,10},{3,11},{4,12},{5,13},{6,14},{7,15},{8,0},{9,1},... | collective-permute-start | bytes 1179656 | tf_op jit(solution)/shard_map/ppermute | solution.py:335
  121.9 34.7 %collective-permute-start.9 = (f32[2,3,128,128]{3,2,1,0:T(8,128)S(1)}, f32[2,3,128,128]{3,2,1,0:T(8,128)S(1)}, u32[]{:S(2)}, u32[]{:S(2)}) collective-permute-start(f32[2,3,128,128]{3,2,1,0:T(8,128)S(1)} %get-tuple-element.68), channel_id=1, source_target_pairs={{0,4},{1,5},{2,6},{3,7},{4,8},{5,9},{6,10},{7,11},{8,12},{9,13},{1... | collective-permute-start | bytes 1179656 | tf_op jit(solution)/shard_map/ppermute | solution.py:335
  156.6 19.9 %collective-permute-start.14 = (f32[1536,128]{1,0:T(8,128)S(1)}, f32[1536,128]{1,0:T(8,128)S(1)}, u32[]{:S(2)}, u32[]{:S(2)}) collective-permute-start(f32[1536,128]{1,0:T(8,128)S(1)} %collective-permute-done.12), channel_id=1, source_target_pairs={{96,64},{112,80},{64,96},{80,112},{97,65},{113,81},{65,97},{81,113... | collective-permute-start | bytes 2359304 | tf_op jit(solution)/shard_map/ppermute | solution.py:284
  158.9 18.9 %copy-start.14 = (f32[4,2,3,128,128]{4,3,2,1,0:T(8,128)}, f32[4,2,3,128,128]{4,3,2,1,0:T(8,128)S(1)}, u32[]{:S(2)}) copy-start(f32[4,2,3,128,128]{4,3,2,1,0:T(8,128)S(1)} %pad_maximum_fusion.1.mine) | copy-start | bytes 4718596
  158.9 25.3 %collective-permute-start.16 = (f32[4,2,3,128,128]{4,3,2,1,0:T(8,128)S(1)}, f32[4,2,3,128,128]{4,3,2,1,0:T(8,128)S(1)}, u32[]{:S(2)}, u32[]{:S(2)}) collective-permute-start(f32[4,2,3,128,128]{4,3,2,1,0:T(8,128)S(1)} %pad_maximum_fusion.1.mine), channel_id=1, source_target_pairs={{0,16},{16,0},{32,48},{48,32},{64,80},{80,64},{96,112},{112,96},{1... | collective-permute-start | bytes 4718600 | tf_op jit(solution)/shard_map/ppermute | solution.py:296
  177.9 2.0 copy-start.2
  178.0 5.0 %copy-start.15 = (f32[2,1536,128]{2,1,0:T(8,128)}, f32[2,1536,128]{2,1,0:T(8,128)S(1)}, u32[]{:S(2)}) copy-start(f32[2,1536,128]{2,1,0:T(8,128)S(1)} %pad_maximum_fusion.mine) | copy-start | bytes 4718596
  178.0 7.4 %copy-start.12 = (s32[4,48]{1,0:T(4,128)S(1)}, s32[4,48]{1,0:T(4,128)}, u32[]{:S(2)}) copy-start(s32[4,48]{1,0:T(4,128)} %lower_fill.3) | copy-start | bytes 2308
  178.0 7.4 %copy-start.13 = (s32[4,48]{1,0:T(4,128)S(1)}, s32[4,48]{1,0:T(4,128)}, u32[]{:S(2)}) copy-start(s32[4,48]{1,0:T(4,128)} %upper_fill.3) | copy-start | bytes 2308
  178.0 13.2 %collective-permute-start.15 = (f32[2,1536,128]{2,1,0:T(8,128)S(1)}, f32[2,1536,128]{2,1,0:T(8,128)}, u32[]{:S(2)}, u32[]{:S(2)}) collective-permute-start(f32[2,1536,128]{2,1,0:T(8,128)S(1)} %pad_maximum_fusion.mine), channel_id=1, source_target_pairs={{0,16},{16,0},{32,48},{48,32},{64,80},{80,64},{96,112},{112,96},{1... | collective-permute-start | bytes 4718600 | tf_op jit(solution)/shard_map/ppermute | solution.py:296
  183.0 1.2 copy-start.9
  184.2 1.1 copy-start.16
Sparse Core Ops, SparseCore 0:
  23.3 5.2 sort.26.cloned.1.call-done
  71.6 85.5 all-gather.1
  (1 shorter events, 0.0 us)

commit v4 on v3

--- a/solution.py
+++ b/solution.py
@@ -7,7 +7,8 @@
 
 VMEM = pl.BlockSpec(memory_space=pltpu.VMEM)
 SMEM = pl.BlockSpec(memory_space=pltpu.SMEM)
-PARAMS = pltpu.CompilerParams(vmem_limit_bytes=50 * 1024 * 1024)
+PARAMS = pltpu.CompilerParams(vmem_limit_bytes=14 * 1024 * 1024)
+LARGE = pltpu.CompilerParams(vmem_limit_bytes=40 * 1024 * 1024)
 BF = jnp.bfloat16
 
 
@@ -177,7 +178,7 @@
     return block(LEFT[k] // 256 + m)
 
 
-def corner_kernel(place, lower_fill, upper_fill, mine, other, inv, vh, vl, ih, il, wh, wl):
+def corner_factors(place, lower_fill, upper_fill, mine, other, inv, vh, vl, wh, wl, ih, il):
     here_x, core = place[0], place[2]
 
     def corner(b, k):
@@ -208,14 +209,22 @@
             vh[:, right(k, j)], vl[:, right(k, j)] = split(t)
 
 
+def scale_kernel(panels, inv, out):
+    for k in range(4):
+        out[:, block(k)] = dot3(split(pair(panels, (0, k), 384)), split(inv[k]))
+
+
 def update_kernel(
-    place, lower_fill, upper_fill, panels, p0, p1, p2, mine, other, vh, vl, ih, il, wh, wl,
-    out, acc, lh, ll, uh, ul
+    place, lower_fill, upper_fill, scaled, p0, p1, p2, mine, other, mine_c, other_c, inv,
+    out, acc, lh, ll, uh, ul, vh, vl, wh, wl, ih, il
 ):
     core, here_col, here_row = place[2], place[3], place[4]
 
     @pl.when(pl.program_id(0) == 0)
     def _():
+        corner_factors(
+            place, lower_fill, upper_fill, mine_c, other_c, inv, vh, vl, wh, wl, ih, il
+        )
         for k in range(4):
             before = slice(0, 256 * k)
             lefts = slice(LEFT[k], LEFT[k] + 256 * k)
@@ -242,17 +251,16 @@
 
     blocks = [g * 8 + here_row for g in range(6)]
     for k in range(4):
-        acc[:, block(k)] = dot3(split(pair(panels, (0, k), 384)), (ih[k], il[k]))
-    for k in range(4):
         keep = [((b > k) & (lower_fill[k, b] == 1)).astype(jnp.float32) for b in blocks]
-        t = acc[:, block(k)] * per_row(keep)
+        t = (acc if k else scaled)[:, block(k)] * per_row(keep)
         acc[:, block(k)] = t
         high, low = split(t)
         lh[:, block(k)], ll[:, block(k)] = high, low
         if k < 3:
             after = slice(256 * k + 256, 1024)
             rights = slice(RIGHT[k], RIGHT[k + 1])
-            acc[:, after] -= dot3((high, low), (vh[:, rights], vl[:, rights]))
+            t = dot3((high, low), (vh[:, rights], vl[:, rights]))
+            acc[:, after] = (acc if k else scaled)[:, after] - t
     done = (here_col < 4) & (per_row(blocks) > here_col)
     own = pl.ds(pl.multiple_of(jnp.minimum(here_col, 3) * 256, 256), 256)
     for c in range(3):
@@ -321,9 +329,9 @@
     all_keys = lax.sort(keys(targets.transpose(1, 0, 2).reshape(8, 1536)), dimension=1)
     places = lax.dynamic_slice(all_keys, (0, here_row * 192), (8, 192)).reshape(1536) % 2048
     backward = lax.sort(places * 2048 + local) % 2048
-    backward, s1 = lax.optimization_barrier((backward, s1))
+    p0 = place_rows(backward, g0)
+    p0, s1 = lax.optimization_barrier((p0, s1))
     g1, g2 = [a2a(s).reshape(1536, 2, 128) for s in (s1, s2)]
-    p0 = place_rows(backward, g0)
     parts0 = p0.reshape(6, 4, 128, 128)
     got, g1 = lax.optimization_barrier((scatter_x([parts0[:, i] for i in range(4)]), g1))
     quarter = scattered(parts0[:, 0], got, here_x)
@@ -346,43 +354,46 @@
     hops, g2 = lax.optimization_barrier((first_hops(corner), g2))
     corner = spread_z(corner, hops, here_z)
     top = top_rows(backward[:256], p0, p1, g2).reshape(1536, 128)
-    far, hops = lax.optimization_barrier((shifts(corner, along_x), first_hops(top)))
+    corner, top = lax.optimization_barrier((corner, top))
+    rows = with_other(spread_z(top, first_hops(top), here_z))
+    p2 = place_rows(backward, g2)
+    corner, panels, p2 = lax.optimization_barrier((corner, panels, p2))
+    scaled = pl.pallas_call(
+        scale_kernel,
+        out_shape=f32(1536, 1024),
+        grid=(4,),
+        in_specs=[pl.BlockSpec((1, 4, 768, 128), lambda i: (i, 0, 0, 0)), whole(4, 256, 256)],
+        out_specs=pl.BlockSpec((384, 1024), lambda i: (i, 0)),
+        compiler_params=PARAMS,
+        name="scale",
+    )(panels, inverses)
+    far, scaled = lax.optimization_barrier((shifts(corner, along_x), scaled))
     corner = with_other(jnp.stack([corner] + far))
-    p2 = place_rows(backward, g2)
-    rows = with_other(spread_z(top, hops, here_z))
-    parts = pl.pallas_call(
-        corner_kernel,
-        out_shape=[b16(256, 1536)] * 2 + [b16(4, 256, 256)] * 2 + [b16(256, 1536)] * 2,
-        in_specs=[SMEM] * 3 + [VMEM] * 3,
-        out_specs=[VMEM] * 6,
-        compiler_params=PARAMS,
-        name="corner",
-    )(place, lower_fill, upper_fill, *corner, inverses)
     part = lambda n: pl.BlockSpec((6, 1, n, 128), lambda i: (0, i, 0, 0))
     out = pl.pallas_call(
         update_kernel,
         out_shape=f32(6, 4, 384, 128),
         grid=(4,),
         in_specs=[SMEM] * 3
-        + [pl.BlockSpec((1, 4, 768, 128), lambda i: (i, 0, 0, 0))]
+        + [pl.BlockSpec((384, 1024), lambda i: (i, 0))]
         + [part(128)] * 3
         + [whole(2, 1536, 128)] * 2
-        + [whole(256, 1536)] * 2
-        + [whole(4, 256, 256)] * 2
-        + [whole(256, 1536)] * 2,
+        + [whole(4, 2, 3, 128, 128)] * 2
+        + [whole(4, 256, 256)],
         out_specs=part(384),
         scratch_shapes=[
             pltpu.VMEM((384, 1024), jnp.float32),
             pltpu.VMEM((384, 1024), BF),
             pltpu.VMEM((384, 1024), BF),
-            pltpu.VMEM((1024, 768), BF),
-            pltpu.VMEM((1024, 768), BF),
-        ],
-        compiler_params=PARAMS,
+        ]
+        + [pltpu.VMEM((1024, 768), BF)] * 2
+        + [pltpu.VMEM((256, 1536), BF)] * 4
+        + [pltpu.VMEM((4, 256, 256), BF)] * 2,
+        compiler_params=LARGE,
         name="update",
     )(
-        place, lower_fill, upper_fill, panels,
-        *[p.reshape(6, 4, 128, 128) for p in (p0, p1, p2)], *rows, *parts
+        place, lower_fill, upper_fill, scaled,
+        *[p.reshape(6, 4, 128, 128) for p in (p0, p1, p2)], *rows, *corner, inverses
     )
     return out.reshape(6, 1, 256, 3, 1, 256)
 

time: 225 us -> 205 us (0.911)
  the two profiles are of different devices: /device:TPU:90 before, /device:TPU:1 now
where the time goes in v4:
time: 205 us; the launch traced here: 202 us
  starting transfers between devices  58.1 us (28%)
  Pallas kernels  51.6 us (25%)
  waiting for transfers between devices  47.9 us (23%)
  local copies, waits for them, and re-layouts  18.4 us (9%)
  between operations  13.6 us (7%)
  other arithmetic  11.9 us (6%)
    pallas_call x1, Pallas kernels, body(): pl.pallas_call(update_kernel, out_shape=f32(6, 4, 384, 128), grid=(4,), i...  25.3 us
    ppermute x6, starting transfers between devices, hop_z(): lax.ppermute(value, 'prow', [(2 * a + c, 2 * b + c) for a, b in pairs for...  19.8 us
    all_to_all x3, starting transfers between devices, body(): lax.all_to_all(s.reshape(8, -1, 128), 'prow', 0, 0, tiled=True)  16.6 us
    ppermute x6, waiting for transfers between devices, hop_z(): lax.ppermute(value, 'prow', [(2 * a + c, 2 * b + c) for a, b in pairs for...  15.7 us
    unnamed x33, local copies, waits for them, and re-layouts  14.8 us
    ppermute x3, waiting for transfers between devices, scatter_x(): lax.ppermute(blocks[s], 'pcol', [(k, k + 4 * s) for k in range(4)])  14.1 us
    pallas_call x3, Pallas kernels, place_rows(): pl.pallas_call(place_kernel, out_shape=f32(*arrived.shape), in_specs=[SME...  9.48 us
    ppermute x3, starting transfers between devices, scatter_x(): lax.ppermute(blocks[s], 'pcol', [(k, k + 4 * s) for k in range(4)])  9.33 us
  transfers between devices with their start and end apart: 21, of which 9 were waited for; matrix products, arithmetic and copies ran while one was open for 6% of the time, Pallas kernels for 9%

profile of v4, /device:TPU:1, one launch (start us, length us, event | category | flops | bytes accessed | tf_op | source)
XLA Modules:
  0.0 201.5 jit_solution(6529190630278206385)
XLA Ops:
  7.4 2.3 %copy-done.1 = f32[6,1,256,3,1,256]{5,4,3,2,1,0:T(1,128)S(1)} copy-done((f32[6,1,256,3,1,256]{5,4,3,2,1,0:T(1,128)S(1)}, f32[6,1,256,3,1,256]{5,4,3,2,1,0:T(1,128)}, u32[]{:S(2)}) %copy-start.1) | copy-done | bytes 4718616
  9.7 5.9 %send_first.1 = (f32[1536,2,128]{2,1,0:T(2,128)}, s32[12,128]{1,0:T(8,128)S(1)}) custom-call(s32[12,128]{1,0:T(8,128)S(1)} %reshape.58.targets, f32[4608,2,128]{2,1,0:T(2,128)S(1)} %bitcast.58), custom_call_target="tpu_custom_call" | custom-call | tf_op jit(solution)/shard_map/send_first/pallas_call | solution.py:66
  15.7 6.8 %all-to-all-start = ((f32[8,384,128]{2,1,0:T(8,128)}), f32[8,384,128]{2,1,0:T(8,128)S(1)}, u32[]{:S(2)}, u32[]{:S(2)}) async-start(f32[8,384,128]{2,1,0:T(8,128)} %bitcast.9), calls=%async_computation | async-start | bytes 3145728 | tf_op jit(solution)/shard_map/all_to_all | solution.py:327
  23.2 2.3 %copy-done.2 = f32[6,1,256,3,1,256]{5,4,3,2,1,0:T(1,128)S(1)} copy-done((f32[6,1,256,3,1,256]{5,4,3,2,1,0:T(1,128)S(1)}, f32[6,1,256,3,1,256]{5,4,3,2,1,0:T(1,128)}, u32[]{:S(2)}) %copy-start.2) | copy-done | bytes 4718616
  25.6 5.0 %send_rest.1 = (f32[1536,2,128]{2,1,0:T(2,128)S(1)}, f32[1536,2,128]{2,1,0:T(2,128)S(1)}) custom-call(s32[12,128]{1,0:T(8,128)S(1)} %get-tuple-element.33.slots, f32[4608,2,128]{2,1,0:T(2,128)S(1)} %bitcast.59), custom_call_target="tpu_custom_call" | custom-call | tf_op jit(solution)/shard_map/send_rest/pallas_call | solution.py:98
  30.6 1.2 copy-done.12
  31.7 1.2 copy-done.13
  33.8 5.0 %sort.22 = (s32[1536]{0:T(1024)S(1)}, s32[1536]{0:T(1024)}) sort(s32[1536]{0:T(1024)S(1)} %fusion.15, s32[1536]{0:T(1024)S(1)} %iota.10), dimensions={0}, to_apply=%region_1.2 | sort | flops 16896 | bytes 24576 | tf_op jit(solution)/shard_map/sort | solution.py:331
  38.9 4.4 %all-to-all-done = f32[8,384,128]{2,1,0:T(8,128)S(1)} async-done(((f32[8,384,128]{2,1,0:T(8,128)}), f32[8,384,128]{2,1,0:T(8,128)S(1)}, u32[]{:S(2)}, u32[]{:S(2)}) %all-to-all-start) | async-done | bytes 1572896 | tf_op jit(solution)/shard_map/all_to_all | solution.py:327
  43.2 3.2 %place_rows.3.p0 = f32[1536,2,128]{2,1,0:T(2,128)S(1)} custom-call(s32[1536]{0:T(1024)S(1)} %add_select_fusion.4.order, f32[1536,2,128]{2,1,0:T(2,128)S(1)} %bitcast.64), custom_call_target="tpu_custom_call" | custom-call | tf_op jit(solution)/shard_map/place_rows/pallas_call | solution.py:142
  46.4 4.4 %all-to-all-start.1 = ((f32[8,384,128]{2,1,0:T(8,128)}), f32[8,384,128]{2,1,0:T(8,128)S(1)}, u32[]{:S(2)}, u32[]{:S(2)}) async-start(f32[8,384,128]{2,1,0:T(8,128)} %bitcast.68), calls=%async_computation.1 | async-start | bytes 3145728 | tf_op jit(solution)/shard_map/all_to_all | solution.py:327
  50.7 0.9 slice_bitcast_fusion
  51.7 5.2 %collective-permute-start.2 = (f32[6,128,128]{2,1,0:T(8,128)}, f32[6,128,128]{2,1,0:T(8,128)}, u32[]{:S(2)}, u32[]{:S(2)}) collective-permute-start(f32[6,128,128]{2,1,0:T(8,128)} %get-tuple-element.58), channel_id=1, source_target_pairs={{0,12},{1,13},{2,14},{3,15},{16,28},{17,29},{18,30},{19,31},{32,44... | collective-permute-start | bytes 1179656 | tf_op jit(solution)/shard_map/ppermute | solution.py:283
  56.9 2.1 %collective-permute-start = (f32[6,128,128]{2,1,0:T(8,128)}, f32[6,128,128]{2,1,0:T(8,128)}, u32[]{:S(2)}, u32[]{:S(2)}) collective-permute-start(f32[6,128,128]{2,1,0:T(8,128)} %get-tuple-element.59), channel_id=1, source_target_pairs={{0,4},{1,5},{2,6},{3,7},{16,20},{17,21},{18,22},{19,23},{32,36},{3... | collective-permute-start | bytes 1179656 | tf_op jit(solution)/shard_map/ppermute | solution.py:283
  58.9 2.1 %collective-permute-start.1 = (f32[6,128,128]{2,1,0:T(8,128)S(1)}, f32[6,128,128]{2,1,0:T(8,128)}, u32[]{:S(2)}, u32[]{:S(2)}) collective-permute-start(f32[6,128,128]{2,1,0:T(8,128)S(1)} %get-tuple-element.60), channel_id=1, source_target_pairs={{0,8},{1,9},{2,10},{3,11},{16,24},{17,25},{18,26},{19,27},{32,40},... | collective-permute-start | bytes 1179656 | tf_op jit(solution)/shard_map/ppermute | solution.py:283
  61.0 3.7 %collective-permute-done.2 = f32[6,128,128]{2,1,0:T(8,128)} collective-permute-done((f32[6,128,128]{2,1,0:T(8,128)}, f32[6,128,128]{2,1,0:T(8,128)}, u32[]{:S(2)}, u32[]{:S(2)}) %collective-permute-start.2) | collective-permute-done | bytes 393248 | tf_op jit(solution)/shard_map/ppermute | solution.py:283
  64.7 2.1 %collective-permute-done = f32[6,128,128]{2,1,0:T(8,128)} collective-permute-done((f32[6,128,128]{2,1,0:T(8,128)}, f32[6,128,128]{2,1,0:T(8,128)}, u32[]{:S(2)}, u32[]{:S(2)}) %collective-permute-start) | collective-permute-done | bytes 393248 | tf_op jit(solution)/shard_map/ppermute | solution.py:283
  66.8 8.3 %collective-permute-done.1 = f32[6,128,128]{2,1,0:T(8,128)} collective-permute-done((f32[6,128,128]{2,1,0:T(8,128)S(1)}, f32[6,128,128]{2,1,0:T(8,128)}, u32[]{:S(2)}, u32[]{:S(2)}) %collective-permute-start.1) | collective-permute-done | bytes 393248 | tf_op jit(solution)/shard_map/ppermute | solution.py:283
  75.1 2.6 %fusion = f32[6,128,128]{2,1,0:T(8,128)} fusion(f32[6,4,128,128]{3,2,1,0:T(8,128)S(1)} %bitcast.56, f32[6,128,128]{2,1,0:T(8,128)} %collective-permute-done.2, f32[6,128,128]{2,1,0:T(8,128)} %collective-permute-done, f32[6,128,128]{2,1,0:T(8,128)} %collective-permute-done.1, pred[]{:T(512)S(6)} %eq.33), kind=kLoop, calls=%fused_computation.8 | loop fusion | flops 294912 | bytes 1966081 | tf_op jit(solution)/shard_map/jit(_where)/select_n | solution.py:288
  77.8 5.4 %all-to-all-start.2 = ((f32[8,384,128]{2,1,0:T(8,128)}), f32[8,384,128]{2,1,0:T(8,128)S(1)}, u32[]{:S(2)}, u32[]{:S(2)}) async-start(f32[8,384,128]{2,1,0:T(8,128)} %bitcast.67), calls=%async_computation.2 | async-start | bytes 3145728 | tf_op jit(solution)/shard_map/all_to_all | solution.py:327
  84.1 2.8 %collective-permute-start.5 = (f32[128,128]{1,0:T(8,128)S(1)}, f32[128,128]{1,0:T(8,128)S(1)}, u32[]{:S(2)}, u32[]{:S(2)}) collective-permute-start(f32[128,128]{1,0:T(8,128)S(1)} %get-tuple-element.64), channel_id=1, source_target_pairs={{0,3},{1,0},{2,1},{3,2},{4,7},{5,4},{6,5},{7,6},{8,11},{9,8},{10,9... | collective-permute-start | bytes 196616 | tf_op jit(solution)/shard_map/ppermute | solution.py:343
  88.0 1.4 copy-done.7
  89.4 3.2 %place_rows.4.p1 = f32[1536,2,128]{2,1,0:T(2,128)S(1)} custom-call(s32[1536]{0:T(1024)S(1)} %add_select_fusion.4.order, f32[1536,2,128]{2,1,0:T(2,128)S(1)} %bitcast.63), custom_call_target="tpu_custom_call" | custom-call | tf_op jit(solution)/shard_map/place_rows/pallas_call | solution.py:142
  92.6 1.1 copy-done.3
  94.4 3.3 %collective-permute-start.7 = (f32[3,128,128]{2,1,0:T(8,128)S(1)}, f32[3,128,128]{2,1,0:T(8,128)S(1)}, u32[]{:S(2)}, u32[]{:S(2)}) collective-permute-start(f32[3,128,128]{2,1,0:T(8,128)S(1)} %corner_rows.1), channel_id=1, source_target_pairs={{0,32},{16,48},{32,0},{48,16},{1,33},{17,49},{33,1},{49,17},{2,34}... | collective-permute-start | bytes 589832 | tf_op jit(solution)/shard_map/ppermute | solution.py:292
  97.7 2.6 %collective-permute-start.6 = (f32[3,128,128]{2,1,0:T(8,128)S(1)}, f32[3,128,128]{2,1,0:T(8,128)}, u32[]{:S(2)}, u32[]{:S(2)}) collective-permute-start(f32[3,128,128]{2,1,0:T(8,128)S(1)} %corner_rows.1), channel_id=1, source_target_pairs={{0,96},{16,112},{32,64},{48,80},{1,97},{17,113},{33,65},{49,81},{2... | collective-permute-start | bytes 589832 | tf_op jit(solution)/shard_map/ppermute | solution.py:292
  100.2 3.7 %all-to-all-done.2 = f32[8,384,128]{2,1,0:T(8,128)S(1)} async-done(((f32[8,384,128]{2,1,0:T(8,128)}), f32[8,384,128]{2,1,0:T(8,128)S(1)}, u32[]{:S(2)}, u32[]{:S(2)}) %all-to-all-start.2) | async-done | bytes 1572896 | tf_op jit(solution)/shard_map/all_to_all | solution.py:327
  104.0 2.7 %collective-permute-done.7 = f32[3,128,128]{2,1,0:T(8,128)S(1)} collective-permute-done((f32[3,128,128]{2,1,0:T(8,128)S(1)}, f32[3,128,128]{2,1,0:T(8,128)S(1)}, u32[]{:S(2)}, u32[]{:S(2)}) %collective-permute-start.7) | collective-permute-done | bytes 196640 | tf_op jit(solution)/shard_map/ppermute | solution.py:292
  106.7 1.4 collective-permute-start.8
  108.1 1.4 copy-done.4
  109.5 1.9 top_rows.1
  111.4 1.1 select_bitcast_fusion.3
  112.5 9.1 %collective-permute-start.13 = (f32[1536,128]{1,0:T(8,128)}, f32[1536,128]{1,0:T(8,128)}, u32[]{:S(2)}, u32[]{:S(2)}) collective-permute-start(f32[1536,128]{1,0:T(8,128)} %bitcast.26), channel_id=1, source_target_pairs={{0,96},{16,112},{32,64},{48,80},{1,97},{17,113},{33,65},{49,81},{2... | collective-permute-start | bytes 2359304 | tf_op jit(solution)/shard_map/ppermute | solution.py:292
  121.6 1.9 collective-permute-start.12
  123.5 12.9 %collective-permute-done.13 = f32[1536,128]{1,0:T(8,128)} collective-permute-done((f32[1536,128]{1,0:T(8,128)}, f32[1536,128]{1,0:T(8,128)}, u32[]{:S(2)}, u32[]{:S(2)}) %collective-permute-start.13) | collective-permute-done | bytes 786464 | tf_op jit(solution)/shard_map/ppermute | solution.py:292
  136.5 1.5 collective-permute-start.14
  138.0 3.2 %place_rows.5 = f32[1536,2,128]{2,1,0:T(2,128)S(1)} custom-call(s32[1536]{0:T(1024)S(1)} %add_select_fusion.4.order, f32[1536,2,128]{2,1,0:T(2,128)S(1)} %bitcast.61), custom_call_target="tpu_custom_call" | custom-call | tf_op jit(solution)/shard_map/place_rows/pallas_call | solution.py:142
  141.2 1.2 copy-done.9
  142.3 2.1 %collective-permute-start.11 = (f32[2,3,128,128]{3,2,1,0:T(8,128)S(1)}, f32[2,3,128,128]{3,2,1,0:T(8,128)S(1)}, u32[]{:S(2)}, u32[]{:S(2)}) collective-permute-start(f32[2,3,128,128]{3,2,1,0:T(8,128)S(1)} %pad_maximum_fusion.2), channel_id=1, source_target_pairs={{0,12},{1,13},{2,14},{3,15},{4,0},{5,1},{6,2},{7,3},{8,4},{9,5},{1... | collective-permute-start | bytes 1179656 | tf_op jit(solution)/shard_map/ppermute | solution.py:343
  144.5 1.5 collective-permute-start.10
  146.0 0.9 collective-permute-start.9
  146.9 2.2 %select_bitcast_fusion.1 = (f32[1,1536,128]{2,1,0:T(8,128)S(1)}, f32[1,1536,128]{2,1,0:T(8,128)S(1)}) fusion(f32[1536,128]{1,0:T(8,128)} %bitcast.26, f32[1536,128]{1,0:T(8,128)} %collective-permute-done.12, f32[1536,128]{1,0:T(8,128)} %collective-permute-done.14, f32[1536,128]{1,0:T(8,128)} %collective-permute-done.13, pred[]{:T(512)S(6)} %eq.35, ...), kind=kLoop, calls=%fused_computation.3 | loop fusion | flops 1179648 | bytes 4718596 | tf_op jit(solution)/shard_map/stack | solution.py:300
  149.2 3.3 %collective-permute-start.15 = (f32[2,1536,128]{2,1,0:T(8,128)S(1)}, f32[2,1536,128]{2,1,0:T(8,128)S(1)}, u32[]{:S(2)}, u32[]{:S(2)}) collective-permute-start(f32[2,1536,128]{2,1,0:T(8,128)S(1)} %pad_maximum_fusion.mine), channel_id=1, source_target_pairs={{0,16},{16,0},{32,48},{48,32},{64,80},{80,64},{96,112},{112,96},{1... | collective-permute-start | bytes 4718600 | tf_op jit(solution)/shard_map/ppermute | solution.py:304
  152.4 3.3 %scale.1.scaled = f32[1536,1024]{1,0:T(8,128)S(1)} custom-call(f32[4,4,768,128]{3,2,1,0:T(8,128)S(1)} %bitcast.65, f32[4,256,256]{2,1,0:T(8,128)S(1)} %copy-done.11), custom_call_target="tpu_custom_call" | custom-call | tf_op jit(solution)/shard_map/scale/pallas_call | solution.py:361
  155.8 2.6 %copy-done = f32[1536,1024]{1,0:T(8,128)} copy-done((f32[1536,1024]{1,0:T(8,128)}, f32[1536,1024]{1,0:T(8,128)S(1)}, u32[]{:S(2)}) %copy-start) | copy-done | bytes 6291480
  158.4 7.0 %collective-permute-done.9 = f32[2,3,128,128]{3,2,1,0:T(8,128)S(1)} collective-permute-done((f32[2,3,128,128]{3,2,1,0:T(8,128)S(1)}, f32[2,3,128,128]{3,2,1,0:T(8,128)S(1)}, u32[]{:S(2)}, u32[]{:S(2)}) %collective-permute-start.9) | collective-permute-done | bytes 393248 | tf_op jit(solution)/shard_map/ppermute | solution.py:343
  166.3 3.0 %collective-permute-done.16.other_c = f32[4,2,3,128,128]{4,3,2,1,0:T(8,128)S(1)} collective-permute-done((f32[4,2,3,128,128]{4,3,2,1,0:T(8,128)S(1)}, f32[4,2,3,128,128]{4,3,2,1,0:T(8,128)S(1)}, u32[]{:S(2)}, u32[]{:S(2)}) %collective-permute-start.16) | collective-permute-done | bytes 1572896 | tf_op jit(solution)/shard_map/ppermute | solution.py:304
  169.3 25.3 %update.1 = f32[6,4,384,128]{3,2,1,0:T(8,128)} custom-call(s32[5]{0:T(128)S(1)} %stack.68.place, s32[4,48]{1,0:T(4,128)S(1)} %copy-done.14, s32[4,48]{1,0:T(4,128)S(1)} %copy-done.15, f32[1536,1024]{1,0:T(8,128)} %copy-done, f32[6,4,128,128]{3,2,1,0:T(8,128)S(1)} %bitcast.57, f32[6,4,128,128]{3,2,1,0:T(8,128)S(1)} %bitcast.62, ...), custom_call_target="tpu_custom_call" | custom-call | tf_op jit(solution)/shard_map/update/pallas_call | solution.py:373
  (60 shorter events, 6.1 us)
Async XLA Ops:
  7.4 2.3 %copy-start.1 = (f32[6,1,256,3,1,256]{5,4,3,2,1,0:T(1,128)S(1)}, f32[6,1,256,3,1,256]{5,4,3,2,1,0:T(1,128)}, u32[]{:S(2)}) copy-start(f32[6,1,256,3,1,256]{5,4,3,2,1,0:T(1,128)} %param.5) | copy-start | bytes 14155780
  15.7 27.5 %all-to-all-start = ((f32[8,384,128]{2,1,0:T(8,128)}), f32[8,384,128]{2,1,0:T(8,128)S(1)}, u32[]{:S(2)}, u32[]{:S(2)}) async-start(f32[8,384,128]{2,1,0:T(8,128)} %bitcast.9), calls=%async_computation | async-start | bytes 3145728 | tf_op jit(solution)/shard_map/all_to_all | solution.py:327
  22.5 10.4 %sort.24.cloned.1.call-start = ((), (), s32[]{:S(2)}) async-start(), calls=%async_computation.4 | async-start | bytes 147488 | tf_op jit(solution)/shard_map/sort | solution.py:329
  23.2 2.3 %copy-start.2 = (f32[6,1,256,3,1,256]{5,4,3,2,1,0:T(1,128)S(1)}, f32[6,1,256,3,1,256]{5,4,3,2,1,0:T(1,128)}, u32[]{:S(2)}) copy-start(f32[6,1,256,3,1,256]{5,4,3,2,1,0:T(1,128)} %param.5) | copy-start | bytes 14155780
  30.6 1.2 copy-start.12
  31.7 1.2 copy-start.13
  46.4 28.8 %all-to-all-start.1 = ((f32[8,384,128]{2,1,0:T(8,128)}), f32[8,384,128]{2,1,0:T(8,128)S(1)}, u32[]{:S(2)}, u32[]{:S(2)}) async-start(f32[8,384,128]{2,1,0:T(8,128)} %bitcast.68), calls=%async_computation.1 | async-start | bytes 3145728 | tf_op jit(solution)/shard_map/all_to_all | solution.py:327
  50.7 91.6 %all-gather.2.cloned.1.call-start = ((), (), s32[]{:S(2)}) async-start(), calls=%async_computation.3 | async-start | bytes 6684672 | tf_op jit(solution)/shard_map/all_gather | solution.py:338
  51.7 13.0 %collective-permute-start.2 = (f32[6,128,128]{2,1,0:T(8,128)}, f32[6,128,128]{2,1,0:T(8,128)}, u32[]{:S(2)}, u32[]{:S(2)}) collective-permute-start(f32[6,128,128]{2,1,0:T(8,128)} %get-tuple-element.58), channel_id=1, source_target_pairs={{0,12},{1,13},{2,14},{3,15},{16,28},{17,29},{18,30},{19,31},{32,44... | collective-permute-start | bytes 1179656 | tf_op jit(solution)/shard_map/ppermute | solution.py:283
  56.9 10.0 %collective-permute-start = (f32[6,128,128]{2,1,0:T(8,128)}, f32[6,128,128]{2,1,0:T(8,128)}, u32[]{:S(2)}, u32[]{:S(2)}) collective-permute-start(f32[6,128,128]{2,1,0:T(8,128)} %get-tuple-element.59), channel_id=1, source_target_pairs={{0,4},{1,5},{2,6},{3,7},{16,20},{17,21},{18,22},{19,23},{32,36},{3... | collective-permute-start | bytes 1179656 | tf_op jit(solution)/shard_map/ppermute | solution.py:283
  58.9 16.2 %collective-permute-start.1 = (f32[6,128,128]{2,1,0:T(8,128)S(1)}, f32[6,128,128]{2,1,0:T(8,128)}, u32[]{:S(2)}, u32[]{:S(2)}) collective-permute-start(f32[6,128,128]{2,1,0:T(8,128)S(1)} %get-tuple-element.60), channel_id=1, source_target_pairs={{0,8},{1,9},{2,10},{3,11},{16,24},{17,25},{18,26},{19,27},{32,40},... | collective-permute-start | bytes 1179656 | tf_op jit(solution)/shard_map/ppermute | solution.py:283
  75.1 2.7 %copy-start.6 = (f32[8,384,128]{2,1,0:T(8,128)}, f32[8,384,128]{2,1,0:T(8,128)S(1)}, u32[]{:S(2)}) copy-start(f32[8,384,128]{2,1,0:T(8,128)S(1)} %all-to-all-done.1) | copy-start | bytes 4718596
  77.8 26.2 %all-to-all-start.2 = ((f32[8,384,128]{2,1,0:T(8,128)}), f32[8,384,128]{2,1,0:T(8,128)S(1)}, u32[]{:S(2)}, u32[]{:S(2)}) async-start(f32[8,384,128]{2,1,0:T(8,128)} %bitcast.67), calls=%async_computation.2 | async-start | bytes 3145728 | tf_op jit(solution)/shard_map/all_to_all | solution.py:327
  84.1 9.6 %collective-permute-start.5 = (f32[128,128]{1,0:T(8,128)S(1)}, f32[128,128]{1,0:T(8,128)S(1)}, u32[]{:S(2)}, u32[]{:S(2)}) collective-permute-start(f32[128,128]{1,0:T(8,128)S(1)} %get-tuple-element.64), channel_id=1, source_target_pairs={{0,3},{1,0},{2,1},{3,2},{4,7},{5,4},{6,5},{7,6},{8,11},{9,8},{10,9... | collective-permute-start | bytes 196616 | tf_op jit(solution)/shard_map/ppermute | solution.py:343
  86.9 6.9 %collective-permute-start.4 = (f32[128,128]{1,0:T(8,128)S(1)}, f32[128,128]{1,0:T(8,128)S(1)}, u32[]{:S(2)}, u32[]{:S(2)}) collective-permute-start(f32[128,128]{1,0:T(8,128)S(1)} %get-tuple-element.64), channel_id=1, source_target_pairs={{0,2},{1,3},{2,0},{3,1},{4,6},{5,7},{6,4},{7,5},{8,10},{9,11},{10,... | collective-permute-start | bytes 196616 | tf_op jit(solution)/shard_map/ppermute | solution.py:343
  87.2 6.5 %collective-permute-start.3 = (f32[128,128]{1,0:T(8,128)S(1)}, f32[128,128]{1,0:T(8,128)S(1)}, u32[]{:S(2)}, u32[]{:S(2)}) collective-permute-start(f32[128,128]{1,0:T(8,128)S(1)} %get-tuple-element.64), channel_id=1, source_target_pairs={{0,1},{1,2},{2,3},{3,0},{4,5},{5,6},{6,7},{7,4},{8,9},{9,10},{10,1... | collective-permute-start | bytes 196616 | tf_op jit(solution)/shard_map/ppermute | solution.py:343
  88.0 1.4 copy-start.7
  92.6 1.1 copy-start.3
  94.4 12.3 %collective-permute-start.7 = (f32[3,128,128]{2,1,0:T(8,128)S(1)}, f32[3,128,128]{2,1,0:T(8,128)S(1)}, u32[]{:S(2)}, u32[]{:S(2)}) collective-permute-start(f32[3,128,128]{2,1,0:T(8,128)S(1)} %corner_rows.1), channel_id=1, source_target_pairs={{0,32},{16,48},{32,0},{48,16},{1,33},{17,49},{33,1},{49,17},{2,34}... | collective-permute-start | bytes 589832 | tf_op jit(solution)/shard_map/ppermute | solution.py:292
  97.7 9.0 %collective-permute-start.6 = (f32[3,128,128]{2,1,0:T(8,128)S(1)}, f32[3,128,128]{2,1,0:T(8,128)}, u32[]{:S(2)}, u32[]{:S(2)}) collective-permute-start(f32[3,128,128]{2,1,0:T(8,128)S(1)} %corner_rows.1), channel_id=1, source_target_pairs={{0,96},{16,112},{32,64},{48,80},{1,97},{17,113},{33,65},{49,81},{2... | collective-permute-start | bytes 589832 | tf_op jit(solution)/shard_map/ppermute | solution.py:292
  106.7 4.7 %collective-permute-start.8 = (f32[3,128,128]{2,1,0:T(8,128)}, f32[3,128,128]{2,1,0:T(8,128)}, u32[]{:S(2)}, u32[]{:S(2)}) collective-permute-start(f32[3,128,128]{2,1,0:T(8,128)} %collective-permute-done.6), channel_id=1, source_target_pairs={{96,64},{112,80},{64,96},{80,112},{97,65},{113,81},{65,97},{81,113... | collective-permute-start | bytes 589832 | tf_op jit(solution)/shard_map/ppermute | solution.py:292
  108.0 1.4 copy-start.4
  112.5 23.9 %collective-permute-start.13 = (f32[1536,128]{1,0:T(8,128)}, f32[1536,128]{1,0:T(8,128)}, u32[]{:S(2)}, u32[]{:S(2)}) collective-permute-start(f32[1536,128]{1,0:T(8,128)} %bitcast.26), channel_id=1, source_target_pairs={{0,96},{16,112},{32,64},{48,80},{1,97},{17,113},{33,65},{49,81},{2... | collective-permute-start | bytes 2359304 | tf_op jit(solution)/shard_map/ppermute | solution.py:292
  121.6 25.3 %collective-permute-start.12 = (f32[1536,128]{1,0:T(8,128)}, f32[1536,128]{1,0:T(8,128)}, u32[]{:S(2)}, u32[]{:S(2)}) collective-permute-start(f32[1536,128]{1,0:T(8,128)} %bitcast.26), channel_id=1, source_target_pairs={{0,32},{16,48},{32,0},{48,16},{1,33},{17,49},{33,1},{49,17},{2,34}... | collective-permute-start | bytes 2359304 | tf_op jit(solution)/shard_map/ppermute | solution.py:292
  136.5 10.4 %collective-permute-start.14 = (f32[1536,128]{1,0:T(8,128)}, f32[1536,128]{1,0:T(8,128)}, u32[]{:S(2)}, u32[]{:S(2)}) collective-permute-start(f32[1536,128]{1,0:T(8,128)} %collective-permute-done.13), channel_id=1, source_target_pairs={{96,64},{112,80},{64,96},{80,112},{97,65},{113,81},{65,97},{81,113... | collective-permute-start | bytes 2359304 | tf_op jit(solution)/shard_map/ppermute | solution.py:292
  141.2 1.2 copy-start.9
  142.3 16.1 %collective-permute-start.11 = (f32[2,3,128,128]{3,2,1,0:T(8,128)S(1)}, f32[2,3,128,128]{3,2,1,0:T(8,128)S(1)}, u32[]{:S(2)}, u32[]{:S(2)}) collective-permute-start(f32[2,3,128,128]{3,2,1,0:T(8,128)S(1)} %pad_maximum_fusion.2), channel_id=1, source_target_pairs={{0,12},{1,13},{2,14},{3,15},{4,0},{5,1},{6,2},{7,3},{8,4},{9,5},{1... | collective-permute-start | bytes 1179656 | tf_op jit(solution)/shard_map/ppermute | solution.py:343
  144.5 14.0 %collective-permute-start.10 = (f32[2,3,128,128]{3,2,1,0:T(8,128)S(1)}, f32[2,3,128,128]{3,2,1,0:T(8,128)S(1)}, u32[]{:S(2)}, u32[]{:S(2)}) collective-permute-start(f32[2,3,128,128]{3,2,1,0:T(8,128)S(1)} %pad_maximum_fusion.2), channel_id=1, source_target_pairs={{0,8},{1,9},{2,10},{3,11},{4,12},{5,13},{6,14},{7,15},{8,0},{9,1},... | collective-permute-start | bytes 1179656 | tf_op jit(solution)/shard_map/ppermute | solution.py:343
  146.0 19.4 %collective-permute-start.9 = (f32[2,3,128,128]{3,2,1,0:T(8,128)S(1)}, f32[2,3,128,128]{3,2,1,0:T(8,128)S(1)}, u32[]{:S(2)}, u32[]{:S(2)}) collective-permute-start(f32[2,3,128,128]{3,2,1,0:T(8,128)S(1)} %pad_maximum_fusion.2), channel_id=1, source_target_pairs={{0,4},{1,5},{2,6},{3,7},{4,8},{5,9},{6,10},{7,11},{8,12},{9,13},{1... | collective-permute-start | bytes 1179656 | tf_op jit(solution)/shard_map/ppermute | solution.py:343
  146.9 5.6 %copy-start.8 = (f32[12288,128]{1,0:T(8,128)S(1)}, f32[12288,128]{1,0:T(8,128)}, u32[]{:S(2)}) copy-start(f32[12288,128]{1,0:T(8,128)} %all-gather.2.cloned.1.call-done) | copy-start | bytes 18874372
  149.0 3.4 %copy-start.11 = (f32[4,256,256]{2,1,0:T(8,128)S(1)}, f32[4,256,256]{2,1,0:T(8,128)}, u32[]{:S(2)}) copy-start(f32[4,256,256]{2,1,0:T(8,128)} %inv.3) | copy-start | bytes 3145732
  149.2 17.1 %collective-permute-start.15 = (f32[2,1536,128]{2,1,0:T(8,128)S(1)}, f32[2,1536,128]{2,1,0:T(8,128)S(1)}, u32[]{:S(2)}, u32[]{:S(2)}) collective-permute-start(f32[2,1536,128]{2,1,0:T(8,128)S(1)} %pad_maximum_fusion.mine), channel_id=1, source_target_pairs={{0,16},{16,0},{32,48},{48,32},{64,80},{80,64},{96,112},{112,96},{1... | collective-permute-start | bytes 4718600 | tf_op jit(solution)/shard_map/ppermute | solution.py:304
  152.4 16.9 %copy-start.15 = (s32[4,48]{1,0:T(4,128)S(1)}, s32[4,48]{1,0:T(4,128)}, u32[]{:S(2)}) copy-start(s32[4,48]{1,0:T(4,128)} %upper_fill.1) | copy-start | bytes 2308
  155.8 2.6 %copy-start = (f32[1536,1024]{1,0:T(8,128)}, f32[1536,1024]{1,0:T(8,128)S(1)}, u32[]{:S(2)}) copy-start(f32[1536,1024]{1,0:T(8,128)S(1)} %scale.1.scaled) | copy-start | bytes 18874372
  165.4 3.9 %copy-start.5 = (f32[1536,2,128]{2,1,0:T(2,128)S(1)}, f32[1536,2,128]{2,1,0:T(2,128)}, u32[]{:S(2)}) copy-start(f32[1536,2,128]{2,1,0:T(2,128)} %copy-done.3) | copy-start | bytes 4718596
  165.4 3.9 %copy-start.10 = (f32[1536,2,128]{2,1,0:T(2,128)S(1)}, f32[1536,2,128]{2,1,0:T(2,128)}, u32[]{:S(2)}) copy-start(f32[1536,2,128]{2,1,0:T(2,128)} %copy-done.9) | copy-start | bytes 4718596
  165.4 3.9 %copy-start.14 = (s32[4,48]{1,0:T(4,128)S(1)}, s32[4,48]{1,0:T(4,128)}, u32[]{:S(2)}) copy-start(s32[4,48]{1,0:T(4,128)} %lower_fill.1) | copy-start | bytes 2308
  165.5 3.8 %collective-permute-start.16 = (f32[4,2,3,128,128]{4,3,2,1,0:T(8,128)S(1)}, f32[4,2,3,128,128]{4,3,2,1,0:T(8,128)S(1)}, u32[]{:S(2)}, u32[]{:S(2)}) collective-permute-start(f32[4,2,3,128,128]{4,3,2,1,0:T(8,128)S(1)} %pad_maximum_fusion.1.mine_c), channel_id=1, source_target_pairs={{0,16},{16,0},{32,48},{48,32},{64,80},{80,64},{96,112},{112,96},{1... | collective-permute-start | bytes 4718600 | tf_op jit(solution)/shard_map/ppermute | solution.py:304
Sparse Core Ops, SparseCore 0:
  25.8 5.2 sort.26.cloned.1.call-done
  77.9 64.0 all-gather.1
  (1 shorter events, 0.0 us)

commit v5 on v4

--- a/solution.py
+++ b/solution.py
@@ -216,23 +216,28 @@
 
 def update_kernel(
     place, lower_fill, upper_fill, scaled, p0, p1, p2, mine, other, mine_c, other_c, inv,
-    out, acc, lh, ll, uh, ul, vh, vl, wh, wl, ih, il
+    out, acc, lh, ll, uh, ul, vh, vl, wh, wl, ih, il, rows, sem
 ):
     core, here_col, here_row = place[2], place[3], place[4]
 
     @pl.when(pl.program_id(0) == 0)
     def _():
+        copies = [
+            pltpu.make_async_copy(mine, rows.at[:, core], sem.at[0]),
+            pltpu.make_async_copy(other, rows.at[:, 1 - core], sem.at[1]),
+        ]
+        for copy in copies:
+            copy.start()
         corner_factors(
             place, lower_fill, upper_fill, mine_c, other_c, inv, vh, vl, wh, wl, ih, il
         )
+        for copy in copies:
+            copy.wait()
         for k in range(4):
             before = slice(0, 256 * k)
             lefts = slice(LEFT[k], LEFT[k] + 256 * k)
             for c in range(3):
-                at, first = (k // 2,), 512 * c
-                t = jnp.where(
-                    core == k % 2, pair(mine, at, 256, first), pair(other, at, 256, first)
-                )
+                t = pair(rows, (k // 2, k % 2), 256, 512 * c)
                 if k:
                     t = t - dot3(
                         (wh[:, lefts], wl[:, lefts]), (uh[before, block(c)], ul[before, block(c)])
@@ -241,27 +246,20 @@
                 keep = ((j > k) & (upper_fill[k, j] == 1)).astype(jnp.float32)
                 uh[block(k), block(c)], ul[block(k), block(c)] = split(t * keep)
 
-    group = lax.broadcasted_iota(jnp.int32, (384, 1), 0) // 64
-
-    def per_row(values):
-        t = values[5]
-        for g in range(5):
-            t = jnp.where(group == g, values[g], t)
-        return t
-
     blocks = [g * 8 + here_row for g in range(6)]
     for k in range(4):
-        keep = [((b > k) & (lower_fill[k, b] == 1)).astype(jnp.float32) for b in blocks]
-        t = (acc if k else scaled)[:, block(k)] * per_row(keep)
-        acc[:, block(k)] = t
-        high, low = split(t)
-        lh[:, block(k)], ll[:, block(k)] = high, low
+        src = acc if k else scaled
+        for g, b in enumerate(blocks):
+            here = slice(64 * g, 64 * g + 64)
+            keep = ((b > k) & (lower_fill[k, b] == 1)).astype(jnp.float32)
+            t = src[here, block(k)] * keep
+            acc[here, block(k)] = t
+            lh[here, block(k)], ll[here, block(k)] = split(t)
         if k < 3:
             after = slice(256 * k + 256, 1024)
             rights = slice(RIGHT[k], RIGHT[k + 1])
-            t = dot3((high, low), (vh[:, rights], vl[:, rights]))
-            acc[:, after] = (acc if k else scaled)[:, after] - t
-    done = (here_col < 4) & (per_row(blocks) > here_col)
+            t = dot3((lh[:, block(k)], ll[:, block(k)]), (vh[:, rights], vl[:, rights]))
+            acc[:, after] = src[:, after] - t
     own = pl.ds(pl.multiple_of(jnp.minimum(here_col, 3) * 256, 256), 256)
     for c in range(3):
         t = dot3((lh[...], ll[...]), (uh[:, block(c)], ul[:, block(c)]))
@@ -269,7 +267,7 @@
             here = slice(64 * g, 64 * g + 64)
             new = pair((p0, p1, p2)[c], (g, 0), 64) - t[here]
             if c == 0:
-                new = jnp.where(done[here], acc[here, own], new)
+                new = jnp.where((here_col < 4) & (blocks[g] > here_col), acc[here, own], new)
             out[g, 0, pl.ds(2 * c, 64, stride=6), :] = new[:, :128]
             out[g, 0, pl.ds(2 * c + 1, 64, stride=6), :] = new[:, 128:]
 
@@ -377,7 +375,7 @@
         in_specs=[SMEM] * 3
         + [pl.BlockSpec((384, 1024), lambda i: (i, 0))]
         + [part(128)] * 3
-        + [whole(2, 1536, 128)] * 2
+        + [pl.BlockSpec(memory_space=pl.ANY)] * 2
         + [whole(4, 2, 3, 128, 128)] * 2
         + [whole(4, 256, 256)],
         out_specs=part(384),
@@ -388,7 +386,8 @@
         ]
         + [pltpu.VMEM((1024, 768), BF)] * 2
         + [pltpu.VMEM((256, 1536), BF)] * 4
-        + [pltpu.VMEM((4, 256, 256), BF)] * 2,
+        + [pltpu.VMEM((4, 256, 256), BF)] * 2
+        + [pltpu.VMEM((2, 2, 1536, 128), jnp.float32), pltpu.SemaphoreType.DMA((2,))],
         compiler_params=LARGE,
         name="update",
     )(

time: 205 us -> 206 us (level)
  no operation moved by 1% of the time
where the time goes in v5:
time: 206 us; the launch traced here: 202 us
  starting transfers between devices  58.1 us (28%)
  Pallas kernels  52 us (25%)
  waiting for transfers between devices  47.9 us (23%)
  local copies, waits for them, and re-layouts  18.4 us (9%)
  between operations  13.7 us (7%)
  other arithmetic  11.9 us (6%)
    pallas_call x1, Pallas kernels, body(): pl.pallas_call(update_kernel, out_shape=f32(6, 4, 384, 128), grid=(4,), i...  25.7 us
    ppermute x6, starting transfers between devices, hop_z(): lax.ppermute(value, 'prow', [(2 * a + c, 2 * b + c) for a, b in pairs for...  19.8 us
    all_to_all x3, starting transfers between devices, body(): lax.all_to_all(s.reshape(8, -1, 128), 'prow', 0, 0, tiled=True)  16.6 us
    ppermute x6, waiting for transfers between devices, hop_z(): lax.ppermute(value, 'prow', [(2 * a + c, 2 * b + c) for a, b in pairs for...  15.7 us
    unnamed x33, local copies, waits for them, and re-layouts  14.8 us
    ppermute x3, waiting for transfers between devices, scatter_x(): lax.ppermute(blocks[s], 'pcol', [(k, k + 4 * s) for k in range(4)])  14.1 us
    pallas_call x3, Pallas kernels, place_rows(): pl.pallas_call(place_kernel, out_shape=f32(*arrived.shape), in_specs=[SME...  9.48 us
    ppermute x3, starting transfers between devices, scatter_x(): lax.ppermute(blocks[s], 'pcol', [(k, k + 4 * s) for k in range(4)])  9.33 us
  transfers between devices with their start and end apart: 21, of which 9 were waited for; matrix products, arithmetic and copies ran while one was open for 6% of the time, Pallas kernels for 9%

profile of v5, /device:TPU:1, one launch (start us, length us, event | category | flops | bytes accessed | tf_op | source)
XLA Modules:
  0.0 201.9 jit_solution(17555573908638494614)
XLA Ops:
  7.4 2.3 %copy-done.1 = f32[6,1,256,3,1,256]{5,4,3,2,1,0:T(1,128)S(1)} copy-done((f32[6,1,256,3,1,256]{5,4,3,2,1,0:T(1,128)S(1)}, f32[6,1,256,3,1,256]{5,4,3,2,1,0:T(1,128)}, u32[]{:S(2)}) %copy-start.1) | copy-done | bytes 4718616
  9.7 5.9 %send_first.1 = (f32[1536,2,128]{2,1,0:T(2,128)}, s32[12,128]{1,0:T(8,128)S(1)}) custom-call(s32[12,128]{1,0:T(8,128)S(1)} %reshape.58.targets, f32[4608,2,128]{2,1,0:T(2,128)S(1)} %bitcast.58), custom_call_target="tpu_custom_call" | custom-call | tf_op jit(solution)/shard_map/send_first/pallas_call | solution.py:66
  15.7 6.8 %all-to-all-start = ((f32[8,384,128]{2,1,0:T(8,128)}), f32[8,384,128]{2,1,0:T(8,128)S(1)}, u32[]{:S(2)}, u32[]{:S(2)}) async-start(f32[8,384,128]{2,1,0:T(8,128)} %bitcast.9), calls=%async_computation | async-start | bytes 3145728 | tf_op jit(solution)/shard_map/all_to_all | solution.py:325
  23.2 2.3 %copy-done.2 = f32[6,1,256,3,1,256]{5,4,3,2,1,0:T(1,128)S(1)} copy-done((f32[6,1,256,3,1,256]{5,4,3,2,1,0:T(1,128)S(1)}, f32[6,1,256,3,1,256]{5,4,3,2,1,0:T(1,128)}, u32[]{:S(2)}) %copy-start.2) | copy-done | bytes 4718616
  25.6 5.0 %send_rest.1 = (f32[1536,2,128]{2,1,0:T(2,128)S(1)}, f32[1536,2,128]{2,1,0:T(2,128)S(1)}) custom-call(s32[12,128]{1,0:T(8,128)S(1)} %get-tuple-element.33.slots, f32[4608,2,128]{2,1,0:T(2,128)S(1)} %bitcast.59), custom_call_target="tpu_custom_call" | custom-call | tf_op jit(solution)/shard_map/send_rest/pallas_call | solution.py:98
  30.6 1.2 copy-done.12
  31.7 1.2 copy-done.13
  33.8 5.0 %sort.22 = (s32[1536]{0:T(1024)S(1)}, s32[1536]{0:T(1024)}) sort(s32[1536]{0:T(1024)S(1)} %fusion.15, s32[1536]{0:T(1024)S(1)} %iota.10), dimensions={0}, to_apply=%region_1.2 | sort | flops 16896 | bytes 24576 | tf_op jit(solution)/shard_map/sort | solution.py:329
  38.9 4.4 %all-to-all-done = f32[8,384,128]{2,1,0:T(8,128)S(1)} async-done(((f32[8,384,128]{2,1,0:T(8,128)}), f32[8,384,128]{2,1,0:T(8,128)S(1)}, u32[]{:S(2)}, u32[]{:S(2)}) %all-to-all-start) | async-done | bytes 1572896 | tf_op jit(solution)/shard_map/all_to_all | solution.py:325
  43.2 3.2 %place_rows.3.p0 = f32[1536,2,128]{2,1,0:T(2,128)S(1)} custom-call(s32[1536]{0:T(1024)S(1)} %add_select_fusion.4.order, f32[1536,2,128]{2,1,0:T(2,128)S(1)} %bitcast.64), custom_call_target="tpu_custom_call" | custom-call | tf_op jit(solution)/shard_map/place_rows/pallas_call | solution.py:142
  46.4 4.4 %all-to-all-start.1 = ((f32[8,384,128]{2,1,0:T(8,128)}), f32[8,384,128]{2,1,0:T(8,128)S(1)}, u32[]{:S(2)}, u32[]{:S(2)}) async-start(f32[8,384,128]{2,1,0:T(8,128)} %bitcast.68), calls=%async_computation.1 | async-start | bytes 3145728 | tf_op jit(solution)/shard_map/all_to_all | solution.py:325
  50.7 0.9 slice_bitcast_fusion
  51.7 5.2 %collective-permute-start.2 = (f32[6,128,128]{2,1,0:T(8,128)}, f32[6,128,128]{2,1,0:T(8,128)}, u32[]{:S(2)}, u32[]{:S(2)}) collective-permute-start(f32[6,128,128]{2,1,0:T(8,128)} %get-tuple-element.58), channel_id=1, source_target_pairs={{0,12},{1,13},{2,14},{3,15},{16,28},{17,29},{18,30},{19,31},{32,44... | collective-permute-start | bytes 1179656 | tf_op jit(solution)/shard_map/ppermute | solution.py:281
  56.9 2.1 %collective-permute-start = (f32[6,128,128]{2,1,0:T(8,128)}, f32[6,128,128]{2,1,0:T(8,128)}, u32[]{:S(2)}, u32[]{:S(2)}) collective-permute-start(f32[6,128,128]{2,1,0:T(8,128)} %get-tuple-element.59), channel_id=1, source_target_pairs={{0,4},{1,5},{2,6},{3,7},{16,20},{17,21},{18,22},{19,23},{32,36},{3... | collective-permute-start | bytes 1179656 | tf_op jit(solution)/shard_map/ppermute | solution.py:281
  58.9 2.1 %collective-permute-start.1 = (f32[6,128,128]{2,1,0:T(8,128)S(1)}, f32[6,128,128]{2,1,0:T(8,128)}, u32[]{:S(2)}, u32[]{:S(2)}) collective-permute-start(f32[6,128,128]{2,1,0:T(8,128)S(1)} %get-tuple-element.60), channel_id=1, source_target_pairs={{0,8},{1,9},{2,10},{3,11},{16,24},{17,25},{18,26},{19,27},{32,40},... | collective-permute-start | bytes 1179656 | tf_op jit(solution)/shard_map/ppermute | solution.py:281
  61.0 3.7 %collective-permute-done.2 = f32[6,128,128]{2,1,0:T(8,128)} collective-permute-done((f32[6,128,128]{2,1,0:T(8,128)}, f32[6,128,128]{2,1,0:T(8,128)}, u32[]{:S(2)}, u32[]{:S(2)}) %collective-permute-start.2) | collective-permute-done | bytes 393248 | tf_op jit(solution)/shard_map/ppermute | solution.py:281
  64.7 2.1 %collective-permute-done = f32[6,128,128]{2,1,0:T(8,128)} collective-permute-done((f32[6,128,128]{2,1,0:T(8,128)}, f32[6,128,128]{2,1,0:T(8,128)}, u32[]{:S(2)}, u32[]{:S(2)}) %collective-permute-start) | collective-permute-done | bytes 393248 | tf_op jit(solution)/shard_map/ppermute | solution.py:281
  66.8 8.3 %collective-permute-done.1 = f32[6,128,128]{2,1,0:T(8,128)} collective-permute-done((f32[6,128,128]{2,1,0:T(8,128)S(1)}, f32[6,128,128]{2,1,0:T(8,128)}, u32[]{:S(2)}, u32[]{:S(2)}) %collective-permute-start.1) | collective-permute-done | bytes 393248 | tf_op jit(solution)/shard_map/ppermute | solution.py:281
  75.1 2.6 %fusion = f32[6,128,128]{2,1,0:T(8,128)} fusion(f32[6,4,128,128]{3,2,1,0:T(8,128)S(1)} %bitcast.56, f32[6,128,128]{2,1,0:T(8,128)} %collective-permute-done.2, f32[6,128,128]{2,1,0:T(8,128)} %collective-permute-done, f32[6,128,128]{2,1,0:T(8,128)} %collective-permute-done.1, pred[]{:T(512)S(6)} %eq.33), kind=kLoop, calls=%fused_computation.8 | loop fusion | flops 294912 | bytes 1966081 | tf_op jit(solution)/shard_map/jit(_where)/select_n | solution.py:286
  77.8 5.4 %all-to-all-start.2 = ((f32[8,384,128]{2,1,0:T(8,128)}), f32[8,384,128]{2,1,0:T(8,128)S(1)}, u32[]{:S(2)}, u32[]{:S(2)}) async-start(f32[8,384,128]{2,1,0:T(8,128)} %bitcast.67), calls=%async_computation.2 | async-start | bytes 3145728 | tf_op jit(solution)/shard_map/all_to_all | solution.py:325
  84.1 2.8 %collective-permute-start.5 = (f32[128,128]{1,0:T(8,128)S(1)}, f32[128,128]{1,0:T(8,128)S(1)}, u32[]{:S(2)}, u32[]{:S(2)}) collective-permute-start(f32[128,128]{1,0:T(8,128)S(1)} %get-tuple-element.64), channel_id=1, source_target_pairs={{0,3},{1,0},{2,1},{3,2},{4,7},{5,4},{6,5},{7,6},{8,11},{9,8},{10,9... | collective-permute-start | bytes 196616 | tf_op jit(solution)/shard_map/ppermute | solution.py:341
  88.0 1.4 copy-done.7
  89.4 3.2 %place_rows.4.p1 = f32[1536,2,128]{2,1,0:T(2,128)S(1)} custom-call(s32[1536]{0:T(1024)S(1)} %add_select_fusion.4.order, f32[1536,2,128]{2,1,0:T(2,128)S(1)} %bitcast.63), custom_call_target="tpu_custom_call" | custom-call | tf_op jit(solution)/shard_map/place_rows/pallas_call | solution.py:142
  92.6 1.1 copy-done.3
  94.4 3.3 %collective-permute-start.7 = (f32[3,128,128]{2,1,0:T(8,128)S(1)}, f32[3,128,128]{2,1,0:T(8,128)S(1)}, u32[]{:S(2)}, u32[]{:S(2)}) collective-permute-start(f32[3,128,128]{2,1,0:T(8,128)S(1)} %corner_rows.1), channel_id=1, source_target_pairs={{0,32},{16,48},{32,0},{48,16},{1,33},{17,49},{33,1},{49,17},{2,34}... | collective-permute-start | bytes 589832 | tf_op jit(solution)/shard_map/ppermute | solution.py:290
  97.7 2.6 %collective-permute-start.6 = (f32[3,128,128]{2,1,0:T(8,128)S(1)}, f32[3,128,128]{2,1,0:T(8,128)}, u32[]{:S(2)}, u32[]{:S(2)}) collective-permute-start(f32[3,128,128]{2,1,0:T(8,128)S(1)} %corner_rows.1), channel_id=1, source_target_pairs={{0,96},{16,112},{32,64},{48,80},{1,97},{17,113},{33,65},{49,81},{2... | collective-permute-start | bytes 589832 | tf_op jit(solution)/shard_map/ppermute | solution.py:290
  100.2 3.7 %all-to-all-done.2 = f32[8,384,128]{2,1,0:T(8,128)S(1)} async-done(((f32[8,384,128]{2,1,0:T(8,128)}), f32[8,384,128]{2,1,0:T(8,128)S(1)}, u32[]{:S(2)}, u32[]{:S(2)}) %all-to-all-start.2) | async-done | bytes 1572896 | tf_op jit(solution)/shard_map/all_to_all | solution.py:325
  104.0 2.7 %collective-permute-done.7 = f32[3,128,128]{2,1,0:T(8,128)S(1)} collective-permute-done((f32[3,128,128]{2,1,0:T(8,128)S(1)}, f32[3,128,128]{2,1,0:T(8,128)S(1)}, u32[]{:S(2)}, u32[]{:S(2)}) %collective-permute-start.7) | collective-permute-done | bytes 196640 | tf_op jit(solution)/shard_map/ppermute | solution.py:290
  106.7 1.4 collective-permute-start.8
  108.1 1.4 copy-done.4
  109.5 1.9 top_rows.1
  111.4 1.1 select_bitcast_fusion.3
  112.5 9.1 %collective-permute-start.13 = (f32[1536,128]{1,0:T(8,128)}, f32[1536,128]{1,0:T(8,128)}, u32[]{:S(2)}, u32[]{:S(2)}) collective-permute-start(f32[1536,128]{1,0:T(8,128)} %bitcast.26), channel_id=1, source_target_pairs={{0,96},{16,112},{32,64},{48,80},{1,97},{17,113},{33,65},{49,81},{2... | collective-permute-start | bytes 2359304 | tf_op jit(solution)/shard_map/ppermute | solution.py:290
  121.6 1.9 collective-permute-start.12
  123.5 12.9 %collective-permute-done.13 = f32[1536,128]{1,0:T(8,128)} collective-permute-done((f32[1536,128]{1,0:T(8,128)}, f32[1536,128]{1,0:T(8,128)}, u32[]{:S(2)}, u32[]{:S(2)}) %collective-permute-start.13) | collective-permute-done | bytes 786464 | tf_op jit(solution)/shard_map/ppermute | solution.py:290
  136.5 1.5 collective-permute-start.14
  138.0 3.2 %place_rows.5 = f32[1536,2,128]{2,1,0:T(2,128)S(1)} custom-call(s32[1536]{0:T(1024)S(1)} %add_select_fusion.4.order, f32[1536,2,128]{2,1,0:T(2,128)S(1)} %bitcast.61), custom_call_target="tpu_custom_call" | custom-call | tf_op jit(solution)/shard_map/place_rows/pallas_call | solution.py:142
  141.2 1.2 copy-done.9
  142.3 2.1 %collective-permute-start.11 = (f32[2,3,128,128]{3,2,1,0:T(8,128)S(1)}, f32[2,3,128,128]{3,2,1,0:T(8,128)S(1)}, u32[]{:S(2)}, u32[]{:S(2)}) collective-permute-start(f32[2,3,128,128]{3,2,1,0:T(8,128)S(1)} %pad_maximum_fusion.2), channel_id=1, source_target_pairs={{0,12},{1,13},{2,14},{3,15},{4,0},{5,1},{6,2},{7,3},{8,4},{9,5},{1... | collective-permute-start | bytes 1179656 | tf_op jit(solution)/shard_map/ppermute | solution.py:341
  144.5 1.5 collective-permute-start.10
  146.0 0.9 collective-permute-start.9
  146.9 2.2 %select_bitcast_fusion.1 = (f32[1,1536,128]{2,1,0:T(8,128)S(1)}, f32[1,1536,128]{2,1,0:T(8,128)S(1)}) fusion(f32[1536,128]{1,0:T(8,128)} %bitcast.26, f32[1536,128]{1,0:T(8,128)} %collective-permute-done.12, f32[1536,128]{1,0:T(8,128)} %collective-permute-done.14, f32[1536,128]{1,0:T(8,128)} %collective-permute-done.13, pred[]{:T(512)S(6)} %eq.35, ...), kind=kLoop, calls=%fused_computation.3 | loop fusion | flops 1179648 | bytes 4718596 | tf_op jit(solution)/shard_map/stack | solution.py:298
  149.2 3.3 %collective-permute-start.15 = (f32[2,1536,128]{2,1,0:T(8,128)S(1)}, f32[2,1536,128]{2,1,0:T(8,128)S(1)}, u32[]{:S(2)}, u32[]{:S(2)}) collective-permute-start(f32[2,1536,128]{2,1,0:T(8,128)S(1)} %pad_maximum_fusion.mine), channel_id=1, source_target_pairs={{0,16},{16,0},{32,48},{48,32},{64,80},{80,64},{96,112},{112,96},{1... | collective-permute-start | bytes 4718600 | tf_op jit(solution)/shard_map/ppermute | solution.py:302
  152.4 3.3 %scale.1.scaled = f32[1536,1024]{1,0:T(8,128)S(1)} custom-call(f32[4,4,768,128]{3,2,1,0:T(8,128)S(1)} %bitcast.65, f32[4,256,256]{2,1,0:T(8,128)S(1)} %copy-done.11), custom_call_target="tpu_custom_call" | custom-call | tf_op jit(solution)/shard_map/scale/pallas_call | solution.py:359
  155.8 2.6 %copy-done = f32[1536,1024]{1,0:T(8,128)} copy-done((f32[1536,1024]{1,0:T(8,128)}, f32[1536,1024]{1,0:T(8,128)S(1)}, u32[]{:S(2)}) %copy-start) | copy-done | bytes 6291480
  158.4 7.0 %collective-permute-done.9 = f32[2,3,128,128]{3,2,1,0:T(8,128)S(1)} collective-permute-done((f32[2,3,128,128]{3,2,1,0:T(8,128)S(1)}, f32[2,3,128,128]{3,2,1,0:T(8,128)S(1)}, u32[]{:S(2)}, u32[]{:S(2)}) %collective-permute-start.9) | collective-permute-done | bytes 393248 | tf_op jit(solution)/shard_map/ppermute | solution.py:341
  166.3 3.0 %collective-permute-done.16.other_c = f32[4,2,3,128,128]{4,3,2,1,0:T(8,128)S(1)} collective-permute-done((f32[4,2,3,128,128]{4,3,2,1,0:T(8,128)S(1)}, f32[4,2,3,128,128]{4,3,2,1,0:T(8,128)S(1)}, u32[]{:S(2)}, u32[]{:S(2)}) %collective-permute-start.16) | collective-permute-done | bytes 1572896 | tf_op jit(solution)/shard_map/ppermute | solution.py:302
  169.3 25.7 %update.1 = f32[6,4,384,128]{3,2,1,0:T(8,128)} custom-call(s32[5]{0:T(128)S(1)} %stack.68.place, s32[4,48]{1,0:T(4,128)S(1)} %copy-done.14, s32[4,48]{1,0:T(4,128)S(1)} %copy-done.15, f32[1536,1024]{1,0:T(8,128)} %copy-done, f32[6,4,128,128]{3,2,1,0:T(8,128)S(1)} %bitcast.57, f32[6,4,128,128]{3,2,1,0:T(8,128)S(1)} %bitcast.62, ...), custom_call_target="tpu_custom_call" | custom-call | tf_op jit(solution)/shard_map/update/pallas_call | solution.py:371
  (60 shorter events, 6.1 us)
Async XLA Ops:
  7.4 2.3 %copy-start.1 = (f32[6,1,256,3,1,256]{5,4,3,2,1,0:T(1,128)S(1)}, f32[6,1,256,3,1,256]{5,4,3,2,1,0:T(1,128)}, u32[]{:S(2)}) copy-start(f32[6,1,256,3,1,256]{5,4,3,2,1,0:T(1,128)} %param.5) | copy-start | bytes 14155780
  15.7 27.5 %all-to-all-start = ((f32[8,384,128]{2,1,0:T(8,128)}), f32[8,384,128]{2,1,0:T(8,128)S(1)}, u32[]{:S(2)}, u32[]{:S(2)}) async-start(f32[8,384,128]{2,1,0:T(8,128)} %bitcast.9), calls=%async_computation | async-start | bytes 3145728 | tf_op jit(solution)/shard_map/all_to_all | solution.py:325
  22.5 10.4 %sort.24.cloned.1.call-start = ((), (), s32[]{:S(2)}) async-start(), calls=%async_computation.4 | async-start | bytes 147488 | tf_op jit(solution)/shard_map/sort | solution.py:327
  23.2 2.3 %copy-start.2 = (f32[6,1,256,3,1,256]{5,4,3,2,1,0:T(1,128)S(1)}, f32[6,1,256,3,1,256]{5,4,3,2,1,0:T(1,128)}, u32[]{:S(2)}) copy-start(f32[6,1,256,3,1,256]{5,4,3,2,1,0:T(1,128)} %param.5) | copy-start | bytes 14155780
  30.6 1.2 copy-start.12
  31.7 1.2 copy-start.13
  46.4 28.8 %all-to-all-start.1 = ((f32[8,384,128]{2,1,0:T(8,128)}), f32[8,384,128]{2,1,0:T(8,128)S(1)}, u32[]{:S(2)}, u32[]{:S(2)}) async-start(f32[8,384,128]{2,1,0:T(8,128)} %bitcast.68), calls=%async_computation.1 | async-start | bytes 3145728 | tf_op jit(solution)/shard_map/all_to_all | solution.py:325
  50.7 91.6 %all-gather.2.cloned.1.call-start = ((), (), s32[]{:S(2)}) async-start(), calls=%async_computation.3 | async-start | bytes 6684672 | tf_op jit(solution)/shard_map/all_gather | solution.py:336
  51.7 13.0 %collective-permute-start.2 = (f32[6,128,128]{2,1,0:T(8,128)}, f32[6,128,128]{2,1,0:T(8,128)}, u32[]{:S(2)}, u32[]{:S(2)}) collective-permute-start(f32[6,128,128]{2,1,0:T(8,128)} %get-tuple-element.58), channel_id=1, source_target_pairs={{0,12},{1,13},{2,14},{3,15},{16,28},{17,29},{18,30},{19,31},{32,44... | collective-permute-start | bytes 1179656 | tf_op jit(solution)/shard_map/ppermute | solution.py:281
  56.9 10.0 %collective-permute-start = (f32[6,128,128]{2,1,0:T(8,128)}, f32[6,128,128]{2,1,0:T(8,128)}, u32[]{:S(2)}, u32[]{:S(2)}) collective-permute-start(f32[6,128,128]{2,1,0:T(8,128)} %get-tuple-element.59), channel_id=1, source_target_pairs={{0,4},{1,5},{2,6},{3,7},{16,20},{17,21},{18,22},{19,23},{32,36},{3... | collective-permute-start | bytes 1179656 | tf_op jit(solution)/shard_map/ppermute | solution.py:281
  58.9 16.2 %collective-permute-start.1 = (f32[6,128,128]{2,1,0:T(8,128)S(1)}, f32[6,128,128]{2,1,0:T(8,128)}, u32[]{:S(2)}, u32[]{:S(2)}) collective-permute-start(f32[6,128,128]{2,1,0:T(8,128)S(1)} %get-tuple-element.60), channel_id=1, source_target_pairs={{0,8},{1,9},{2,10},{3,11},{16,24},{17,25},{18,26},{19,27},{32,40},... | collective-permute-start | bytes 1179656 | tf_op jit(solution)/shard_map/ppermute | solution.py:281
  75.1 2.7 %copy-start.6 = (f32[8,384,128]{2,1,0:T(8,128)}, f32[8,384,128]{2,1,0:T(8,128)S(1)}, u32[]{:S(2)}) copy-start(f32[8,384,128]{2,1,0:T(8,128)S(1)} %all-to-all-done.1) | copy-start | bytes 4718596
  77.8 26.2 %all-to-all-start.2 = ((f32[8,384,128]{2,1,0:T(8,128)}), f32[8,384,128]{2,1,0:T(8,128)S(1)}, u32[]{:S(2)}, u32[]{:S(2)}) async-start(f32[8,384,128]{2,1,0:T(8,128)} %bitcast.67), calls=%async_computation.2 | async-start | bytes 3145728 | tf_op jit(solution)/shard_map/all_to_all | solution.py:325
  84.1 9.6 %collective-permute-start.5 = (f32[128,128]{1,0:T(8,128)S(1)}, f32[128,128]{1,0:T(8,128)S(1)}, u32[]{:S(2)}, u32[]{:S(2)}) collective-permute-start(f32[128,128]{1,0:T(8,128)S(1)} %get-tuple-element.64), channel_id=1, source_target_pairs={{0,3},{1,0},{2,1},{3,2},{4,7},{5,4},{6,5},{7,6},{8,11},{9,8},{10,9... | collective-permute-start | bytes 196616 | tf_op jit(solution)/shard_map/ppermute | solution.py:341
  86.9 6.9 %collective-permute-start.4 = (f32[128,128]{1,0:T(8,128)S(1)}, f32[128,128]{1,0:T(8,128)S(1)}, u32[]{:S(2)}, u32[]{:S(2)}) collective-permute-start(f32[128,128]{1,0:T(8,128)S(1)} %get-tuple-element.64), channel_id=1, source_target_pairs={{0,2},{1,3},{2,0},{3,1},{4,6},{5,7},{6,4},{7,5},{8,10},{9,11},{10,... | collective-permute-start | bytes 196616 | tf_op jit(solution)/shard_map/ppermute | solution.py:341
  87.2 6.5 %collective-permute-start.3 = (f32[128,128]{1,0:T(8,128)S(1)}, f32[128,128]{1,0:T(8,128)S(1)}, u32[]{:S(2)}, u32[]{:S(2)}) collective-permute-start(f32[128,128]{1,0:T(8,128)S(1)} %get-tuple-element.64), channel_id=1, source_target_pairs={{0,1},{1,2},{2,3},{3,0},{4,5},{5,6},{6,7},{7,4},{8,9},{9,10},{10,1... | collective-permute-start | bytes 196616 | tf_op jit(solution)/shard_map/ppermute | solution.py:341
  88.0 1.4 copy-start.7
  92.6 1.1 copy-start.3
  94.4 12.3 %collective-permute-start.7 = (f32[3,128,128]{2,1,0:T(8,128)S(1)}, f32[3,128,128]{2,1,0:T(8,128)S(1)}, u32[]{:S(2)}, u32[]{:S(2)}) collective-permute-start(f32[3,128,128]{2,1,0:T(8,128)S(1)} %corner_rows.1), channel_id=1, source_target_pairs={{0,32},{16,48},{32,0},{48,16},{1,33},{17,49},{33,1},{49,17},{2,34}... | collective-permute-start | bytes 589832 | tf_op jit(solution)/shard_map/ppermute | solution.py:290
  97.7 9.0 %collective-permute-start.6 = (f32[3,128,128]{2,1,0:T(8,128)S(1)}, f32[3,128,128]{2,1,0:T(8,128)}, u32[]{:S(2)}, u32[]{:S(2)}) collective-permute-start(f32[3,128,128]{2,1,0:T(8,128)S(1)} %corner_rows.1), channel_id=1, source_target_pairs={{0,96},{16,112},{32,64},{48,80},{1,97},{17,113},{33,65},{49,81},{2... | collective-permute-start | bytes 589832 | tf_op jit(solution)/shard_map/ppermute | solution.py:290
  106.7 4.7 %collective-permute-start.8 = (f32[3,128,128]{2,1,0:T(8,128)}, f32[3,128,128]{2,1,0:T(8,128)}, u32[]{:S(2)}, u32[]{:S(2)}) collective-permute-start(f32[3,128,128]{2,1,0:T(8,128)} %collective-permute-done.6), channel_id=1, source_target_pairs={{96,64},{112,80},{64,96},{80,112},{97,65},{113,81},{65,97},{81,113... | collective-permute-start | bytes 589832 | tf_op jit(solution)/shard_map/ppermute | solution.py:290
  108.0 1.4 copy-start.4
  112.5 23.9 %collective-permute-start.13 = (f32[1536,128]{1,0:T(8,128)}, f32[1536,128]{1,0:T(8,128)}, u32[]{:S(2)}, u32[]{:S(2)}) collective-permute-start(f32[1536,128]{1,0:T(8,128)} %bitcast.26), channel_id=1, source_target_pairs={{0,96},{16,112},{32,64},{48,80},{1,97},{17,113},{33,65},{49,81},{2... | collective-permute-start | bytes 2359304 | tf_op jit(solution)/shard_map/ppermute | solution.py:290
  121.6 25.3 %collective-permute-start.12 = (f32[1536,128]{1,0:T(8,128)}, f32[1536,128]{1,0:T(8,128)}, u32[]{:S(2)}, u32[]{:S(2)}) collective-permute-start(f32[1536,128]{1,0:T(8,128)} %bitcast.26), channel_id=1, source_target_pairs={{0,32},{16,48},{32,0},{48,16},{1,33},{17,49},{33,1},{49,17},{2,34}... | collective-permute-start | bytes 2359304 | tf_op jit(solution)/shard_map/ppermute | solution.py:290
  136.5 10.4 %collective-permute-start.14 = (f32[1536,128]{1,0:T(8,128)}, f32[1536,128]{1,0:T(8,128)}, u32[]{:S(2)}, u32[]{:S(2)}) collective-permute-start(f32[1536,128]{1,0:T(8,128)} %collective-permute-done.13), channel_id=1, source_target_pairs={{96,64},{112,80},{64,96},{80,112},{97,65},{113,81},{65,97},{81,113... | collective-permute-start | bytes 2359304 | tf_op jit(solution)/shard_map/ppermute | solution.py:290
  141.2 1.2 copy-start.9
  142.3 16.1 %collective-permute-start.11 = (f32[2,3,128,128]{3,2,1,0:T(8,128)S(1)}, f32[2,3,128,128]{3,2,1,0:T(8,128)S(1)}, u32[]{:S(2)}, u32[]{:S(2)}) collective-permute-start(f32[2,3,128,128]{3,2,1,0:T(8,128)S(1)} %pad_maximum_fusion.2), channel_id=1, source_target_pairs={{0,12},{1,13},{2,14},{3,15},{4,0},{5,1},{6,2},{7,3},{8,4},{9,5},{1... | collective-permute-start | bytes 1179656 | tf_op jit(solution)/shard_map/ppermute | solution.py:341
  144.5 14.0 %collective-permute-start.10 = (f32[2,3,128,128]{3,2,1,0:T(8,128)S(1)}, f32[2,3,128,128]{3,2,1,0:T(8,128)S(1)}, u32[]{:S(2)}, u32[]{:S(2)}) collective-permute-start(f32[2,3,128,128]{3,2,1,0:T(8,128)S(1)} %pad_maximum_fusion.2), channel_id=1, source_target_pairs={{0,8},{1,9},{2,10},{3,11},{4,12},{5,13},{6,14},{7,15},{8,0},{9,1},... | collective-permute-start | bytes 1179656 | tf_op jit(solution)/shard_map/ppermute | solution.py:341
  146.0 19.4 %collective-permute-start.9 = (f32[2,3,128,128]{3,2,1,0:T(8,128)S(1)}, f32[2,3,128,128]{3,2,1,0:T(8,128)S(1)}, u32[]{:S(2)}, u32[]{:S(2)}) collective-permute-start(f32[2,3,128,128]{3,2,1,0:T(8,128)S(1)} %pad_maximum_fusion.2), channel_id=1, source_target_pairs={{0,4},{1,5},{2,6},{3,7},{4,8},{5,9},{6,10},{7,11},{8,12},{9,13},{1... | collective-permute-start | bytes 1179656 | tf_op jit(solution)/shard_map/ppermute | solution.py:341
  146.9 5.6 %copy-start.8 = (f32[12288,128]{1,0:T(8,128)S(1)}, f32[12288,128]{1,0:T(8,128)}, u32[]{:S(2)}) copy-start(f32[12288,128]{1,0:T(8,128)} %all-gather.2.cloned.1.call-done) | copy-start | bytes 18874372
  149.0 3.4 %copy-start.11 = (f32[4,256,256]{2,1,0:T(8,128)S(1)}, f32[4,256,256]{2,1,0:T(8,128)}, u32[]{:S(2)}) copy-start(f32[4,256,256]{2,1,0:T(8,128)} %inv.3) | copy-start | bytes 3145732
  149.2 17.1 %collective-permute-start.15 = (f32[2,1536,128]{2,1,0:T(8,128)S(1)}, f32[2,1536,128]{2,1,0:T(8,128)S(1)}, u32[]{:S(2)}, u32[]{:S(2)}) collective-permute-start(f32[2,1536,128]{2,1,0:T(8,128)S(1)} %pad_maximum_fusion.mine), channel_id=1, source_target_pairs={{0,16},{16,0},{32,48},{48,32},{64,80},{80,64},{96,112},{112,96},{1... | collective-permute-start | bytes 4718600 | tf_op jit(solution)/shard_map/ppermute | solution.py:302
  152.4 16.9 %copy-start.15 = (s32[4,48]{1,0:T(4,128)S(1)}, s32[4,48]{1,0:T(4,128)}, u32[]{:S(2)}) copy-start(s32[4,48]{1,0:T(4,128)} %upper_fill.1) | copy-start | bytes 2308
  155.8 2.6 %copy-start = (f32[1536,1024]{1,0:T(8,128)}, f32[1536,1024]{1,0:T(8,128)S(1)}, u32[]{:S(2)}) copy-start(f32[1536,1024]{1,0:T(8,128)S(1)} %scale.1.scaled) | copy-start | bytes 18874372
  165.4 3.9 %copy-start.5 = (f32[1536,2,128]{2,1,0:T(2,128)S(1)}, f32[1536,2,128]{2,1,0:T(2,128)}, u32[]{:S(2)}) copy-start(f32[1536,2,128]{2,1,0:T(2,128)} %copy-done.3) | copy-start | bytes 4718596
  165.4 3.9 %copy-start.10 = (f32[1536,2,128]{2,1,0:T(2,128)S(1)}, f32[1536,2,128]{2,1,0:T(2,128)}, u32[]{:S(2)}) copy-start(f32[1536,2,128]{2,1,0:T(2,128)} %copy-done.9) | copy-start | bytes 4718596
  165.4 3.9 %copy-start.14 = (s32[4,48]{1,0:T(4,128)S(1)}, s32[4,48]{1,0:T(4,128)}, u32[]{:S(2)}) copy-start(s32[4,48]{1,0:T(4,128)} %lower_fill.1) | copy-start | bytes 2308
  165.5 3.8 %collective-permute-start.16 = (f32[4,2,3,128,128]{4,3,2,1,0:T(8,128)S(1)}, f32[4,2,3,128,128]{4,3,2,1,0:T(8,128)S(1)}, u32[]{:S(2)}, u32[]{:S(2)}) collective-permute-start(f32[4,2,3,128,128]{4,3,2,1,0:T(8,128)S(1)} %pad_maximum_fusion.1.mine_c), channel_id=1, source_target_pairs={{0,16},{16,0},{32,48},{48,32},{64,80},{80,64},{96,112},{112,96},{1... | collective-permute-start | bytes 4718600 | tf_op jit(solution)/shard_map/ppermute | solution.py:302
Sparse Core Ops, SparseCore 0:
  25.8 5.2 sort.26.cloned.1.call-done
  77.9 64.0 all-gather.1
  (1 shorter events, 0.0 us)

commit v6 on v4

--- a/solution.py
+++ b/solution.py
@@ -367,8 +367,7 @@
         compiler_params=PARAMS,
         name="scale",
     )(panels, inverses)
-    far, scaled = lax.optimization_barrier((shifts(corner, along_x), scaled))
-    corner = with_other(jnp.stack([corner] + far))
+    corner = with_other(jnp.stack([corner] + shifts(corner, along_x)))
     part = lambda n: pl.BlockSpec((6, 1, n, 128), lambda i: (0, i, 0, 0))
     out = pl.pallas_call(
         update_kernel,

time: 205 us -> 206 us (level); the launches traced: 202 us -> 205 us
  waiting for transfers between devices: 47.9 us -> 51 us
    ppermute x6, waiting for transfers between devices: 7.01 us -> 13.1 us  [body(): lax.ppermute(v, 'pcol', along(s))]
    ppermute x2, waiting for transfers between devices: 3.04 us -> 0.01 us  [with_other(): return (mine, lax.ppermute(mine, 'prow', [(p, p ^ 1) for p in range(8)]))]
  transfers between devices with their start and end apart: 21 -> 21, of which waited for: 9 -> 10; matrix products, arithmetic and copies ran while one was open for 6% -> 6% of each run, Pallas kernels for 9% -> 8%
where the time goes in v6:
time: 206 us; the launch traced here: 205 us
  starting transfers between devices  58.1 us (28%)
  Pallas kernels  51.7 us (25%)
  waiting for transfers between devices  51 us (25%)
  local copies, waits for them, and re-layouts  18.4 us (9%)
  between operations  13.7 us (7%)
  other arithmetic  11.9 us (6%)
    pallas_call x1, Pallas kernels, body(): pl.pallas_call(update_kernel, out_shape=f32(6, 4, 384, 128), grid=(4,), i...  25.4 us
    ppermute x6, starting transfers between devices, hop_z(): lax.ppermute(value, 'prow', [(2 * a + c, 2 * b + c) for a, b in pairs for...  19.8 us
    all_to_all x3, starting transfers between devices, body(): lax.all_to_all(s.reshape(8, -1, 128), 'prow', 0, 0, tiled=True)  16.6 us
    ppermute x6, waiting for transfers between devices, hop_z(): lax.ppermute(value, 'prow', [(2 * a + c, 2 * b + c) for a, b in pairs for...  15.7 us
    unnamed x33, local copies, waits for them, and re-layouts  14.8 us
    ppermute x3, waiting for transfers between devices, scatter_x(): lax.ppermute(blocks[s], 'pcol', [(k, k + 4 * s) for k in range(4)])  14.1 us
    ppermute x6, waiting for transfers between devices, body(): lax.ppermute(v, 'pcol', along(s))  13.1 us
    pallas_call x3, Pallas kernels, place_rows(): pl.pallas_call(place_kernel, out_shape=f32(*arrived.shape), in_specs=[SME...  9.48 us
  transfers between devices with their start and end apart: 21, of which 10 were waited for; matrix products, arithmetic and copies ran while one was open for 6% of the time, Pallas kernels for 8%

profile of v6, /device:TPU:1, one launch (start us, length us, event | category | flops | bytes accessed | tf_op | source)
XLA Modules:
  0.0 204.6 jit_solution(224127617195096496)
XLA Ops:
  7.4 2.3 %copy-done.1 = f32[6,1,256,3,1,256]{5,4,3,2,1,0:T(1,128)S(1)} copy-done((f32[6,1,256,3,1,256]{5,4,3,2,1,0:T(1,128)S(1)}, f32[6,1,256,3,1,256]{5,4,3,2,1,0:T(1,128)}, u32[]{:S(2)}) %copy-start.1) | copy-done | bytes 4718616
  9.7 5.9 %send_first.1 = (f32[1536,2,128]{2,1,0:T(2,128)}, s32[12,128]{1,0:T(8,128)S(1)}) custom-call(s32[12,128]{1,0:T(8,128)S(1)} %reshape.58.targets, f32[4608,2,128]{2,1,0:T(2,128)S(1)} %bitcast.58), custom_call_target="tpu_custom_call" | custom-call | tf_op jit(solution)/shard_map/send_first/pallas_call | solution.py:66
  15.7 6.8 %all-to-all-start = ((f32[8,384,128]{2,1,0:T(8,128)}), f32[8,384,128]{2,1,0:T(8,128)S(1)}, u32[]{:S(2)}, u32[]{:S(2)}) async-start(f32[8,384,128]{2,1,0:T(8,128)} %bitcast.9), calls=%async_computation | async-start | bytes 3145728 | tf_op jit(solution)/shard_map/all_to_all | solution.py:327
  23.2 2.3 %copy-done.2 = f32[6,1,256,3,1,256]{5,4,3,2,1,0:T(1,128)S(1)} copy-done((f32[6,1,256,3,1,256]{5,4,3,2,1,0:T(1,128)S(1)}, f32[6,1,256,3,1,256]{5,4,3,2,1,0:T(1,128)}, u32[]{:S(2)}) %copy-start.2) | copy-done | bytes 4718616
  25.6 5.0 %send_rest.1 = (f32[1536,2,128]{2,1,0:T(2,128)S(1)}, f32[1536,2,128]{2,1,0:T(2,128)S(1)}) custom-call(s32[12,128]{1,0:T(8,128)S(1)} %get-tuple-element.29.slots, f32[4608,2,128]{2,1,0:T(2,128)S(1)} %bitcast.59), custom_call_target="tpu_custom_call" | custom-call | tf_op jit(solution)/shard_map/send_rest/pallas_call | solution.py:98
  30.6 1.2 copy-done.12
  31.7 1.2 copy-done.13
  33.8 5.0 %sort.22 = (s32[1536]{0:T(1024)S(1)}, s32[1536]{0:T(1024)}) sort(s32[1536]{0:T(1024)S(1)} %fusion.15, s32[1536]{0:T(1024)S(1)} %iota.10), dimensions={0}, to_apply=%region_1.2 | sort | flops 16896 | bytes 24576 | tf_op jit(solution)/shard_map/sort | solution.py:331
  38.9 4.4 %all-to-all-done = f32[8,384,128]{2,1,0:T(8,128)S(1)} async-done(((f32[8,384,128]{2,1,0:T(8,128)}), f32[8,384,128]{2,1,0:T(8,128)S(1)}, u32[]{:S(2)}, u32[]{:S(2)}) %all-to-all-start) | async-done | bytes 1572896 | tf_op jit(solution)/shard_map/all_to_all | solution.py:327
  43.2 3.2 %place_rows.3.p0 = f32[1536,2,128]{2,1,0:T(2,128)S(1)} custom-call(s32[1536]{0:T(1024)S(1)} %add_select_fusion.4.order, f32[1536,2,128]{2,1,0:T(2,128)S(1)} %bitcast.64), custom_call_target="tpu_custom_call" | custom-call | tf_op jit(solution)/shard_map/place_rows/pallas_call | solution.py:142
  46.4 4.4 %all-to-all-start.1 = ((f32[8,384,128]{2,1,0:T(8,128)}), f32[8,384,128]{2,1,0:T(8,128)S(1)}, u32[]{:S(2)}, u32[]{:S(2)}) async-start(f32[8,384,128]{2,1,0:T(8,128)} %bitcast.68), calls=%async_computation.1 | async-start | bytes 3145728 | tf_op jit(solution)/shard_map/all_to_all | solution.py:327
  50.7 0.9 slice_bitcast_fusion
  51.7 5.2 %collective-permute-start.2 = (f32[6,128,128]{2,1,0:T(8,128)}, f32[6,128,128]{2,1,0:T(8,128)}, u32[]{:S(2)}, u32[]{:S(2)}) collective-permute-start(f32[6,128,128]{2,1,0:T(8,128)} %get-tuple-element.50), channel_id=1, source_target_pairs={{0,12},{1,13},{2,14},{3,15},{16,28},{17,29},{18,30},{19,31},{32,44... | collective-permute-start | bytes 1179656 | tf_op jit(solution)/shard_map/ppermute | solution.py:283
  56.9 2.1 %collective-permute-start = (f32[6,128,128]{2,1,0:T(8,128)}, f32[6,128,128]{2,1,0:T(8,128)}, u32[]{:S(2)}, u32[]{:S(2)}) collective-permute-start(f32[6,128,128]{2,1,0:T(8,128)} %get-tuple-element.51), channel_id=1, source_target_pairs={{0,4},{1,5},{2,6},{3,7},{16,20},{17,21},{18,22},{19,23},{32,36},{3... | collective-permute-start | bytes 1179656 | tf_op jit(solution)/shard_map/ppermute | solution.py:283
  58.9 2.1 %collective-permute-start.1 = (f32[6,128,128]{2,1,0:T(8,128)S(1)}, f32[6,128,128]{2,1,0:T(8,128)}, u32[]{:S(2)}, u32[]{:S(2)}) collective-permute-start(f32[6,128,128]{2,1,0:T(8,128)S(1)} %get-tuple-element.52), channel_id=1, source_target_pairs={{0,8},{1,9},{2,10},{3,11},{16,24},{17,25},{18,26},{19,27},{32,40},... | collective-permute-start | bytes 1179656 | tf_op jit(solution)/shard_map/ppermute | solution.py:283
  61.0 3.7 %collective-permute-done.2 = f32[6,128,128]{2,1,0:T(8,128)} collective-permute-done((f32[6,128,128]{2,1,0:T(8,128)}, f32[6,128,128]{2,1,0:T(8,128)}, u32[]{:S(2)}, u32[]{:S(2)}) %collective-permute-start.2) | collective-permute-done | bytes 393248 | tf_op jit(solution)/shard_map/ppermute | solution.py:283
  64.7 2.1 %collective-permute-done = f32[6,128,128]{2,1,0:T(8,128)} collective-permute-done((f32[6,128,128]{2,1,0:T(8,128)}, f32[6,128,128]{2,1,0:T(8,128)}, u32[]{:S(2)}, u32[]{:S(2)}) %collective-permute-start) | collective-permute-done | bytes 393248 | tf_op jit(solution)/shard_map/ppermute | solution.py:283
  66.8 8.3 %collective-permute-done.1 = f32[6,128,128]{2,1,0:T(8,128)} collective-permute-done((f32[6,128,128]{2,1,0:T(8,128)S(1)}, f32[6,128,128]{2,1,0:T(8,128)}, u32[]{:S(2)}, u32[]{:S(2)}) %collective-permute-start.1) | collective-permute-done | bytes 393248 | tf_op jit(solution)/shard_map/ppermute | solution.py:283
  75.1 2.6 %fusion = f32[6,128,128]{2,1,0:T(8,128)} fusion(f32[6,4,128,128]{3,2,1,0:T(8,128)S(1)} %bitcast.56, f32[6,128,128]{2,1,0:T(8,128)} %collective-permute-done.2, f32[6,128,128]{2,1,0:T(8,128)} %collective-permute-done, f32[6,128,128]{2,1,0:T(8,128)} %collective-permute-done.1, pred[]{:T(512)S(6)} %eq.33), kind=kLoop, calls=%fused_computation.8 | loop fusion | flops 294912 | bytes 1966081 | tf_op jit(solution)/shard_map/jit(_where)/select_n | solution.py:288
  77.8 5.4 %all-to-all-start.2 = ((f32[8,384,128]{2,1,0:T(8,128)}), f32[8,384,128]{2,1,0:T(8,128)S(1)}, u32[]{:S(2)}, u32[]{:S(2)}) async-start(f32[8,384,128]{2,1,0:T(8,128)} %bitcast.67), calls=%async_computation.2 | async-start | bytes 3145728 | tf_op jit(solution)/shard_map/all_to_all | solution.py:327
  84.1 2.8 %collective-permute-start.5 = (f32[128,128]{1,0:T(8,128)S(1)}, f32[128,128]{1,0:T(8,128)S(1)}, u32[]{:S(2)}, u32[]{:S(2)}) collective-permute-start(f32[128,128]{1,0:T(8,128)S(1)} %get-tuple-element.56), channel_id=1, source_target_pairs={{0,3},{1,0},{2,1},{3,2},{4,7},{5,4},{6,5},{7,6},{8,11},{9,8},{10,9... | collective-permute-start | bytes 196616 | tf_op jit(solution)/shard_map/ppermute | solution.py:343
  88.0 1.4 copy-done.7
  89.4 3.2 %place_rows.4.p1 = f32[1536,2,128]{2,1,0:T(2,128)S(1)} custom-call(s32[1536]{0:T(1024)S(1)} %add_select_fusion.4.order, f32[1536,2,128]{2,1,0:T(2,128)S(1)} %bitcast.63), custom_call_target="tpu_custom_call" | custom-call | tf_op jit(solution)/shard_map/place_rows/pallas_call | solution.py:142
  92.6 1.1 copy-done.3
  94.4 3.3 %collective-permute-start.7 = (f32[3,128,128]{2,1,0:T(8,128)S(1)}, f32[3,128,128]{2,1,0:T(8,128)S(1)}, u32[]{:S(2)}, u32[]{:S(2)}) collective-permute-start(f32[3,128,128]{2,1,0:T(8,128)S(1)} %corner_rows.1), channel_id=1, source_target_pairs={{0,32},{16,48},{32,0},{48,16},{1,33},{17,49},{33,1},{49,17},{2,34}... | collective-permute-start | bytes 589832 | tf_op jit(solution)/shard_map/ppermute | solution.py:292
  97.7 2.6 %collective-permute-start.6 = (f32[3,128,128]{2,1,0:T(8,128)S(1)}, f32[3,128,128]{2,1,0:T(8,128)}, u32[]{:S(2)}, u32[]{:S(2)}) collective-permute-start(f32[3,128,128]{2,1,0:T(8,128)S(1)} %corner_rows.1), channel_id=1, source_target_pairs={{0,96},{16,112},{32,64},{48,80},{1,97},{17,113},{33,65},{49,81},{2... | collective-permute-start | bytes 589832 | tf_op jit(solution)/shard_map/ppermute | solution.py:292
  100.2 3.7 %all-to-all-done.2 = f32[8,384,128]{2,1,0:T(8,128)S(1)} async-done(((f32[8,384,128]{2,1,0:T(8,128)}), f32[8,384,128]{2,1,0:T(8,128)S(1)}, u32[]{:S(2)}, u32[]{:S(2)}) %all-to-all-start.2) | async-done | bytes 1572896 | tf_op jit(solution)/shard_map/all_to_all | solution.py:327
  104.0 2.7 %collective-permute-done.7 = f32[3,128,128]{2,1,0:T(8,128)S(1)} collective-permute-done((f32[3,128,128]{2,1,0:T(8,128)S(1)}, f32[3,128,128]{2,1,0:T(8,128)S(1)}, u32[]{:S(2)}, u32[]{:S(2)}) %collective-permute-start.7) | collective-permute-done | bytes 196640 | tf_op jit(solution)/shard_map/ppermute | solution.py:292
  106.7 1.4 collective-permute-start.8
  108.1 1.4 copy-done.4
  109.5 1.9 top_rows.1
  111.4 1.1 select_bitcast_fusion.3
  112.5 9.1 %collective-permute-start.10 = (f32[1536,128]{1,0:T(8,128)}, f32[1536,128]{1,0:T(8,128)}, u32[]{:S(2)}, u32[]{:S(2)}) collective-permute-start(f32[1536,128]{1,0:T(8,128)} %bitcast.26), channel_id=1, source_target_pairs={{0,96},{16,112},{32,64},{48,80},{1,97},{17,113},{33,65},{49,81},{2... | collective-permute-start | bytes 2359304 | tf_op jit(solution)/shard_map/ppermute | solution.py:292
  121.6 1.9 collective-permute-start.9
  123.5 12.9 %collective-permute-done.10 = f32[1536,128]{1,0:T(8,128)} collective-permute-done((f32[1536,128]{1,0:T(8,128)}, f32[1536,128]{1,0:T(8,128)}, u32[]{:S(2)}, u32[]{:S(2)}) %collective-permute-start.10) | collective-permute-done | bytes 786464 | tf_op jit(solution)/shard_map/ppermute | solution.py:292
  136.5 1.5 collective-permute-start.11
  138.0 3.2 %place_rows.5 = f32[1536,2,128]{2,1,0:T(2,128)S(1)} custom-call(s32[1536]{0:T(1024)S(1)} %add_select_fusion.4.order, f32[1536,2,128]{2,1,0:T(2,128)S(1)} %bitcast.61), custom_call_target="tpu_custom_call" | custom-call | tf_op jit(solution)/shard_map/place_rows/pallas_call | solution.py:142
  141.2 1.2 copy-done.9
  142.3 2.1 %collective-permute-start.15 = (f32[2,3,128,128]{3,2,1,0:T(8,128)S(1)}, f32[2,3,128,128]{3,2,1,0:T(8,128)S(1)}, u32[]{:S(2)}, u32[]{:S(2)}) collective-permute-start(f32[2,3,128,128]{3,2,1,0:T(8,128)S(1)} %pad_maximum_fusion.2), channel_id=1, source_target_pairs={{0,12},{1,13},{2,14},{3,15},{4,0},{5,1},{6,2},{7,3},{8,4},{9,5},{1... | collective-permute-start | bytes 1179656 | tf_op jit(solution)/shard_map/ppermute | solution.py:343
  144.5 1.5 collective-permute-start.14
  146.9 2.1 %select_bitcast_fusion.1 = (f32[1,1536,128]{2,1,0:T(8,128)S(1)}, f32[1,1536,128]{2,1,0:T(8,128)S(1)}) fusion(f32[1536,128]{1,0:T(8,128)} %bitcast.26, f32[1536,128]{1,0:T(8,128)} %collective-permute-done.9, f32[1536,128]{1,0:T(8,128)} %collective-permute-done.11, f32[1536,128]{1,0:T(8,128)} %collective-permute-done.10, pred[]{:T(512)S(6)} %eq.35, ...), kind=kLoop, calls=%fused_computation.3 | loop fusion | flops 1179648 | bytes 4718596 | tf_op jit(solution)/shard_map/stack | solution.py:300
  149.1 3.3 %collective-permute-start.12 = (f32[2,1536,128]{2,1,0:T(8,128)S(1)}, f32[2,1536,128]{2,1,0:T(8,128)S(1)}, u32[]{:S(2)}, u32[]{:S(2)}) collective-permute-start(f32[2,1536,128]{2,1,0:T(8,128)S(1)} %pad_maximum_fusion.mine), channel_id=1, source_target_pairs={{0,16},{16,0},{32,48},{48,32},{64,80},{80,64},{96,112},{112,96},{1... | collective-permute-start | bytes 4718600 | tf_op jit(solution)/shard_map/ppermute | solution.py:304
  152.4 2.0 collective-permute-done.15
  154.3 1.3 collective-permute-done.14
  155.7 9.8 %collective-permute-done.13 = f32[2,3,128,128]{3,2,1,0:T(8,128)S(1)} collective-permute-done((f32[2,3,128,128]{3,2,1,0:T(8,128)S(1)}, f32[2,3,128,128]{3,2,1,0:T(8,128)S(1)}, u32[]{:S(2)}, u32[]{:S(2)}) %collective-permute-start.13) | collective-permute-done | bytes 393248 | tf_op jit(solution)/shard_map/ppermute | solution.py:343
  166.4 3.4 %scale.1.scaled = f32[1536,1024]{1,0:T(8,128)S(1)} custom-call(f32[4,4,768,128]{3,2,1,0:T(8,128)S(1)} %bitcast.65, f32[4,256,256]{2,1,0:T(8,128)S(1)} %copy-done.11), custom_call_target="tpu_custom_call" | custom-call | tf_op jit(solution)/shard_map/scale/pallas_call | solution.py:361
  169.8 2.6 %copy-done = f32[1536,1024]{1,0:T(8,128)} copy-done((f32[1536,1024]{1,0:T(8,128)}, f32[1536,1024]{1,0:T(8,128)S(1)}, u32[]{:S(2)}) %copy-start) | copy-done | bytes 6291480
  172.4 25.4 %update.1 = f32[6,4,384,128]{3,2,1,0:T(8,128)} custom-call(s32[5]{0:T(128)S(1)} %stack.68.place, s32[4,48]{1,0:T(4,128)S(1)} %copy-done.14, s32[4,48]{1,0:T(4,128)S(1)} %copy-done.15, f32[1536,1024]{1,0:T(8,128)} %copy-done, f32[6,4,128,128]{3,2,1,0:T(8,128)S(1)} %bitcast.57, f32[6,4,128,128]{3,2,1,0:T(8,128)S(1)} %bitcast.62, ...), custom_call_target="tpu_custom_call" | custom-call | tf_op jit(solution)/shard_map/update/pallas_call | solution.py:372
  (60 shorter events, 7.0 us)
Async XLA Ops:
  7.4 2.3 %copy-start.1 = (f32[6,1,256,3,1,256]{5,4,3,2,1,0:T(1,128)S(1)}, f32[6,1,256,3,1,256]{5,4,3,2,1,0:T(1,128)}, u32[]{:S(2)}) copy-start(f32[6,1,256,3,1,256]{5,4,3,2,1,0:T(1,128)} %param.5) | copy-start | bytes 14155780
  15.7 27.5 %all-to-all-start = ((f32[8,384,128]{2,1,0:T(8,128)}), f32[8,384,128]{2,1,0:T(8,128)S(1)}, u32[]{:S(2)}, u32[]{:S(2)}) async-start(f32[8,384,128]{2,1,0:T(8,128)} %bitcast.9), calls=%async_computation | async-start | bytes 3145728 | tf_op jit(solution)/shard_map/all_to_all | solution.py:327
  22.5 10.4 %sort.24.cloned.1.call-start = ((), (), s32[]{:S(2)}) async-start(), calls=%async_computation.4 | async-start | bytes 147488 | tf_op jit(solution)/shard_map/sort | solution.py:329
  23.2 2.3 %copy-start.2 = (f32[6,1,256,3,1,256]{5,4,3,2,1,0:T(1,128)S(1)}, f32[6,1,256,3,1,256]{5,4,3,2,1,0:T(1,128)}, u32[]{:S(2)}) copy-start(f32[6,1,256,3,1,256]{5,4,3,2,1,0:T(1,128)} %param.5) | copy-start | bytes 14155780
  30.6 1.2 copy-start.12
  31.7 1.2 copy-start.13
  46.4 28.8 %all-to-all-start.1 = ((f32[8,384,128]{2,1,0:T(8,128)}), f32[8,384,128]{2,1,0:T(8,128)S(1)}, u32[]{:S(2)}, u32[]{:S(2)}) async-start(f32[8,384,128]{2,1,0:T(8,128)} %bitcast.68), calls=%async_computation.1 | async-start | bytes 3145728 | tf_op jit(solution)/shard_map/all_to_all | solution.py:327
  50.7 91.6 %all-gather.2.cloned.1.call-start = ((), (), s32[]{:S(2)}) async-start(), calls=%async_computation.3 | async-start | bytes 6684672 | tf_op jit(solution)/shard_map/all_gather | solution.py:338
  51.7 13.0 %collective-permute-start.2 = (f32[6,128,128]{2,1,0:T(8,128)}, f32[6,128,128]{2,1,0:T(8,128)}, u32[]{:S(2)}, u32[]{:S(2)}) collective-permute-start(f32[6,128,128]{2,1,0:T(8,128)} %get-tuple-element.50), channel_id=1, source_target_pairs={{0,12},{1,13},{2,14},{3,15},{16,28},{17,29},{18,30},{19,31},{32,44... | collective-permute-start | bytes 1179656 | tf_op jit(solution)/shard_map/ppermute | solution.py:283
  56.9 10.0 %collective-permute-start = (f32[6,128,128]{2,1,0:T(8,128)}, f32[6,128,128]{2,1,0:T(8,128)}, u32[]{:S(2)}, u32[]{:S(2)}) collective-permute-start(f32[6,128,128]{2,1,0:T(8,128)} %get-tuple-element.51), channel_id=1, source_target_pairs={{0,4},{1,5},{2,6},{3,7},{16,20},{17,21},{18,22},{19,23},{32,36},{3... | collective-permute-start | bytes 1179656 | tf_op jit(solution)/shard_map/ppermute | solution.py:283
  58.9 16.2 %collective-permute-start.1 = (f32[6,128,128]{2,1,0:T(8,128)S(1)}, f32[6,128,128]{2,1,0:T(8,128)}, u32[]{:S(2)}, u32[]{:S(2)}) collective-permute-start(f32[6,128,128]{2,1,0:T(8,128)S(1)} %get-tuple-element.52), channel_id=1, source_target_pairs={{0,8},{1,9},{2,10},{3,11},{16,24},{17,25},{18,26},{19,27},{32,40},... | collective-permute-start | bytes 1179656 | tf_op jit(solution)/shard_map/ppermute | solution.py:283
  75.1 2.7 %copy-start.6 = (f32[8,384,128]{2,1,0:T(8,128)}, f32[8,384,128]{2,1,0:T(8,128)S(1)}, u32[]{:S(2)}) copy-start(f32[8,384,128]{2,1,0:T(8,128)S(1)} %all-to-all-done.1) | copy-start | bytes 4718596
  77.8 26.2 %all-to-all-start.2 = ((f32[8,384,128]{2,1,0:T(8,128)}), f32[8,384,128]{2,1,0:T(8,128)S(1)}, u32[]{:S(2)}, u32[]{:S(2)}) async-start(f32[8,384,128]{2,1,0:T(8,128)} %bitcast.67), calls=%async_computation.2 | async-start | bytes 3145728 | tf_op jit(solution)/shard_map/all_to_all | solution.py:327
  84.1 9.6 %collective-permute-start.5 = (f32[128,128]{1,0:T(8,128)S(1)}, f32[128,128]{1,0:T(8,128)S(1)}, u32[]{:S(2)}, u32[]{:S(2)}) collective-permute-start(f32[128,128]{1,0:T(8,128)S(1)} %get-tuple-element.56), channel_id=1, source_target_pairs={{0,3},{1,0},{2,1},{3,2},{4,7},{5,4},{6,5},{7,6},{8,11},{9,8},{10,9... | collective-permute-start | bytes 196616 | tf_op jit(solution)/shard_map/ppermute | solution.py:343
  86.9 6.9 %collective-permute-start.4 = (f32[128,128]{1,0:T(8,128)S(1)}, f32[128,128]{1,0:T(8,128)S(1)}, u32[]{:S(2)}, u32[]{:S(2)}) collective-permute-start(f32[128,128]{1,0:T(8,128)S(1)} %get-tuple-element.56), channel_id=1, source_target_pairs={{0,2},{1,3},{2,0},{3,1},{4,6},{5,7},{6,4},{7,5},{8,10},{9,11},{10,... | collective-permute-start | bytes 196616 | tf_op jit(solution)/shard_map/ppermute | solution.py:343
  87.2 6.5 %collective-permute-start.3 = (f32[128,128]{1,0:T(8,128)S(1)}, f32[128,128]{1,0:T(8,128)S(1)}, u32[]{:S(2)}, u32[]{:S(2)}) collective-permute-start(f32[128,128]{1,0:T(8,128)S(1)} %get-tuple-element.56), channel_id=1, source_target_pairs={{0,1},{1,2},{2,3},{3,0},{4,5},{5,6},{6,7},{7,4},{8,9},{9,10},{10,1... | collective-permute-start | bytes 196616 | tf_op jit(solution)/shard_map/ppermute | solution.py:343
  88.0 1.4 copy-start.7
  92.6 1.1 copy-start.3
  94.4 12.3 %collective-permute-start.7 = (f32[3,128,128]{2,1,0:T(8,128)S(1)}, f32[3,128,128]{2,1,0:T(8,128)S(1)}, u32[]{:S(2)}, u32[]{:S(2)}) collective-permute-start(f32[3,128,128]{2,1,0:T(8,128)S(1)} %corner_rows.1), channel_id=1, source_target_pairs={{0,32},{16,48},{32,0},{48,16},{1,33},{17,49},{33,1},{49,17},{2,34}... | collective-permute-start | bytes 589832 | tf_op jit(solution)/shard_map/ppermute | solution.py:292
  97.7 9.0 %collective-permute-start.6 = (f32[3,128,128]{2,1,0:T(8,128)S(1)}, f32[3,128,128]{2,1,0:T(8,128)}, u32[]{:S(2)}, u32[]{:S(2)}) collective-permute-start(f32[3,128,128]{2,1,0:T(8,128)S(1)} %corner_rows.1), channel_id=1, source_target_pairs={{0,96},{16,112},{32,64},{48,80},{1,97},{17,113},{33,65},{49,81},{2... | collective-permute-start | bytes 589832 | tf_op jit(solution)/shard_map/ppermute | solution.py:292
  106.7 4.7 %collective-permute-start.8 = (f32[3,128,128]{2,1,0:T(8,128)}, f32[3,128,128]{2,1,0:T(8,128)}, u32[]{:S(2)}, u32[]{:S(2)}) collective-permute-start(f32[3,128,128]{2,1,0:T(8,128)} %collective-permute-done.6), channel_id=1, source_target_pairs={{96,64},{112,80},{64,96},{80,112},{97,65},{113,81},{65,97},{81,113... | collective-permute-start | bytes 589832 | tf_op jit(solution)/shard_map/ppermute | solution.py:292
  108.0 1.4 copy-start.4
  112.5 23.9 %collective-permute-start.10 = (f32[1536,128]{1,0:T(8,128)}, f32[1536,128]{1,0:T(8,128)}, u32[]{:S(2)}, u32[]{:S(2)}) collective-permute-start(f32[1536,128]{1,0:T(8,128)} %bitcast.26), channel_id=1, source_target_pairs={{0,96},{16,112},{32,64},{48,80},{1,97},{17,113},{33,65},{49,81},{2... | collective-permute-start | bytes 2359304 | tf_op jit(solution)/shard_map/ppermute | solution.py:292
  121.6 25.3 %collective-permute-start.9 = (f32[1536,128]{1,0:T(8,128)}, f32[1536,128]{1,0:T(8,128)}, u32[]{:S(2)}, u32[]{:S(2)}) collective-permute-start(f32[1536,128]{1,0:T(8,128)} %bitcast.26), channel_id=1, source_target_pairs={{0,32},{16,48},{32,0},{48,16},{1,33},{17,49},{33,1},{49,17},{2,34}... | collective-permute-start | bytes 2359304 | tf_op jit(solution)/shard_map/ppermute | solution.py:292
  136.5 10.4 %collective-permute-start.11 = (f32[1536,128]{1,0:T(8,128)}, f32[1536,128]{1,0:T(8,128)}, u32[]{:S(2)}, u32[]{:S(2)}) collective-permute-start(f32[1536,128]{1,0:T(8,128)} %collective-permute-done.10), channel_id=1, source_target_pairs={{96,64},{112,80},{64,96},{80,112},{97,65},{113,81},{65,97},{81,113... | collective-permute-start | bytes 2359304 | tf_op jit(solution)/shard_map/ppermute | solution.py:292
  141.2 1.2 copy-start.9
  142.3 12.0 %collective-permute-start.15 = (f32[2,3,128,128]{3,2,1,0:T(8,128)S(1)}, f32[2,3,128,128]{3,2,1,0:T(8,128)S(1)}, u32[]{:S(2)}, u32[]{:S(2)}) collective-permute-start(f32[2,3,128,128]{3,2,1,0:T(8,128)S(1)} %pad_maximum_fusion.2), channel_id=1, source_target_pairs={{0,12},{1,13},{2,14},{3,15},{4,0},{5,1},{6,2},{7,3},{8,4},{9,5},{1... | collective-permute-start | bytes 1179656 | tf_op jit(solution)/shard_map/ppermute | solution.py:343
  144.5 11.2 %collective-permute-start.14 = (f32[2,3,128,128]{3,2,1,0:T(8,128)S(1)}, f32[2,3,128,128]{3,2,1,0:T(8,128)S(1)}, u32[]{:S(2)}, u32[]{:S(2)}) collective-permute-start(f32[2,3,128,128]{3,2,1,0:T(8,128)S(1)} %pad_maximum_fusion.2), channel_id=1, source_target_pairs={{0,8},{1,9},{2,10},{3,11},{4,12},{5,13},{6,14},{7,15},{8,0},{9,1},... | collective-permute-start | bytes 1179656 | tf_op jit(solution)/shard_map/ppermute | solution.py:343
  146.0 19.4 %collective-permute-start.13 = (f32[2,3,128,128]{3,2,1,0:T(8,128)S(1)}, f32[2,3,128,128]{3,2,1,0:T(8,128)S(1)}, u32[]{:S(2)}, u32[]{:S(2)}) collective-permute-start(f32[2,3,128,128]{3,2,1,0:T(8,128)S(1)} %pad_maximum_fusion.2), channel_id=1, source_target_pairs={{0,4},{1,5},{2,6},{3,7},{4,8},{5,9},{6,10},{7,11},{8,12},{9,13},{1... | collective-permute-start | bytes 1179656 | tf_op jit(solution)/shard_map/ppermute | solution.py:343
  146.9 19.5 %copy-start.11 = (f32[4,256,256]{2,1,0:T(8,128)S(1)}, f32[4,256,256]{2,1,0:T(8,128)}, u32[]{:S(2)}) copy-start(f32[4,256,256]{2,1,0:T(8,128)} %inv.3) | copy-start | bytes 3145732
  149.0 17.4 %copy-start.8 = (f32[12288,128]{1,0:T(8,128)S(1)}, f32[12288,128]{1,0:T(8,128)}, u32[]{:S(2)}) copy-start(f32[12288,128]{1,0:T(8,128)} %all-gather.2.cloned.1.call-done) | copy-start | bytes 18874372
  149.1 23.3 %collective-permute-start.12 = (f32[2,1536,128]{2,1,0:T(8,128)S(1)}, f32[2,1536,128]{2,1,0:T(8,128)S(1)}, u32[]{:S(2)}, u32[]{:S(2)}) collective-permute-start(f32[2,1536,128]{2,1,0:T(8,128)S(1)} %pad_maximum_fusion.mine), channel_id=1, source_target_pairs={{0,16},{16,0},{32,48},{48,32},{64,80},{80,64},{96,112},{112,96},{1... | collective-permute-start | bytes 4718600 | tf_op jit(solution)/shard_map/ppermute | solution.py:304
  165.6 6.8 %copy-start.5 = (f32[1536,2,128]{2,1,0:T(2,128)S(1)}, f32[1536,2,128]{2,1,0:T(2,128)}, u32[]{:S(2)}) copy-start(f32[1536,2,128]{2,1,0:T(2,128)} %copy-done.3) | copy-start | bytes 4718596
  165.6 6.8 %copy-start.10 = (f32[1536,2,128]{2,1,0:T(2,128)S(1)}, f32[1536,2,128]{2,1,0:T(2,128)}, u32[]{:S(2)}) copy-start(f32[1536,2,128]{2,1,0:T(2,128)} %copy-done.9) | copy-start | bytes 4718596
  165.6 6.8 %copy-start.14 = (s32[4,48]{1,0:T(4,128)S(1)}, s32[4,48]{1,0:T(4,128)}, u32[]{:S(2)}) copy-start(s32[4,48]{1,0:T(4,128)} %lower_fill.1) | copy-start | bytes 2308
  165.6 6.8 %copy-start.15 = (s32[4,48]{1,0:T(4,128)S(1)}, s32[4,48]{1,0:T(4,128)}, u32[]{:S(2)}) copy-start(s32[4,48]{1,0:T(4,128)} %upper_fill.1) | copy-start | bytes 2308
  165.6 6.8 %collective-permute-start.16 = (f32[4,2,3,128,128]{4,3,2,1,0:T(8,128)S(1)}, f32[4,2,3,128,128]{4,3,2,1,0:T(8,128)S(1)}, u32[]{:S(2)}, u32[]{:S(2)}) collective-permute-start(f32[4,2,3,128,128]{4,3,2,1,0:T(8,128)S(1)} %pad_maximum_fusion.1.mine_c), channel_id=1, source_target_pairs={{0,16},{16,0},{32,48},{48,32},{64,80},{80,64},{96,112},{112,96},{1... | collective-permute-start | bytes 4718600 | tf_op jit(solution)/shard_map/ppermute | solution.py:304
  169.8 2.6 %copy-start = (f32[1536,1024]{1,0:T(8,128)}, f32[1536,1024]{1,0:T(8,128)S(1)}, u32[]{:S(2)}) copy-start(f32[1536,1024]{1,0:T(8,128)S(1)} %scale.1.scaled) | copy-start | bytes 18874372
Sparse Core Ops, SparseCore 0:
  25.8 5.2 sort.26.cloned.1.call-done
  77.9 64.0 all-gather.1
  (1 shorter events, 0.0 us)
